TPU v7x, 128 devices: a whole 4x4x4 slice. The times are simulated.
128 devices in a mesh: group: 4 (over x), head: 32 (over z, y, core).
Axes of the slice: x: 4, y: 4, z: 4, core: 2. Of those that a mesh axis runs over, the one named last changes fastest.
Arguments:
- queries: bfloat16 [256, 8192], P(('group', 'head')), may hold values from -124 to 124
- prefix_keys: bfloat16 [16384, 1024], P('head'), may hold values from -4.5 to 4.5
- prefix_values: bfloat16 [16384, 1024], P('head'), may hold values from -6 to 6
- suffix_keys: bfloat16 [256, 64, 1024], P('group', 'head'), may hold values from -6 to 6
- suffix_values: bfloat16 [256, 64, 1024], P('group', 'head'), may hold values from -6 to 6
- suffix_lengths: int32 [256], P('group'), may hold values from 1 to 64
- hidden_in: bfloat16 [256, 8192], P(('group', 'head')), may hold values from -0.29882812 to 0.29882812
- w_out: bfloat16 [8192, 8192], P('head'), may hold values from -0.0625 to 0.0625
- norm_gain: bfloat16 [8192], replicated, may hold values from 0.099609375 to 1.8984375
- expert_ids: int32 [256, 2], P(('group', 'head')), may hold values from 0 to 3, all different within a row; in each aligned block of 2 rows (0 to 1, 2 to 3, ...) at most 2 rows name the same one
- expert_weights: float32 [256, 2], P(('group', 'head')), may hold values from 0.2 to 1
- w_gate: bfloat16 [4, 8192, 12288], P('group', None, 'head'), may hold values from -0.0625 to 0.0625
- w_up: bfloat16 [4, 8192, 12288], P('group', None, 'head'), may hold values from -0.0625 to 0.0625
- w_down: bfloat16 [4, 12288, 8192], P('group', 'head'), may hold values from -0.0546875 to 0.0546875
Outputs:
- mixed: bfloat16 [256, 8192], P(('group', 'head'))
Inputs may be any that keep to these rules, and one draw needn't show every extreme that they name: `expert_ids`: each row names 2 different experts; the 2 rows of one device name any one expert 2 times at most.
All inputs are finite; a program needn't handle non-finite values.
Results may differ from a plain program's by a relative error of at most 0.027.
Values may be sent and summed in bfloat16 or wider, within the bound.
No kernel may reach another device: no remote copies, remote signals or barrier semaphores. Data moves between devices by JAX's collectives and lax.ppermute only.
A program may use at most 320 MiB of HBM per device.

v0:
```python
import jax
import jax.numpy as jnp
from jax import lax
from jax.sharding import PartitionSpec as P

HEADS = 64
KV = 8
HD = 128
CAP = 2


NEG = -1e30
EPS = 1e-05


def merged(value, axis, join):
    pieces = jax.tree.map(lambda part: lax.all_gather(part, axis), value)
    head = jax.tree.map(lambda part: part[0], pieces)
    tail = jax.tree.map(lambda part: part[1:], pieces)
    running, _ = lax.scan(lambda running, share: (join(running, share), None), head, tail)
    return running


def local_softmax(
    queries_all, prefix_keys, prefix_values, suffix_keys, suffix_values, suffix_lengths, offset
):
    count_rows = queries_all.shape[0]
    per_group = HEADS // KV
    scaling = 1.0 / HD**0.5
    query_grid = queries_all.reshape(count_rows, KV, per_group, HD)
    prefix_k = prefix_keys.reshape(-1, KV, HD)
    prefix_v = prefix_values.reshape(-1, KV, HD)
    suffix_k = suffix_keys.reshape(count_rows, -1, KV, HD)
    suffix_v = suffix_values.reshape(count_rows, -1, KV, HD)
    prefix_scores = (
        jnp.einsum("rkgd,pkd->rkgp", query_grid, prefix_k, preferred_element_type=jnp.float32)
        * scaling
    )
    suffix_scores = (
        jnp.einsum("rkgd,rskd->rkgs", query_grid, suffix_k, preferred_element_type=jnp.float32)
        * scaling
    )
    position = offset + jnp.arange(suffix_k.shape[1], dtype=jnp.int32)
    live_mask = position[None, :] < suffix_lengths[:, None]
    suffix_scores = jnp.where(live_mask[:, None, None, :], suffix_scores, NEG)
    highest = jnp.maximum(jnp.max(prefix_scores, axis=-1), jnp.max(suffix_scores, axis=-1))
    prefix_prob = jnp.exp(prefix_scores - highest[..., None])
    suffix_prob = jnp.exp(suffix_scores - highest[..., None])
    totals = jnp.sum(prefix_prob, axis=-1) + jnp.sum(suffix_prob, axis=-1)
    weighted = jnp.einsum(
        "rkgp,pkd->rkgd",
        prefix_prob.astype(jnp.bfloat16),
        prefix_v,
        preferred_element_type=jnp.float32,
    )
    weighted = weighted + jnp.einsum(
        "rkgs,rskd->rkgd",
        suffix_prob.astype(jnp.bfloat16),
        suffix_v,
        preferred_element_type=jnp.float32,
    )
    return (
        highest.reshape(count_rows, HEADS),
        totals.reshape(count_rows, HEADS),
        weighted.reshape(count_rows, HEADS, HD),
    )


def join_parts(first, second):
    top_first, sum_first, weighted_first = first
    top_second, sum_second, weighted_second = second
    top_both = jnp.maximum(top_first, top_second)
    factor_first = jnp.exp(top_first - top_both)
    factor_second = jnp.exp(top_second - top_both)
    sum_both = sum_first * factor_first + sum_second * factor_second
    weighted_both = (
        weighted_first * factor_first[..., None] + weighted_second * factor_second[..., None]
    )
    return (top_both, sum_both, weighted_both)


def expert_rows(block, w_gate, w_up, w_down):
    flat = block.reshape(-1, block.shape[-1])
    gate_val = jnp.dot(flat, w_gate[0], preferred_element_type=jnp.float32)
    up_val = jnp.dot(flat, w_up[0], preferred_element_type=jnp.float32)
    inner = (jax.nn.silu(gate_val) * up_val).astype(jnp.bfloat16)
    output = jnp.dot(inner, w_down[0], preferred_element_type=jnp.float32).astype(jnp.bfloat16)
    return output.reshape(block.shape[:-1] + (w_down.shape[-1],))


def local(
    queries,
    prefix_keys,
    prefix_values,
    suffix_keys,
    suffix_values,
    suffix_lengths,
    hidden_in,
    w_out,
    norm_gain,
    expert_ids,
    expert_weights,
    w_gate,
    w_up,
    w_down,
):
    head_count = lax.axis_size("head")
    own_head = lax.axis_index("head")
    queries_all = lax.all_gather(queries, "head", axis=0, tiled=True)
    count_rows = queries_all.shape[0]
    offset = own_head * suffix_keys.shape[1]
    highest, totals, weighted = local_softmax(
        queries_all, prefix_keys, prefix_values, suffix_keys, suffix_values, suffix_lengths, offset
    )
    per_device = HEADS // head_count
    highest, totals, weighted = merged((highest, totals, weighted), "head", join_parts)
    own_sums = lax.dynamic_slice_in_dim(weighted, own_head * per_device, per_device, 1)
    own_totals = lax.dynamic_slice_in_dim(totals, own_head * per_device, per_device, 1)
    attended = (
        (own_sums / own_totals[..., None]).reshape(count_rows, per_device * HD).astype(jnp.bfloat16)
    )
    local_rows = hidden_in.shape[0]
    projected = lax.psum_scatter(
        jnp.dot(attended, w_out, preferred_element_type=jnp.float32),
        "head",
        scatter_dimension=0,
        tiled=True,
    )
    residual = hidden_in.astype(jnp.float32) + projected
    mean_square = jnp.mean(residual * residual, axis=-1, keepdims=True)
    normed = (residual * lax.rsqrt(mean_square + EPS) * norm_gain.astype(jnp.float32)).astype(
        jnp.bfloat16
    )
    expert_count = lax.axis_size("group")
    width = normed.shape[1]
    pair_ids = expert_ids.reshape(-1)
    one_hot = (pair_ids[:, None] == jnp.arange(expert_count, dtype=jnp.int32)[None, :]).astype(
        jnp.int32
    )
    earlier = jnp.cumsum(one_hot, axis=0) - one_hot
    rank = jnp.sum(earlier * one_hot, axis=1)
    slot = pair_ids * CAP + rank
    table = slot[:, None] == jnp.arange(expert_count * CAP, dtype=jnp.int32)[None, :]
    repeated = jnp.repeat(normed, expert_ids.shape[1], axis=0)
    outgoing = jnp.dot(table.T.astype(jnp.bfloat16), repeated, preferred_element_type=jnp.float32)
    outgoing = outgoing.astype(jnp.bfloat16).reshape(expert_count, CAP, width)
    fanned = jnp.broadcast_to(outgoing[:, None], (expert_count, head_count, CAP, width))
    fanned = fanned.reshape(expert_count * head_count, CAP, width)
    arrived = lax.all_to_all(fanned, ("group", "head"), split_axis=0, concat_axis=0, tiled=True)
    arrived = jnp.swapaxes(arrived.reshape(expert_count, head_count, CAP, width), 0, 1)
    partial_out = expert_rows(arrived, w_gate, w_up, w_down)
    summed = lax.psum_scatter(partial_out, "head", scatter_dimension=0, tiled=True).astype(
        jnp.float32
    )
    returned = lax.all_to_all(
        summed.reshape(expert_count, CAP, width), "group", split_axis=0, concat_axis=0, tiled=True
    )
    weighted_table = table.astype(jnp.float32) * expert_weights.reshape(-1)[:, None]
    row_table = weighted_table.reshape(local_rows, expert_ids.shape[1], expert_count * CAP).sum(
        axis=1
    )
    mixture = jnp.dot(
        row_table, returned.reshape(expert_count * CAP, width), precision=lax.Precision.HIGHEST
    )
    return (residual + mixture).astype(jnp.bfloat16)


def solution(mesh):
    placed = (
        P(("group", "head"), None),
        P("head", None),
        P("head", None),
        P("group", "head", None),
        P("group", "head", None),
        P("group"),
        P(("group", "head"), None),
        P("head", None),
        P(),
        P(("group", "head"), None),
        P(("group", "head"), None),
        P("group", None, "head"),
        P("group", None, "head"),
        P("group", "head", None),
    )
    return jax.shard_map(
        local, mesh=mesh, in_specs=placed, out_specs=P(("group", "head"), None), check_vma=False
    )
```

profile of v0, /device:TPU:1, one launch (start us, length us, event | category | flops | bytes accessed | tf_op | source)
XLA Modules:
  0.0 790.8 jit_solution(17652045051046055554)
XLA Ops:
  7.3 1.5 copy.128
  8.8 1.5 copy.129
  10.4 45.8 %all-gather.6.cloned.1.call-done = bf16[32,2,8192]{2,1,0:T(2,128)(2,1)} async-done(((bf16[1,2,8192]{2,1,0:T(2,128)(2,1)}), bf16[32,2,8192]{2,1,0:T(2,128)(2,1)}) %all-gather.6.cloned.1.call-update) | async-done | bytes 1048592 | tf_op jit(solution)/shard_map/all_gather | solution.py:109
  56.2 1.8 reshape.149
  58.1 3.6 fusion.41
  62.7 4.8 bitcast_reduce_fusion
  67.7 4.6 fusion.5
  74.1 2.6 bitcast_add_fusion
  76.7 1.6 copy.154
  78.6 25.5 %all_gather.14 = f32[32,64,64]{2,1,0:T(8,128)S(1)} all-gather(f32[1,64,64]{2,1,0:T(8,128)S(1)} %copy.109), channel_id=1, replica_groups=mesh['group'=4,'head'=32] {'head'}, dimensions={0}, use_global_device_ids=true | all-gather | bytes 540672 | tf_op jit(solution)/shard_map/all_gather | solution.py:17
  104.3 33.9 %all_gather.13 = f32[32,64,64]{2,1,0:T(8,128)S(1)} all-gather(f32[1,64,64]{2,1,0:T(8,128)S(1)} %copy.106), channel_id=1, replica_groups=mesh['group'=4,'head'=32] {'head'}, dimensions={0}, use_global_device_ids=true | all-gather | bytes 540672 | tf_op jit(solution)/shard_map/all_gather | solution.py:17
  139.3 142.2 %all-gather.4.cloned.1.call-done = f32[32,64,64,128]{3,2,1,0:T(8,128)} async-done(((f32[1,64,64,128]{3,2,1,0:T(8,128)}), f32[32,64,64,128]{3,2,1,0:T(8,128)}) %all-gather.4.cloned.1.call-update) | async-done | bytes 67108880 | tf_op jit(solution)/shard_map/all_gather | solution.py:17
  281.5 42.7 %slice.29 = f32[31,64,64,128]{3,2,1,0:T(8,128)} slice(f32[32,64,64,128]{3,2,1,0:T(8,128)} %all-gather.4.cloned.1.call-done), slice={[1:32], [0:64], [0:64], [0:128]} | slice | bytes 130023424 | tf_op jit(solution)/shard_map/slice | solution.py:19
  324.2 1.7 slice_bitcast_fusion
  325.9 107.9 %while.14 = (s32[]{:T(128)}, f32[64,64]{1,0:T(8,128)S(1)}, f32[64,64]{1,0:T(8,128)S(1)}, f32[64,64,128]{2,1,0:T(8,128)S(1)}, f32[31,64,64]{2,1,0:T(8,128)}, /*in...) while((s32[]{:T(128)}, f32[64,64]{1,0:T(8,128)S(1)}, f32[64,64]{1,0:T(8,128)S(1)}, ...), condition=%wide.region_5.6_spmd, body=%wide.region_4.5_spmd.sunk | while | flops 1597442 | bytes 6455389 | solution.py:20
  326.7 2.7 fusion.54
  330.2 2.7 fusion.54
  333.7 2.7 fusion.54
  337.2 2.7 fusion.54
  340.6 2.7 fusion.54
  344.1 2.7 fusion.54
  347.6 2.7 fusion.54
  351.1 2.7 fusion.54
  354.6 2.7 fusion.54
  358.1 2.7 fusion.54
  361.5 2.7 fusion.54
  365.0 2.7 fusion.54
  368.5 2.7 fusion.54
  372.0 2.7 fusion.54
  375.5 2.7 fusion.54
  378.9 2.7 fusion.54
  382.4 2.7 fusion.54
  385.9 2.7 fusion.54
  389.4 2.7 fusion.54
  392.9 2.7 fusion.54
  396.3 2.7 fusion.54
  399.8 2.7 fusion.54
  403.3 2.7 fusion.54
  406.8 2.7 fusion.54
  410.3 2.7 fusion.54
  413.7 2.7 fusion.54
  417.2 2.7 fusion.54
  420.7 2.7 fusion.54
  424.2 2.7 fusion.54
  427.7 2.7 fusion.54
  431.2 2.7 fusion.54
  434.1 4.4 fusion.34
  440.2 104.5 %all-reduce.5.cloned.1.call-done = f32[64,8192]{1,0:T(8,128)} async-done(((f32[64,8192]{1,0:T(8,128)}), f32[64,8192]{1,0:T(8,128)}) %all-reduce.5.cloned.1.call-update) | async-done | bytes 2097168
  544.7 1.1 multiply_reduce_fusion
  547.4 4.2 broadcast_in_dim.24
  551.6 60.5 %all_to_all.10 = bf16[128,2,8192]{2,1,0:T(2,128)(2,1)S(1)} all-to-all(bf16[128,2,8192]{2,1,0:T(2,128)(2,1)S(1)} %bitcast.93), channel_id=1, replica_groups=mesh['group'=4,'head'=32] {'group','head'}, dimensions={0} | all-to-all | bytes 8388608 | tf_op jit(solution)/shard_map/all_to_all | solution.py:149
  612.1 2.7 copy.115
  614.8 6.3 copy.116
  621.1 7.2 reshape.156
  628.3 6.6 fusion.10
  634.9 5.4 fusion.20
  640.4 4.4 convolution_convert_fusion
  644.7 7.6 reshape.157
  652.3 8.2 %copy.117 = bf16[32,4,2,8192]{3,1,2,0:T(4,128)(2,1)} copy(bf16[32,4,2,8192]{3,2,1,0:T(2,128)(2,1)} %reshape.157) | data formatting | bytes 8388608 | tf_op jit(solution)/shard_map/reshape | solution.py:88
  660.6 109.2 %all-reduce.7.cloned.1.call-done = bf16[32,4,2,8192]{3,1,2,0:T(4,128)(2,1)} async-done(((bf16[32,4,2,8192]{3,1,2,0:T(4,128)(2,1)}), bf16[32,4,2,8192]{3,1,2,0:T(4,128)(2,1)}) %all-reduce.7.cloned.1.call-update) | async-done | bytes 4194320
  769.8 1.6 bitcast_convert_fusion
  772.3 4.0 all-to-all-start.1
  776.3 5.5 all-to-all-done.1
  782.0 1.9 fusion.3
  (99 shorter events, 34.3 us)
Async XLA Ops:
  6.5 66.8 %copy-start = (bf16[64,2,1024]{2,1,0:T(2,128)(2,1)S(1)}, bf16[64,2,1024]{2,1,0:T(2,128)(2,1)}, u32[]{:S(2)}) copy-start(bf16[64,2,1024]{2,1,0:T(2,128)(2,1)} %param.20) | copy-start | bytes 786436
  6.5 3.8 copy-start.8
  6.5 49.7 %all-gather.6.cloned.1.call-start = ((), (), s32[]{:S(2)}) async-start(), calls=%async_computation.3 | async-start | bytes 1081344 | tf_op jit(solution)/shard_map/all_gather | solution.py:109
  7.3 274.2 %all-gather.4.cloned.1.call-start = ((), (), s32[]{:S(2)}) async-start(), calls=%async_computation.2 | async-start | bytes 69206016 | tf_op jit(solution)/shard_map/all_gather | solution.py:17
  67.7 4.6 copy-start.3
  78.3 466.4 %all-reduce.5.cloned.1.call-start = ((), (), s32[]{:S(2)}) async-start(), calls=%async_computation.4 | async-start | bytes 4194304
  434.1 4.5 copy-start.5
  434.1 4.5 copy-start.6
  434.1 4.7 copy-start.9
  434.1 110.6 %copy-start.4 = (bf16[2,8192]{1,0:T(2,128)(2,1)S(1)}, bf16[2,8192]{1,0:T(2,128)(2,1)}, u32[]{:S(2)}) copy-start(bf16[2,8192]{1,0:T(2,128)(2,1)} %param.22) | copy-start | bytes 98308
  438.5 331.3 %all-reduce.7.cloned.1.call-start = ((), (), s32[]{:S(2)}) async-start(), calls=%async_computation.5 | async-start | bytes 8388608
  628.3 6.6 copy-start.2
  628.3 12.0 %slice-start = ((s8[6291456]{0:T(1024)(128)(4,1)}), s8[4194304]{0:T(1024)(128)(4,1)S(1)}, s32[]{:S(2)}) async-start(s8[6291456]{0:T(1024)(128)(4,1)} %bitcast.96), calls=%async_computation.6 | async-start | bytes 8388608
  634.9 5.4 slice-start.1
  652.3 131.6 %copy-start.1 = (bf16[64,2,1024]{2,1,0:T(2,128)(2,1)S(1)}, bf16[64,2,1024]{2,1,0:T(2,128)(2,1)}, u32[]{:S(2)}) copy-start(bf16[64,2,1024]{2,1,0:T(2,128)(2,1)} %param.20) | copy-start | bytes 786436
  660.5 115.7 %copy-start.7 = (f32[2,2]{1,0:T(2,128)S(1)}, f32[2,2]{1,0:T(2,128)}, u32[]{:S(2)}) copy-start(f32[2,2]{1,0:T(2,128)} %param.26) | copy-start | bytes 52
  772.3 9.5 %all-to-all-start.1 = ((f32[4,2,8192]{2,1,0:T(2,128)}), f32[4,2,8192]{2,1,0:T(2,128)S(1)}, u32[]{:S(2)}, u32[]{:S(2)}) async-start(f32[4,2,8192]{2,1,0:T(2,128)} %copy.118), calls=%async_computation.1 | async-start | bytes 524288 | tf_op jit(solution)/shard_map/all_to_all | solution.py:155
Sparse Core Ops, SparseCore 0:
  9.6 46.5 all-gather.5
  78.5 202.9 all-gather.3
  438.6 106.0 all-reduce.4
  660.7 109.0 all-reduce.6
where the time goes:
time: 804 us; the launch traced here: 791 us
  waiting for transfers between devices  408 us (51%)
  blocking collectives  120 us (15%)
  other arithmetic  117 us (15%)
  local copies, waits for them, and re-layouts  91.8 us (11%)
  matrix products  34.7 us (4%)
  between operations  14.5 us (2%)
    unnamed x6, waiting for transfers between devices  214 us
    all_gather x1, waiting for transfers between devices, merged(): pieces = jax.tree.map(lambda part: lax.all_gather(part, axis), value)  142 us
    add x31, other arithmetic, join_parts(): weighted_first * factor_first[..., None]  82.4 us
    all_to_all x1, blocking collectives, local(): lax.all_to_all(fanned, ('group', 'head'), split_axis=0, concat_axis=0, ti...  60.5 us
    all_gather x2, blocking collectives, merged(): pieces = jax.tree.map(lambda part: lax.all_gather(part, axis), value)  59.4 us
    all_gather x1, waiting for transfers between devices, local(): queries_all = lax.all_gather(queries, 'head', axis=0, tiled=True)  45.8 us
    slice x3, local copies, waits for them, and re-layouts, merged(): tail = jax.tree.map(lambda part: part[1:], pieces)  43.9 us
    add x31, other arithmetic, join_parts(): sum_both = sum_first * factor_first + sum_second * factor_second  24.8 us
  transfers between devices with their start and end apart: 5, of which 5 were waited for; matrix products, arithmetic and copies ran while one was open for 1% of the time, Pallas kernels for 0%

commit v1 on v0

v1 whole, which is shorter than its diff:
```python
import functools

import jax
import jax.numpy as jnp
from jax import lax
from jax.experimental import pallas as pl
from jax.experimental.pallas import tpu as pltpu
from jax.sharding import Mesh, PartitionSpec as P

HEADS = 64
KV = 8
HD = 128
D = 8192
HALF = D // 2
EPS = 1e-05
NEG = -1e30
LOG2E = 1.4426950408889634
SCALE = LOG2E / HD**0.5
BF = jnp.bfloat16
F32 = jnp.float32
ALL = ("x", "z", "y", "c")
PLANE = ("z", "y", "c")
SWAP = [(0, 1), (1, 0)]
MB = 1 << 20


def dot(a, b):
    return jnp.dot(a, b, preferred_element_type=F32)


def dot_t(a, b):
    return lax.dot_general(a, b, (((1,), (1,)), ((), ())), preferred_element_type=F32)


def attend_kernel(q_ref, ka_ref, kb_ref, va_ref, vb_ref, ska_ref, skb_ref, sva_ref, svb_ref, left_ref, out_ref):
    rows = 64
    q = jnp.concatenate([q_ref[:, g * HD : (g + 1) * HD] for g in range(4)], axis=0)
    row = lax.broadcasted_iota(jnp.int32, (4 * rows, 2 * rows), 0) % rows
    col = lax.broadcasted_iota(jnp.int32, (4 * rows, 2 * rows), 1)
    own_row = row == col // 2
    spot = col % 2
    left = left_ref[...]
    scores = [
        dot_t(q, ka_ref[...]) * SCALE,
        dot_t(q, kb_ref[...]) * SCALE,
        jnp.where(own_row & (spot < left[:, 0:1]), dot_t(q, ska_ref[...]) * SCALE, NEG),
        jnp.where(own_row & (spot < left[:, 1:2]), dot_t(q, skb_ref[...]) * SCALE, NEG),
    ]
    tops = [jnp.max(s, axis=1, keepdims=True) for s in scores]
    top = jnp.maximum(jnp.maximum(tops[0], tops[1]), jnp.maximum(tops[2], tops[3]))
    top = top.astype(BF).astype(F32)
    total = jnp.zeros((4 * rows, 1), F32)
    acc = jnp.zeros((4 * rows, HD), F32)
    for s, v in zip(scores, (va_ref, vb_ref, sva_ref, svb_ref)):
        prob = jnp.exp2(s - top)
        total = total + jnp.sum(prob, axis=1, keepdims=True)
        acc = acc + dot(prob.astype(BF), v[...])
    eye = lax.broadcasted_iota(jnp.int32, (4 * rows, 4 * rows), 0) == lax.broadcasted_iota(
        jnp.int32, (4 * rows, 4 * rows), 1
    )
    top_row = jnp.sum(jnp.where(eye, top, 0.0), axis=0, keepdims=True)
    total_row = jnp.sum(jnp.where(eye, total, 0.0), axis=0, keepdims=True)
    total_high = total_row.astype(BF).astype(F32)
    total_low = total_row - total_high
    line = lax.broadcasted_iota(jnp.int32, (16, 4 * rows), 0)
    for k in range(2):
        for j in range(2):
            g = 2 * k + j
            out_ref[k, 0:rows, j * HD : (j + 1) * HD] = acc[g * rows : (g + 1) * rows].astype(BF)
        part = slice(k * 2 * rows, (k + 1) * 2 * rows)
        high = jnp.concatenate([top_row[:, part], total_high[:, part]], axis=1)
        low = jnp.concatenate([top_row[:, part], total_low[:, part]], axis=1)
        tail = jnp.where(line == 0, high, jnp.where(line == 1, low, 0.0))
        out_ref[k, rows : rows + 16, :] = tail.astype(BF)


def attend(q, ka, kb, va, vb, sa, sb, left):
    full = lambda n: pl.BlockSpec((n, HD), lambda i: (0, i))
    second = lambda n: pl.BlockSpec((n, HD), lambda i: (0, i + KV))
    return pl.pallas_call(
        attend_kernel,
        grid=(KV,),
        in_specs=[
            pl.BlockSpec((64, 4 * HD), lambda i: (0, i)),
            full(512),
            full(512),
            full(512),
            full(512),
            full(128),
            full(128),
            second(128),
            second(128),
            pl.BlockSpec((256, 2), lambda i: (0, 0)),
        ],
        out_specs=pl.BlockSpec((2, 80, 2 * HD), lambda i: (i, 0, 0)),
        out_shape=jax.ShapeDtypeStruct((16, 80, 2 * HD), BF),
        compiler_params=pltpu.CompilerParams(vmem_limit_bytes=32 * MB),
        cost_estimate=pl.CostEstimate(flops=1400000000, bytes_accessed=6 * MB, transcendentals=2700000),
    )(q, ka, kb, va, vb, sa, sb, sa, sb, left)


def project_kernel(c_ref, got_ref, w_ref, mine_ref, other_ref, att_ref):
    rows = 64
    n = pl.program_id(0)

    @pl.when(n == 0)
    def _():
        tops = [got_ref[s, rows : rows + 1, 0 : 2 * rows].astype(F32) for s in range(16)]
        sums = [
            got_ref[s, rows : rows + 1, 2 * rows :].astype(F32)
            + got_ref[s, rows + 1 : rows + 2, 2 * rows :].astype(F32)
            for s in range(16)
        ]
        top = functools.reduce(jnp.maximum, tops)
        factors = [jnp.exp2(t - top) for t in tops]
        total = functools.reduce(jnp.add, [f * s for f, s in zip(factors, sums)])
        lane = lax.broadcasted_iota(jnp.int32, (rows, 2 * rows), 1)
        line = lax.broadcasted_iota(jnp.int32, (rows, 2 * rows), 0)
        for j in range(2):
            here = lane == line + j * rows
            acc = jnp.zeros((rows, HD), F32)
            for s in range(16):
                share = jnp.sum(jnp.where(here, factors[s] / total, 0.0), axis=1, keepdims=True)
                acc = acc + got_ref[s, 0:rows, j * HD : (j + 1) * HD].astype(F32) * share
            att_ref[:, j * HD : (j + 1) * HD] = acc.astype(BF)

    value = dot(att_ref[...], w_ref[...]).astype(BF)

    @pl.when(n < 4)
    def _():
        other_ref[...] = value

    @pl.when(n >= 4)
    def _():
        mine_ref[...] = value


def project(core, got, w_out):
    block = D // 8
    return pl.pallas_call(
        project_kernel,
        grid_spec=pltpu.PrefetchScalarGridSpec(
            num_scalar_prefetch=1,
            grid=(8,),
            in_specs=[
                pl.BlockSpec((16, 80, 256), lambda n, c: (0, 0, 0)),
                pl.BlockSpec((256, block), lambda n, c: (0, (n + 4 * (1 - c[0])) % 8)),
            ],
            out_specs=[
                pl.BlockSpec((64, block), lambda n, c: (0, jnp.maximum(n - 4, 0))),
                pl.BlockSpec((64, block), lambda n, c: (0, jnp.minimum(n, 3))),
            ],
            scratch_shapes=[pltpu.VMEM((64, 256), BF)],
        ),
        out_shape=[jax.ShapeDtypeStruct((64, HALF), BF)] * 2,
        compiler_params=pltpu.CompilerParams(vmem_limit_bytes=32 * MB),
        cost_estimate=pl.CostEstimate(flops=270000000, bytes_accessed=6 * MB, transcendentals=0),
    )(core, got, w_out)


def first_kernel(c_ref, x_ref, wg_ref, wu_ref, g_ref, u_ref):
    @pl.when(pl.program_id(0) == 0)
    def _():
        g_ref[...] = jnp.zeros_like(g_ref)
        u_ref[...] = jnp.zeros_like(u_ref)

    x = x_ref[...]
    g_ref[...] += dot(x, wg_ref[...])
    u_ref[...] += dot(x, wu_ref[...])


def expert_first(core, x, w_gate, w_up):
    rows, units = x.shape[0], w_gate.shape[1]
    block = 1024
    return pl.pallas_call(
        first_kernel,
        grid_spec=pltpu.PrefetchScalarGridSpec(
            num_scalar_prefetch=1,
            grid=(4,),
            in_specs=[
                pl.BlockSpec((rows, block), lambda n, c: (0, n)),
                pl.BlockSpec((block, units), lambda n, c: (n + 4 * c[0], 0)),
                pl.BlockSpec((block, units), lambda n, c: (n + 4 * c[0], 0)),
            ],
            out_specs=[pl.BlockSpec((rows, units), lambda n, c: (0, 0))] * 2,
        ),
        out_shape=[jax.ShapeDtypeStruct((rows, units), F32)] * 2,
        compiler_params=pltpu.CompilerParams(vmem_limit_bytes=32 * MB),
        cost_estimate=pl.CostEstimate(flops=1600000000, bytes_accessed=9 * MB, transcendentals=0),
    )(core, x, w_gate, w_up)


def second_kernel(c_ref, x_ref, wg_ref, wu_ref, g0_ref, u0_ref, wd_ref, inner_ref, out_ref, g_ref, u_ref):
    n = pl.program_id(0)

    @pl.when(n == 0)
    def _():
        g_ref[...] = g0_ref[...]
        u_ref[...] = u0_ref[...]

    @pl.when(n < 4)
    def _():
        x = x_ref[...]
        g_ref[...] += dot(x, wg_ref[...])
        u_ref[...] += dot(x, wu_ref[...])

    @pl.when(n == 3)
    def _():
        g = g_ref[...]
        inner_ref[...] = (g / (1.0 + jnp.exp(-g)) * u_ref[...]).astype(BF)

    @pl.when(n >= 4)
    def _():
        out_ref[...] = dot(inner_ref[...], wd_ref[...]).astype(BF)


def expert_second(core, x, w_gate, w_up, gate, up, w_down):
    rows, units = x.shape[0], w_gate.shape[1]
    block = 1024
    early = lambda n: jnp.minimum(n, 3)
    late = lambda n: jnp.maximum(n - 4, 0)
    whole = pl.BlockSpec((rows, units), lambda n, c: (0, 0))
    return pl.pallas_call(
        second_kernel,
        grid_spec=pltpu.PrefetchScalarGridSpec(
            num_scalar_prefetch=1,
            grid=(8,),
            in_specs=[
                pl.BlockSpec((rows, block), lambda n, c: (0, early(n))),
                pl.BlockSpec((block, units), lambda n, c: (early(n) + 4 * (1 - c[0]), 0)),
                pl.BlockSpec((block, units), lambda n, c: (early(n) + 4 * (1 - c[0]), 0)),
                whole,
                whole,
                pl.BlockSpec((units, block), lambda n, c: (0, late(n) + 4 * (1 - c[0]))),
            ],
            out_specs=[whole, pl.BlockSpec((rows, block), lambda n, c: (0, late(n)))],
            scratch_shapes=[pltpu.VMEM((rows, units), F32), pltpu.VMEM((rows, units), F32)],
        ),
        out_shape=[
            jax.ShapeDtypeStruct((rows, units), BF),
            jax.ShapeDtypeStruct((rows, HALF), BF),
        ],
        compiler_params=pltpu.CompilerParams(vmem_limit_bytes=32 * MB),
        cost_estimate=pl.CostEstimate(flops=2400000000, bytes_accessed=15 * MB, transcendentals=0),
    )(core, x, w_gate, w_up, gate, up, w_down)


def third_kernel(c_ref, inner_ref, wd_ref, out_ref):
    out_ref[...] = dot(inner_ref[...], wd_ref[...]).astype(BF)


def expert_third(core, inner, w_down):
    rows, units = inner.shape
    block = 1024
    return pl.pallas_call(
        third_kernel,
        grid_spec=pltpu.PrefetchScalarGridSpec(
            num_scalar_prefetch=1,
            grid=(4,),
            in_specs=[
                pl.BlockSpec((rows, units), lambda n, c: (0, 0)),
                pl.BlockSpec((units, block), lambda n, c: (0, n + 4 * c[0])),
            ],
            out_specs=pl.BlockSpec((rows, block), lambda n, c: (0, n)),
        ),
        out_shape=jax.ShapeDtypeStruct((rows, HALF), BF),
        compiler_params=pltpu.CompilerParams(vmem_limit_bytes=32 * MB),
        cost_estimate=pl.CostEstimate(flops=800000000, bytes_accessed=6 * MB, transcendentals=0),
    )(core, inner, w_down)


def local(
    queries,
    prefix_keys,
    prefix_values,
    suffix_keys,
    suffix_values,
    suffix_lengths,
    hidden_in,
    w_out,
    norm_gain,
    expert_ids,
    expert_weights,
    w_gate,
    w_up,
    w_down,
):
    c = lax.axis_index("c")
    chip = lax.axis_index(("z", "y"))
    core = c.astype(jnp.int32).reshape(1)
    suffix = jnp.concatenate([suffix_keys, suffix_values], axis=-1).reshape(128, 2 * KV * HD)
    suffix_b = lax.ppermute(suffix, "c", SWAP)
    keys_b = lax.ppermute(prefix_keys, "c", SWAP)
    values_b = lax.ppermute(prefix_values, "c", SWAP)
    q = queries.reshape(2, 16, 2, 2 * HD).transpose(2, 0, 1, 3).reshape(1, 2, 2, HALF)
    q = jnp.broadcast_to(q, (16, 2, 2, HALF)).reshape(32, 2, HALF)
    q = lax.all_to_all(q, PLANE, split_axis=0, concat_axis=0, tiled=True).reshape(64, HALF)
    first = 4 * chip
    left = jnp.stack([suffix_lengths - (first + 2 * c), suffix_lengths - (first + 2 * (1 - c))], axis=1)
    left = jnp.tile(left.astype(jnp.int32), (4, 1))
    parts = attend(q, prefix_keys, keys_b, prefix_values, values_b, suffix, suffix_b, left)
    parts = lax.all_to_all(parts, ("z", "y"), split_axis=0, concat_axis=0, tiled=True)
    mine, other = project(core, parts, w_out)
    other = lax.ppermute(other, "c", SWAP)
    summed = (mine.astype(F32) + other.astype(F32)).astype(BF).reshape(32, 2, HALF)
    summed = lax.all_to_all(summed, PLANE, split_axis=0, concat_axis=0, tiled=True)
    summed = jnp.sum(summed.reshape(16, 2, 2, HALF).astype(F32), axis=0)
    residual = hidden_in.astype(F32) + jnp.swapaxes(summed, 0, 1).reshape(2, D)
    mean_square = jnp.mean(residual * residual, axis=-1, keepdims=True)
    normed = (residual * lax.rsqrt(mean_square + EPS) * norm_gain.astype(F32)).astype(BF)
    sent = jnp.swapaxes(normed.reshape(2, 2, HALF), 0, 1)[None]
    sent = jnp.broadcast_to(sent, (64, 2, 2, HALF)).reshape(128, 2, HALF)
    rows_a = lax.all_to_all(sent, ALL, split_axis=0, concat_axis=0, tiled=True).reshape(256, HALF)
    rows_b = lax.ppermute(rows_a, "c", SWAP)
    gate, up = expert_first(core, rows_a, w_gate[0], w_up[0])
    inner, other_out = expert_second(core, rows_b, w_gate[0], w_up[0], gate, up, w_down[0])
    other_out = lax.ppermute(other_out, "c", SWAP)
    mine_out = expert_third(core, inner, w_down[0])
    out = (mine_out.astype(F32) + other_out.astype(F32)).astype(BF).reshape(128, 2, HALF)
    out = lax.all_to_all(out, ALL, split_axis=0, concat_axis=0, tiled=True)
    out = jnp.sum(out.reshape(4, 16, 2, 2, HALF).astype(F32), axis=1)
    match = expert_ids[:, :, None] == jnp.arange(4, dtype=jnp.int32)[None, None, :]
    weights = jnp.sum(jnp.where(match, expert_weights[:, :, None], 0.0), axis=1)
    mixture = jnp.sum(out * weights.T[:, None, :, None], axis=0)
    mixture = jnp.swapaxes(mixture, 0, 1).reshape(2, D)
    return (residual + mixture).astype(BF)


def solution(mesh):
    grid = Mesh(mesh.devices.reshape(4, 4, 4, 2), ALL)
    placed = (
        P(ALL, None),
        P(PLANE, None),
        P(PLANE, None),
        P("x", PLANE, None),
        P("x", PLANE, None),
        P("x"),
        P(ALL, None),
        P(PLANE, None),
        P(),
        P(ALL, None),
        P(ALL, None),
        P("x", None, PLANE),
        P("x", None, PLANE),
        P("x", PLANE, None),
    )
    return jax.shard_map(
        local, mesh=grid, in_specs=placed, out_specs=P(ALL, None), check_vma=False
    )
```

time: 804 us -> 186 us (0.23); the launches traced: 791 us -> 185 us
  waiting for transfers between devices: 408 us -> 54.9 us
  other arithmetic: 117 us -> 6.35 us
  blocking collectives: 120 us -> 51.7 us
  local copies, waits for them, and re-layouts: 91.8 us -> 26.1 us
  matrix products: 34.7 us -> 0 us
  Pallas kernels: 0 us -> 24.9 us
  starting transfers between devices: 4.09 us -> 21.1 us
  between operations: 14.5 us -> 0.35 us
    unnamed x6 -> x0, waiting for transfers between devices: 214 us -> none
    all_gather x2 -> x0, waiting for transfers between devices: 188 us -> none  [the longest x1 142 us: merged(): pieces = jax.tree.map(lambda part: lax.all_gather(part, axis), value)]
    add x66 -> x0, other arithmetic: 107 us -> none  [the longest x31 82.4 us: join_parts(): weighted_first * factor_first[..., None]]
    all_gather x2 -> x0, blocking collectives: 59.4 us -> none  [merged(): pieces = jax.tree.map(lambda part: lax.all_gather(part, axis), value)]
    all_to_all x1 -> x3, waiting for transfers between devices: 5.46 us -> 53.4 us  [the longest x1 30.3 us: local(): out = lax.all_to_all(out, ALL, split_axis=0, concat_axis=0, tiled=True)]
    slice x3 -> x0, local copies, waits for them, and re-layouts: 43.9 us -> none  [merged(): tail = jax.tree.map(lambda part: part[1:], pieces)]
    dot_general x10 -> x0, matrix products: 34.7 us -> none  [the longest x1 6.61 us: expert_rows(): gate_val = jnp.dot(flat, w_gate[0], preferred_element_type=jnp.float32)]
    pallas_call x0 -> x5, Pallas kernels: none -> 24.9 us  [the longest x1 9.04 us: attend(): pl.pallas_call(attend_kernel, grid=(KV,), in_specs=[pl.BlockSpec((64, 4 *...]
  transfers between devices with their start and end apart: 5 -> 9, of which waited for: 5 -> 4; matrix products, arithmetic and copies ran while one was open for 1% -> 2% of each run, Pallas kernels for 0% -> 3%
where the time goes in v1:
time: 186 us; the launch traced here: 185 us
  waiting for transfers between devices  54.9 us (30%)
  blocking collectives  51.7 us (28%)
  local copies, waits for them, and re-layouts  26.1 us (14%)
  Pallas kernels  24.9 us (13%)
  starting transfers between devices  21.1 us (11%)
  other arithmetic  6.35 us (3%)
    all_to_all x1, blocking collectives, local(): lax.all_to_all(sent, ALL, split_axis=0, concat_axis=0, tiled=True)  36.1 us
    all_to_all x1, waiting for transfers between devices, local(): out = lax.all_to_all(out, ALL, split_axis=0, concat_axis=0, tiled=True)  30.3 us
    all_to_all x1, blocking collectives, local(): lax.all_to_all(parts, ('z', 'y'), split_axis=0, concat_axis=0, tiled=True)  15.6 us
    unnamed x32, local copies, waits for them, and re-layouts  14 us
    all_to_all x1, waiting for transfers between devices, local(): lax.all_to_all(summed, PLANE, split_axis=0, concat_axis=0, tiled=True)  11.6 us
    all_to_all x1, waiting for transfers between devices, local(): lax.all_to_all(q, PLANE, split_axis=0, concat_axis=0, tiled=True)  11.4 us
    pallas_call x1, Pallas kernels, attend(): pl.pallas_call(attend_kernel, grid=(KV,), in_specs=[pl.BlockSpec((64, 4 *...  9.04 us
    all_to_all x1, starting transfers between devices, local(): lax.all_to_all(q, PLANE, split_axis=0, concat_axis=0, tiled=True)  8.31 us
  transfers between devices with their start and end apart: 9, of which 4 were waited for; matrix products, arithmetic and copies ran while one was open for 2% of the time, Pallas kernels for 3%

profile of v1, /device:TPU:1, one launch (start us, length us, event | category | flops | bytes accessed | tf_op | source)
XLA Modules:
  0.0 185.4 jit_solution(11353462080522002209)
XLA Ops:
  0.0 1.4 collective-permute-start
  1.4 0.0 collective-permute-start.1
  1.4 1.5 pad_maximum_fusion
  2.9 0.0 copy-start.6
  2.9 0.2 reshape.65.ska_ref.sva_ref
  3.2 0.6 collective-permute-start.2
  3.7 0.0 copy-done.9
  3.8 1.3 broadcast_in_dim.15
  5.1 8.3 %all-to-all-start = ((bf16[32,2,4096]{2,1,0:T(2,128)(2,1)}), bf16[32,2,4096]{2,1,0:T(2,128)(2,1)S(1)}, u32[]{:S(2)}, u32[]{:S(2)}) async-start(bf16[32,2,4096]{2,1,0:T(2,128)(2,1)} %bitcast.2), calls=%async_computation | async-start | bytes 1048576 | tf_op jit(solution)/shard_map/all_to_all | solution.py:297
  13.4 0.0 copy-done.13
  13.5 0.1 copy.27
  13.6 11.4 %all-to-all-done = bf16[32,2,4096]{2,1,0:T(2,128)(2,1)S(1)} async-done(((bf16[32,2,4096]{2,1,0:T(2,128)(2,1)}), bf16[32,2,4096]{2,1,0:T(2,128)(2,1)S(1)}, u32[]{:S(2)}, u32[]{:S(2)}) %all-to-all-start) | async-done | bytes 524320 | tf_op jit(solution)/shard_map/all_to_all | solution.py:297
  25.0 0.2 reshape.64.q_ref
  25.2 0.0 collective-permute-done.2.skb_ref.svb_ref
  25.2 0.0 collective-permute-done.kb_ref
  25.2 0.0 collective-permute-done.1.vb_ref
  25.2 0.0 copy-done.6
  25.2 0.0 copy-start.7
  25.2 1.2 copy-done.7
  26.4 9.0 %shard_map.136 = bf16[16,80,256]{2,1,0:T(8,128)(2,1)S(1)} custom-call(bf16[64,4096]{1,0:T(8,128)(2,1)S(1)} %reshape.64.q_ref, bf16[512,1024]{1,0:T(8,128)(2,1)S(1)} %copy-done.6, bf16[512,1024]{1,0:T(8,128)(2,1)} %collective-permute-done.kb_ref, bf16[512,1024]{1,0:T(8,128)(2,1)S(1)} %copy-done.7, bf16[512,1024]{1,0:T(8,128)(2,1)} %collective-permute-done.1.vb_ref, ...), custom_call_target="tpu_custom_call" | custom-call | flops 1400000000 | bytes 6291456 | tf_op jit(solution)/shard_map/pallas_call | solution.py:80
  35.5 15.6 %all_to_all.25.got_ref = bf16[16,80,256]{2,1,0:T(8,128)(2,1)S(1)} all-to-all(bf16[16,80,256]{2,1,0:T(8,128)(2,1)S(1)} %shard_map.136), channel_id=1, replica_groups=mesh['x'=4,'z'=4,'y'=4,'c'=2] {'z','y'}, dimensions={0} | all-to-all | bytes 1310720 | tf_op jit(solution)/shard_map/all_to_all | solution.py:302
  51.1 0.0 copy-done.5
  51.1 2.9 %shard_map.137 = (bf16[64,4096]{1,0:T(8,128)(2,1)S(1)}, bf16[64,4096]{1,0:T(8,128)(2,1)S(1)}) custom-call(s32[1]{0:T(128)} %bitcast.c_ref, bf16[16,80,256]{2,1,0:T(8,128)(2,1)S(1)} %all_to_all.25.got_ref, bf16[256,8192]{1,0:T(8,128)(2,1)S(1)} %copy-done.5), custom_call_target="tpu_custom_call" | custom-call | flops 270000000 | bytes 6291456 | tf_op jit(solution)/shard_map/pallas_call | solution.py:140
  54.0 0.0 copy-start.10
  54.0 1.4 collective-permute-start.3
  55.5 1.5 collective-permute-done.3
  57.0 0.1 add_convert_fusion.1
  57.1 1.1 reshape.66
  58.3 3.9 %all-to-all-start.2 = ((bf16[32,2,4096]{2,1,0:T(2,128)(2,1)}), bf16[32,2,4096]{2,1,0:T(2,128)(2,1)S(1)}, u32[]{:S(2)}, u32[]{:S(2)}) async-start(bf16[32,2,4096]{2,1,0:T(2,128)(2,1)} %reshape.66), calls=%async_computation.2 | async-start | bytes 1048576 | tf_op jit(solution)/shard_map/all_to_all | solution.py:306
  62.2 0.0 copy-done.10
  62.2 11.6 %all-to-all-done.2 = bf16[32,2,4096]{2,1,0:T(2,128)(2,1)S(1)} async-done(((bf16[32,2,4096]{2,1,0:T(2,128)(2,1)}), bf16[32,2,4096]{2,1,0:T(2,128)(2,1)S(1)}, u32[]{:S(2)}, u32[]{:S(2)}) %all-to-all-start.2) | async-done | bytes 524320 | tf_op jit(solution)/shard_map/all_to_all | solution.py:306
  73.9 0.4 convert_reduce_fusion.1
  74.3 0.0 copy-done.8
  74.3 0.2 multiply_reduce_fusion.1
  74.5 0.1 multiply_convert_fusion
  74.7 2.1 %broadcast_in_dim.20 = bf16[64,2,2,4096]{3,2,1,0:T(2,128)(2,1)S(1)} broadcast(bf16[2,2,4096]{2,1,0:T(2,128)(2,1)S(1)} %copy.28), dimensions={1,2,3} | broadcast | bytes 2129920 | tf_op jit(solution)/shard_map/broadcast_in_dim | solution.py:312
  76.8 36.1 %all_to_all.26 = bf16[128,2,4096]{2,1,0:T(2,128)(2,1)} all-to-all(bf16[128,2,4096]{2,1,0:T(2,128)(2,1)S(1)} %bitcast.38), channel_id=1, replica_groups=mesh['x'=4,'z'=4,'y'=4,'c'=2] {'x','z','y','c'}, dimensions={0} | all-to-all | bytes 4194304 | tf_op jit(solution)/shard_map/all_to_all | solution.py:313
  112.9 4.3 %reshape.70.x_ref = bf16[256,4096]{1,0:T(8,128)(2,1)} reshape(bf16[128,2,4096]{2,1,0:T(2,128)(2,1)} %all_to_all.26) | data formatting | bytes 4194304 | tf_op jit(solution)/shard_map/reshape | solution.py:313
  117.1 1.1 collective-permute-start.4
  118.2 2.8 %copy-done = bf16[1,8192,384]{2,1,0:T(8,128)(2,1)S(1)} copy-done((bf16[1,8192,384]{2,1,0:T(8,128)(2,1)S(1)}, bf16[1,8192,384]{2,1,0:T(8,128)(2,1)}, u32[]{:S(2)}) %copy-start) | copy-done | bytes 6291480
  121.0 2.8 %copy-done.1 = bf16[1,8192,384]{2,1,0:T(8,128)(2,1)S(1)} copy-done((bf16[1,8192,384]{2,1,0:T(8,128)(2,1)S(1)}, bf16[1,8192,384]{2,1,0:T(8,128)(2,1)}, u32[]{:S(2)}) %copy-start.1) | copy-done | bytes 6291480
  123.8 1.6 copy-done.4
  125.4 3.1 %shard_map.138 = (f32[256,384]{1,0:T(8,128)S(1)}, f32[256,384]{1,0:T(8,128)S(1)}) custom-call(s32[1]{0:T(128)} %bitcast.c_ref, bf16[256,4096]{1,0:T(8,128)(2,1)S(1)} %copy-done.4, bf16[8192,384]{1,0:T(8,128)(2,1)S(1)} %bitcast.28, bf16[8192,384]{1,0:T(8,128)(2,1)S(1)} %bitcast.32), custom_call_target="tpu_custom_call" | custom-call | flops 1600000000 | bytes 9437184 | tf_op jit(solution)/shard_map/pallas_call | solution.py:175
  128.5 0.0 collective-permute-done.4.x_ref
  128.5 0.0 slice-done
  128.5 0.0 slice-done.1
  128.5 0.0 copy-start.2
  128.6 2.8 %copy-done.2 = bf16[1,8192,384]{2,1,0:T(8,128)(2,1)S(1)} copy-done((bf16[1,8192,384]{2,1,0:T(8,128)(2,1)S(1)}, bf16[1,8192,384]{2,1,0:T(8,128)(2,1)}, u32[]{:S(2)}) %copy-start.2) | copy-done | bytes 6291480
  131.3 7.7 %shard_map.139 = (bf16[256,384]{1,0:T(8,128)(2,1)S(1)}, bf16[256,4096]{1,0:T(8,128)(2,1)S(1)}) custom-call(s32[1]{0:T(128)} %bitcast.c_ref, bf16[256,4096]{1,0:T(8,128)(2,1)S(1)} %collective-permute-done.4.x_ref, bf16[8192,384]{1,0:T(8,128)(2,1)S(1)} %bitcast.31, bf16[8192,384]{1,0:T(8,128)(2,1)S(1)} %bitcast.33, f32[256,384]{1,0:T(8,128)S(1)} %get-tuple-element.13.g0_ref, ...), custom_call_target="tpu_custom_call" | custom-call | flops 2400000000 | bytes 15728640 | tf_op jit(solution)/shard_map/pallas_call | solution.py:223
  139.1 0.3 collective-permute-start.5
  139.3 0.0 copy-start.3
  139.3 2.8 %copy-done.3 = bf16[1,384,8192]{2,1,0:T(8,128)(2,1)S(1)} copy-done((bf16[1,384,8192]{2,1,0:T(8,128)(2,1)S(1)}, bf16[1,384,8192]{2,1,0:T(8,128)(2,1)}, u32[]{:S(2)}) %copy-start.3) | copy-done | bytes 6291480
  142.1 2.1 %shard_map.140 = bf16[256,4096]{1,0:T(8,128)(2,1)S(1)} custom-call(s32[1]{0:T(128)} %bitcast.c_ref, bf16[256,384]{1,0:T(8,128)(2,1)S(1)} %get-tuple-element.15.inner_ref, bf16[384,8192]{1,0:T(8,128)(2,1)S(1)} %bitcast.35), custom_call_target="tpu_custom_call" | custom-call | flops 800000000 | bytes 6291456 | tf_op jit(solution)/shard_map/pallas_call | solution.py:255
  144.2 0.0 collective-permute-done.5
  144.3 0.8 add_convert_fusion
  145.0 2.7 %reshape.71 = bf16[128,2,4096]{2,1,0:T(2,128)(2,1)} reshape(bf16[256,4096]{1,0:T(8,128)(2,1)S(1)} %add_convert_fusion) | data formatting | bytes 4194304 | tf_op jit(solution)/shard_map/reshape | solution.py:319
  147.7 4.1 %all-to-all-start.4 = ((bf16[128,2,4096]{2,1,0:T(2,128)(2,1)}), bf16[128,2,4096]{2,1,0:T(2,128)(2,1)S(1)}, u32[]{:S(2)}, u32[]{:S(2)}) async-start(bf16[128,2,4096]{2,1,0:T(2,128)(2,1)} %reshape.71), calls=%async_computation.4 | async-start | bytes 4194304 | tf_op jit(solution)/shard_map/all_to_all | solution.py:320
  151.8 0.0 copy-done.11
  151.8 0.1 fusion
  151.9 0.1 copy.29
  152.0 30.3 %all-to-all-done.4 = bf16[128,2,4096]{2,1,0:T(2,128)(2,1)S(1)} async-done(((bf16[128,2,4096]{2,1,0:T(2,128)(2,1)}), bf16[128,2,4096]{2,1,0:T(2,128)(2,1)S(1)}, u32[]{:S(2)}, u32[]{:S(2)}) %all-to-all-start.4) | async-done | bytes 2097184 | tf_op jit(solution)/shard_map/all_to_all | solution.py:320
  182.3 2.2 %convert_reduce_fusion = f32[4,2,2,4096]{3,2,1,0:T(2,128)S(1)} fusion(bf16[4,16,2,2,4096]{4,3,2,1,0:T(2,128)(2,1)S(1)} %bitcast.37), kind=kLoop, calls=%fused_computation | loop fusion | flops 2031616 | bytes 2359296 | tf_op jit(solution)/shard_map/reduce_sum | solution.py:321
  184.6 0.2 multiply_reduce_fusion
  184.8 0.7 add_convert_fusion.2
  (23 shorter events, 0.2 us)
Async XLA Ops:
  0.0 3.7 %copy-start.9 = (bf16[2,8192]{1,0:T(2,128)(2,1)S(1)}, bf16[2,8192]{1,0:T(2,128)(2,1)}, u32[]{:S(2)}) copy-start(bf16[2,8192]{1,0:T(2,128)(2,1)} %param.14) | copy-start | bytes 98308
  0.0 13.4 %copy-start.13 = (s32[64]{0:T(128)S(1)}, s32[64]{0:T(128)}, u32[]{:S(2)}) copy-start(s32[64]{0:T(128)} %param.19) | copy-start | bytes 772
  0.0 25.2 %collective-permute-start = (bf16[512,1024]{1,0:T(8,128)(2,1)}, bf16[512,1024]{1,0:T(8,128)(2,1)}, u32[]{:S(2)}, u32[]{:S(2)}) collective-permute-start(bf16[512,1024]{1,0:T(8,128)(2,1)} %ka_ref.1), channel_id=1, source_target_pairs={{0,1},{1,0},{2,3},{3,2},{4,5},{5,4},{6,7},{7,6},{8,9},{9,8},{10,11... | collective-permute-start | bytes 3145736 | tf_op jit(solution)/shard_map/ppermute | solution.py:293
  1.4 23.8 %collective-permute-start.1 = (bf16[512,1024]{1,0:T(8,128)(2,1)}, bf16[512,1024]{1,0:T(8,128)(2,1)}, u32[]{:S(2)}, u32[]{:S(2)}) collective-permute-start(bf16[512,1024]{1,0:T(8,128)(2,1)} %va_ref.1), channel_id=1, source_target_pairs={{0,1},{1,0},{2,3},{3,2},{4,5},{5,4},{6,7},{7,6},{8,9},{9,8},{10,11... | collective-permute-start | bytes 3145736 | tf_op jit(solution)/shard_map/ppermute | solution.py:294
  2.9 22.3 %copy-start.6 = (bf16[512,1024]{1,0:T(8,128)(2,1)S(1)}, bf16[512,1024]{1,0:T(8,128)(2,1)}, u32[]{:S(2)}) copy-start(bf16[512,1024]{1,0:T(8,128)(2,1)} %ka_ref.1) | copy-start | bytes 3145732
  3.2 22.0 %collective-permute-start.2 = (bf16[128,2048]{1,0:T(8,128)(2,1)S(1)}, bf16[128,2048]{1,0:T(8,128)(2,1)S(1)}, u32[]{:S(2)}, u32[]{:S(2)}) collective-permute-start(bf16[128,2048]{1,0:T(8,128)(2,1)S(1)} %reshape.65.ska_ref.sva_ref), channel_id=1, source_target_pairs={{0,1},{1,0},{2,3},{3,2},{4,5},{5,4},{6,7},{7,6},{8,9},{9,8},{10,11... | collective-permute-start | bytes 1572872 | tf_op jit(solution)/shard_map/ppermute | solution.py:292
  5.1 19.9 %all-to-all-start = ((bf16[32,2,4096]{2,1,0:T(2,128)(2,1)}), bf16[32,2,4096]{2,1,0:T(2,128)(2,1)S(1)}, u32[]{:S(2)}, u32[]{:S(2)}) async-start(bf16[32,2,4096]{2,1,0:T(2,128)(2,1)} %bitcast.2), calls=%async_computation | async-start | bytes 1048576 | tf_op jit(solution)/shard_map/all_to_all | solution.py:297
  25.2 1.2 copy-start.7
  26.4 24.7 %copy-start.5 = (bf16[256,8192]{1,0:T(8,128)(2,1)S(1)}, bf16[256,8192]{1,0:T(8,128)(2,1)}, u32[]{:S(2)}) copy-start(bf16[256,8192]{1,0:T(8,128)(2,1)} %w_ref.1) | copy-start | bytes 12582916
  54.0 8.2 %copy-start.10 = (bf16[8192]{0:T(1024)(128)(2,1)S(1)}, bf16[8192]{0:T(1024)(128)(2,1)}, u32[]{:S(2)}) copy-start(bf16[8192]{0:T(1024)(128)(2,1)} %param.22) | copy-start | bytes 49156
  54.0 3.0 %collective-permute-start.3 = (bf16[64,4096]{1,0:T(8,128)(2,1)S(1)}, bf16[64,4096]{1,0:T(8,128)(2,1)S(1)}, u32[]{:S(2)}, u32[]{:S(2)}) collective-permute-start(bf16[64,4096]{1,0:T(8,128)(2,1)S(1)} %get-tuple-element.12), channel_id=1, source_target_pairs={{0,1},{1,0},{2,3},{3,2},{4,5},{5,4},{6,7},{7,6},{8,9},{9,8},{10,11... | collective-permute-start | bytes 1572872 | tf_op jit(solution)/shard_map/ppermute | solution.py:304
  57.0 17.3 %copy-start.8 = (bf16[2,8192]{1,0:T(2,128)(2,1)S(1)}, bf16[2,8192]{1,0:T(2,128)(2,1)}, u32[]{:S(2)}) copy-start(bf16[2,8192]{1,0:T(2,128)(2,1)} %param.20) | copy-start | bytes 98308
  58.3 15.6 %all-to-all-start.2 = ((bf16[32,2,4096]{2,1,0:T(2,128)(2,1)}), bf16[32,2,4096]{2,1,0:T(2,128)(2,1)S(1)}, u32[]{:S(2)}, u32[]{:S(2)}) async-start(bf16[32,2,4096]{2,1,0:T(2,128)(2,1)} %reshape.66), calls=%async_computation.2 | async-start | bytes 1048576 | tf_op jit(solution)/shard_map/all_to_all | solution.py:306
  112.9 15.6 %slice-start = ((s8[6291456]{0:T(1024)(128)(4,1)}), s8[2097152]{0:T(1024)(128)(4,1)S(1)}, s32[]{:S(2)}) async-start(s8[6291456]{0:T(1024)(128)(4,1)} %bitcast.29), calls=%async_computation.5 | async-start | bytes 4194304
  117.1 11.4 %collective-permute-start.4 = (bf16[256,4096]{1,0:T(8,128)(2,1)}, bf16[256,4096]{1,0:T(8,128)(2,1)S(1)}, u32[]{:S(2)}, u32[]{:S(2)}) collective-permute-start(bf16[256,4096]{1,0:T(8,128)(2,1)} %reshape.70.x_ref), channel_id=1, source_target_pairs={{0,1},{1,0},{2,3},{3,2},{4,5},{5,4},{6,7},{7,6},{8,9},{9,8},{10,11... | collective-permute-start | bytes 6291464 | tf_op jit(solution)/shard_map/ppermute | solution.py:314
  118.2 2.8 %copy-start = (bf16[1,8192,384]{2,1,0:T(8,128)(2,1)S(1)}, bf16[1,8192,384]{2,1,0:T(8,128)(2,1)}, u32[]{:S(2)}) copy-start(bf16[1,8192,384]{2,1,0:T(8,128)(2,1)} %param.25) | copy-start | bytes 18874372
  121.0 2.8 %copy-start.1 = (bf16[1,8192,384]{2,1,0:T(8,128)(2,1)S(1)}, bf16[1,8192,384]{2,1,0:T(8,128)(2,1)}, u32[]{:S(2)}) copy-start(bf16[1,8192,384]{2,1,0:T(8,128)(2,1)} %param.26) | copy-start | bytes 18874372
  123.8 1.6 copy-start.4
  125.4 3.1 %slice-start.1 = ((s8[6291456]{0:T(1024)(128)(4,1)}), s8[4194304]{0:T(1024)(128)(4,1)S(1)}, s32[]{:S(2)}) async-start(s8[6291456]{0:T(1024)(128)(4,1)} %bitcast.29), calls=%async_computation.6 | async-start | bytes 8388608
  128.5 2.8 %copy-start.2 = (bf16[1,8192,384]{2,1,0:T(8,128)(2,1)S(1)}, bf16[1,8192,384]{2,1,0:T(8,128)(2,1)}, u32[]{:S(2)}) copy-start(bf16[1,8192,384]{2,1,0:T(8,128)(2,1)} %param.26) | copy-start | bytes 18874372
  139.1 5.2 %collective-permute-start.5 = (bf16[256,4096]{1,0:T(8,128)(2,1)S(1)}, bf16[256,4096]{1,0:T(8,128)(2,1)S(1)}, u32[]{:S(2)}, u32[]{:S(2)}) collective-permute-start(bf16[256,4096]{1,0:T(8,128)(2,1)S(1)} %get-tuple-element.16), channel_id=1, source_target_pairs={{0,1},{1,0},{2,3},{3,2},{4,5},{5,4},{6,7},{7,6},{8,9},{9,8},{10,11... | collective-permute-start | bytes 6291464 | tf_op jit(solution)/shard_map/ppermute | solution.py:317
  139.3 2.8 %copy-start.3 = (bf16[1,384,8192]{2,1,0:T(8,128)(2,1)S(1)}, bf16[1,384,8192]{2,1,0:T(8,128)(2,1)}, u32[]{:S(2)}) copy-start(bf16[1,384,8192]{2,1,0:T(8,128)(2,1)} %param.27) | copy-start | bytes 18874372
  147.7 4.1 %copy-start.11 = (f32[2,2]{1,0:T(2,128)S(1)}, f32[2,2]{1,0:T(2,128)}, u32[]{:S(2)}) copy-start(f32[2,2]{1,0:T(2,128)} %param.24) | copy-start | bytes 52
  147.7 4.1 %copy-start.12 = (s32[2,2]{1,0:T(2,128)S(1)}, s32[2,2]{1,0:T(2,128)}, u32[]{:S(2)}) copy-start(s32[2,2]{1,0:T(2,128)} %param.23) | copy-start | bytes 52
  147.7 34.6 %all-to-all-start.4 = ((bf16[128,2,4096]{2,1,0:T(2,128)(2,1)}), bf16[128,2,4096]{2,1,0:T(2,128)(2,1)S(1)}, u32[]{:S(2)}, u32[]{:S(2)}) async-start(bf16[128,2,4096]{2,1,0:T(2,128)(2,1)} %reshape.71), calls=%async_computation.4 | async-start | bytes 4194304 | tf_op jit(solution)/shard_map/all_to_all | solution.py:320

commit v2 on v1

v2 whole, which is shorter than its diff:
```python
import functools

import jax
import jax.numpy as jnp
from jax import lax
from jax.experimental import pallas as pl
from jax.experimental.pallas import tpu as pltpu
from jax.sharding import Mesh, PartitionSpec as P

HEADS = 64
KV = 8
HD = 128
D = 8192
HALF = D // 2
EPS = 1e-05
NEG = -1e30
LOG2E = 1.4426950408889634
SCALE = LOG2E / HD**0.5
BF = jnp.bfloat16
F32 = jnp.float32
ALL = ("x", "z", "y", "c")
PLANE = ("z", "y", "c")
SWAP = [(0, 1), (1, 0)]
MB = 1 << 20


def device(x, z, y, c):
    return ((x * 4 + z) * 4 + y) * 2 + c


def wide_groups():
    four = range(4)
    zeros = [[device(x, z, y, 0) for z in four for x in four] for y in four]
    return zeros + [[device(x, z, y, 1) for y in four for x in four] for z in four]


def line_shift(step):
    pairs = []
    for z in range(4):
        for y in range(4):
            pairs.append(((z * 4 + y) * 2, (z * 4 + (y + step) % 4) * 2))
            pairs.append(((z * 4 + y) * 2 + 1, (((z + step) % 4) * 4 + y) * 2 + 1))
    return pairs


def dot(a, b):
    return jnp.dot(a, b, preferred_element_type=F32)


def dot_t(a, b):
    return lax.dot_general(a, b, (((1,), (1,)), ((), ())), preferred_element_type=F32)


def fetch_kernel(*refs):
    sources, targets, sems = refs[1:4], refs[4:7], refs[7]
    copies = []
    for source, target in zip(sources, targets):
        rows = source.shape[0] // 4
        for part in range(4):
            at = pl.ds(part * rows, rows)
            copies.append(pltpu.make_async_copy(source.at[at], target.at[at], sems.at[len(copies)]))
    for copy in copies:
        copy.start()
    for copy in copies:
        copy.wait()


def fetch(after, *arrays):
    return pl.pallas_call(
        fetch_kernel,
        in_specs=[pl.BlockSpec(memory_space=pl.ANY)] * 4,
        out_specs=[pl.BlockSpec(memory_space=pltpu.VMEM)] * 3,
        out_shape=[pltpu.VMEM(a.shape, a.dtype) for a in arrays],
        scratch_shapes=[pltpu.SemaphoreType.DMA((12,))],
        compiler_params=pltpu.CompilerParams(vmem_limit_bytes=4 * MB),
        cost_estimate=pl.CostEstimate(flops=0, bytes_accessed=22 * MB, transcendentals=0),
    )(after, *[in_hbm(a) for a in arrays])


def in_vmem(array):
    return pltpu.with_memory_space_constraint(array, pltpu.VMEM)


def in_hbm(array):
    return pltpu.with_memory_space_constraint(array, pltpu.HBM)


def attend_kernel(q_ref, ka_ref, kb_ref, va_ref, vb_ref, ska_ref, skb_ref, sva_ref, svb_ref, left_ref, out_ref):
    rows = 64
    q = jnp.concatenate([q_ref[:, g * HD : (g + 1) * HD] for g in range(4)], axis=0)
    row = lax.broadcasted_iota(jnp.int32, (4 * rows, 2 * rows), 0) % rows
    col = lax.broadcasted_iota(jnp.int32, (4 * rows, 2 * rows), 1)
    own_row = row == col // 2
    spot = col % 2
    left = left_ref[...]
    scores = [
        dot_t(q, ka_ref[...]) * SCALE,
        dot_t(q, kb_ref[...]) * SCALE,
        jnp.where(own_row & (spot < left[:, 0:1]), dot_t(q, ska_ref[...]) * SCALE, NEG),
        jnp.where(own_row & (spot < left[:, 1:2]), dot_t(q, skb_ref[...]) * SCALE, NEG),
    ]
    tops = [jnp.max(s, axis=1, keepdims=True) for s in scores]
    top = jnp.maximum(jnp.maximum(tops[0], tops[1]), jnp.maximum(tops[2], tops[3]))
    top = top.astype(BF).astype(F32)
    total = jnp.zeros((4 * rows, 1), F32)
    acc = jnp.zeros((4 * rows, HD), F32)
    for s, v in zip(scores, (va_ref, vb_ref, sva_ref, svb_ref)):
        prob = jnp.exp2(s - top)
        total = total + jnp.sum(prob, axis=1, keepdims=True)
        acc = acc + dot(prob.astype(BF), v[...])
    eye = lax.broadcasted_iota(jnp.int32, (4 * rows, 4 * rows), 0) == lax.broadcasted_iota(
        jnp.int32, (4 * rows, 4 * rows), 1
    )
    top_row = jnp.sum(jnp.where(eye, top, 0.0), axis=0, keepdims=True)
    total_row = jnp.sum(jnp.where(eye, total, 0.0), axis=0, keepdims=True)
    total_high = total_row.astype(BF).astype(F32)
    total_low = total_row - total_high
    line = lax.broadcasted_iota(jnp.int32, (16, 4 * rows), 0)
    for k in range(2):
        for j in range(2):
            g = 2 * k + j
            out_ref[k, 0:rows, j * HD : (j + 1) * HD] = acc[g * rows : (g + 1) * rows].astype(BF)
        part = slice(k * 2 * rows, (k + 1) * 2 * rows)
        high = jnp.concatenate([top_row[:, part], total_high[:, part]], axis=1)
        low = jnp.concatenate([top_row[:, part], total_low[:, part]], axis=1)
        tail = jnp.where(line == 0, high, jnp.where(line == 1, low, 0.0))
        out_ref[k, rows : rows + 16, :] = tail.astype(BF)


def attend(q, ka, kb, va, vb, sa, sb, left):
    full = lambda n: pl.BlockSpec((n, HD), lambda i: (0, i))
    second = lambda n: pl.BlockSpec((n, HD), lambda i: (0, i + KV))
    return pl.pallas_call(
        attend_kernel,
        grid=(KV,),
        in_specs=[
            pl.BlockSpec((64, 4 * HD), lambda i: (0, i)),
            full(512),
            full(512),
            full(512),
            full(512),
            full(128),
            full(128),
            second(128),
            second(128),
            pl.BlockSpec((256, 2), lambda i: (0, 0)),
        ],
        out_specs=pl.BlockSpec((2, 80, 2 * HD), lambda i: (i, 0, 0)),
        out_shape=jax.ShapeDtypeStruct((16, 80, 2 * HD), BF),
        compiler_params=pltpu.CompilerParams(vmem_limit_bytes=16 * MB),
        cost_estimate=pl.CostEstimate(flops=1400000000, bytes_accessed=6 * MB, transcendentals=2700000),
    )(q, in_hbm(ka), in_hbm(kb), in_hbm(va), in_hbm(vb), sa, sb, sa, sb, left)


def columns_of(w_ref, half, buffer, sems):
    width = HALF // 4
    return [
        pltpu.make_async_copy(
            w_ref.at[:, pl.ds(pl.multiple_of(half * HALF + part * width, width), width)],
            buffer.at[:, pl.ds(part * width, width)],
            sems.at[part],
        )
        for part in range(4)
    ]


def project_parts(copies, attended, buffer, out_ref):
    width = HALF // 4
    for part, copy in enumerate(copies):
        copy.wait()
        at = slice(part * width, (part + 1) * width)
        out_ref[:, at] = dot(attended, buffer[:, at]).astype(BF)


def project_kernel(at_ref, got_ref, w_ref, out_ref, att_ref, buffer, sems):
    rows = 64
    copies = columns_of(w_ref, 1 - at_ref[0], buffer, sems)
    for copy in copies:
        copy.start()
    tops = [got_ref[s, rows : rows + 1, 0 : 2 * rows].astype(F32) for s in range(16)]
    sums = [
        got_ref[s, rows : rows + 1, 2 * rows :].astype(F32)
        + got_ref[s, rows + 1 : rows + 2, 2 * rows :].astype(F32)
        for s in range(16)
    ]
    top = functools.reduce(jnp.maximum, tops)
    factors = [jnp.exp2(t - top) for t in tops]
    total = functools.reduce(jnp.add, [f * s for f, s in zip(factors, sums)])
    lane = lax.broadcasted_iota(jnp.int32, (rows, 2 * rows), 1)
    line = lax.broadcasted_iota(jnp.int32, (rows, 2 * rows), 0)
    for j in range(2):
        here = lane == line + j * rows
        acc = jnp.zeros((rows, HD), F32)
        for s in range(16):
            share = jnp.sum(jnp.where(here, factors[s] / total, 0.0), axis=1, keepdims=True)
            acc = acc + got_ref[s, 0:rows, j * HD : (j + 1) * HD].astype(F32) * share
        att_ref[:, j * HD : (j + 1) * HD] = acc.astype(BF)
    project_parts(copies, att_ref[...], buffer, out_ref)


def project_other(at, got, w_out):
    return pl.pallas_call(
        project_kernel,
        in_specs=[
            pl.BlockSpec(memory_space=pltpu.SMEM),
            pl.BlockSpec(memory_space=pltpu.VMEM),
            pl.BlockSpec(memory_space=pl.ANY),
        ],
        out_specs=[pl.BlockSpec(memory_space=pltpu.VMEM)] * 2,
        out_shape=[jax.ShapeDtypeStruct((64, HALF), BF), jax.ShapeDtypeStruct((64, 256), BF)],
        scratch_shapes=[pltpu.VMEM((256, HALF), BF), pltpu.SemaphoreType.DMA((4,))],
        compiler_params=pltpu.CompilerParams(vmem_limit_bytes=16 * MB),
        cost_estimate=pl.CostEstimate(flops=140000000, bytes_accessed=3 * MB, transcendentals=0),
    )(at, got, in_hbm(w_out))


def project_mine_kernel(at_ref, att_ref, w_ref, out_ref, buffer, sems):
    copies = columns_of(w_ref, at_ref[0], buffer, sems)
    for copy in copies:
        copy.start()
    project_parts(copies, att_ref[...], buffer, out_ref)


def project_mine(at, attended, w_out):
    return pl.pallas_call(
        project_mine_kernel,
        in_specs=[
            pl.BlockSpec(memory_space=pltpu.SMEM),
            pl.BlockSpec(memory_space=pltpu.VMEM),
            pl.BlockSpec(memory_space=pl.ANY),
        ],
        out_specs=pl.BlockSpec(memory_space=pltpu.VMEM),
        out_shape=jax.ShapeDtypeStruct((64, HALF), BF),
        scratch_shapes=[pltpu.VMEM((256, HALF), BF), pltpu.SemaphoreType.DMA((4,))],
        compiler_params=pltpu.CompilerParams(vmem_limit_bytes=16 * MB),
        cost_estimate=pl.CostEstimate(flops=140000000, bytes_accessed=3 * MB, transcendentals=0),
    )(at, attended, in_hbm(w_out))


def rolled(place, back):
    return pl.multiple_of(((place + 4 - back) & 3) * 16, 16)


def first_kernel(at_ref, p0, p1, p2, p3, wg_ref, wu_ref, g_ref, u_ref):
    @pl.when(pl.program_id(0) == 0)
    def _():
        g_ref[...] = jnp.zeros_like(g_ref)
        u_ref[...] = jnp.zeros_like(u_ref)

    pieces = (p0, p1, p2, p3)
    x = jnp.concatenate(
        [pieces[a][pl.ds(rolled(at_ref[1], b), 16), :] for a in range(4) for b in range(4)], axis=0
    )
    g_ref[...] += dot(x, wg_ref[...])
    u_ref[...] += dot(x, wu_ref[...])


def expert_first(at, pieces, w_gate, w_up):
    units = w_gate.shape[1]
    block = 1024
    return pl.pallas_call(
        first_kernel,
        grid_spec=pltpu.PrefetchScalarGridSpec(
            num_scalar_prefetch=1,
            grid=(4,),
            in_specs=[pl.BlockSpec((64, block), lambda n, t: (0, n))] * 4
            + [pl.BlockSpec((block, units), lambda n, t: (n + 4 * t[0], 0))] * 2,
            out_specs=[pl.BlockSpec((256, units), lambda n, t: (0, 0))] * 2,
        ),
        out_shape=[jax.ShapeDtypeStruct((256, units), F32)] * 2,
        compiler_params=pltpu.CompilerParams(vmem_limit_bytes=12 * MB),
        cost_estimate=pl.CostEstimate(flops=16000000000, bytes_accessed=9 * MB, transcendentals=0),
    )(at, *pieces, in_vmem(w_gate), in_vmem(w_up))


def second_kernel(at_ref, p0, p1, p2, p3, wg_ref, wu_ref, g0_ref, u0_ref, wd_ref, inner_ref, out_ref, g_ref, u_ref):
    n = pl.program_id(0)

    @pl.when(n == 0)
    def _():
        g_ref[...] = g0_ref[...]
        u_ref[...] = u0_ref[...]

    @pl.when(n < 4)
    def _():
        pieces = (p0, p1, p2, p3)
        x = jnp.concatenate(
            [pieces[b][pl.ds(rolled(at_ref[2], a), 16), :] for a in range(4) for b in range(4)], axis=0
        )
        g_ref[...] += dot(x, wg_ref[...])
        u_ref[...] += dot(x, wu_ref[...])

    @pl.when(n == 3)
    def _():
        g = g_ref[...]
        inner_ref[...] = (g / (1.0 + jnp.exp(-g)) * u_ref[...]).astype(BF)

    @pl.when(n >= 4)
    def _():
        value = dot(inner_ref[...], wd_ref[...]).astype(BF)
        for a in range(4):
            for b in range(4):
                line = (4 * a + b) * 16
                out_ref[b, pl.ds(rolled(at_ref[2], a), 16), :] = value[line : line + 16]


def expert_second(at, pieces, w_gate, w_up, gate, up, w_down):
    units = w_gate.shape[1]
    block = 1024
    early = lambda n: jnp.minimum(n, 3)
    late = lambda n: jnp.maximum(n - 4, 0)
    whole = pl.BlockSpec((256, units), lambda n, t: (0, 0))
    return pl.pallas_call(
        second_kernel,
        grid_spec=pltpu.PrefetchScalarGridSpec(
            num_scalar_prefetch=1,
            grid=(8,),
            in_specs=[pl.BlockSpec((64, block), lambda n, t: (0, early(n)))] * 4
            + [pl.BlockSpec((block, units), lambda n, t: (early(n) + 4 * (1 - t[0]), 0))] * 2
            + [whole, whole, pl.BlockSpec((units, block), lambda n, t: (0, late(n) + 4 * (1 - t[0])))],
            out_specs=[whole, pl.BlockSpec((4, 64, block), lambda n, t: (0, 0, late(n)))],
            scratch_shapes=[pltpu.VMEM((256, units), F32), pltpu.VMEM((256, units), F32)],
        ),
        out_shape=[
            jax.ShapeDtypeStruct((256, units), BF),
            jax.ShapeDtypeStruct((4, 64, HALF), BF),
        ],
        compiler_params=pltpu.CompilerParams(vmem_limit_bytes=12 * MB),
        cost_estimate=pl.CostEstimate(flops=2400000000, bytes_accessed=15 * MB, transcendentals=0),
    )(at, *pieces, in_vmem(w_gate), in_vmem(w_up), gate, up, in_vmem(w_down))


def third_kernel(at_ref, inner_ref, wd_ref, out_ref):
    value = dot(inner_ref[...], wd_ref[...]).astype(BF)
    for a in range(4):
        for b in range(4):
            line = (4 * a + b) * 16
            out_ref[a, pl.ds(rolled(at_ref[1], b), 16), :] = value[line : line + 16]


def expert_third(at, inner, w_down):
    rows, units = inner.shape
    block = 1024
    return pl.pallas_call(
        third_kernel,
        grid_spec=pltpu.PrefetchScalarGridSpec(
            num_scalar_prefetch=1,
            grid=(4,),
            in_specs=[
                pl.BlockSpec((rows, units), lambda n, t: (0, 0)),
                pl.BlockSpec((units, block), lambda n, t: (0, n + 4 * t[0])),
            ],
            out_specs=pl.BlockSpec((4, 64, block), lambda n, t: (0, 0, n)),
        ),
        out_shape=jax.ShapeDtypeStruct((4, 64, HALF), BF),
        compiler_params=pltpu.CompilerParams(vmem_limit_bytes=12 * MB),
        cost_estimate=pl.CostEstimate(flops=800000000, bytes_accessed=6 * MB, transcendentals=0),
    )(at, inner, in_vmem(w_down))


def swap(value):
    return lax.ppermute(value, "c", SWAP)


def local(
    queries,
    prefix_keys,
    prefix_values,
    suffix_keys,
    suffix_values,
    suffix_lengths,
    hidden_in,
    w_out,
    norm_gain,
    expert_ids,
    expert_weights,
    w_gate,
    w_up,
    w_down,
):
    c = lax.axis_index("c").astype(jnp.int32)
    z = lax.axis_index("z").astype(jnp.int32)
    y = lax.axis_index("y").astype(jnp.int32)
    chip = 4 * z + y
    at = jnp.stack([c, jnp.where(c == 0, z, y), jnp.where(c == 0, y, z)])

    def in_order(own, got, axis):
        return jnp.where(
            c == 0, jnp.concatenate([own, got], axis=axis), jnp.concatenate([got, own], axis=axis)
        )

    q = queries.reshape(2, 16, 2, 2 * HD).transpose(2, 0, 1, 3).reshape(1, 2, 2, HALF)
    q = jnp.broadcast_to(q, (16, 2, 2, HALF)).reshape(32, 2, HALF)
    keys_b = swap(prefix_keys)
    values_b = swap(prefix_values)
    suffix_keys_b = swap(suffix_keys)
    suffix_values_b = swap(suffix_values)
    q = lax.all_to_all(q, PLANE, split_axis=0, concat_axis=0, tiled=True).reshape(64, HALF)
    suffix = jnp.concatenate([suffix_keys, suffix_values], axis=-1).reshape(128, 2 * KV * HD)
    suffix_b = jnp.concatenate([suffix_keys_b, suffix_values_b], axis=-1).reshape(128, 2 * KV * HD)
    first = 4 * chip
    left = jnp.stack([suffix_lengths - (first + 2 * c), suffix_lengths - (first + 2 * (1 - c))], axis=1)
    left = jnp.tile(left.astype(jnp.int32), (4, 1))
    hidden = in_order(
        lax.dynamic_slice_in_dim(hidden_in, c * HALF, HALF, 1),
        swap(lax.dynamic_slice_in_dim(hidden_in, (1 - c) * HALF, HALF, 1)),
        0,
    ).astype(F32)
    match = expert_ids[:, :, None] == jnp.arange(4, dtype=jnp.int32)[None, None, :]
    weights = jnp.sum(jnp.where(match, expert_weights[:, :, None], 0.0), axis=1)
    weights = in_order(weights, swap(weights), 0)
    gain = lax.dynamic_slice_in_dim(norm_gain, c * HALF, HALF, 0).astype(F32)

    parts = attend(q, prefix_keys, keys_b, prefix_values, values_b, suffix, suffix_b, left)
    parts = lax.all_to_all(parts, ("z", "y"), split_axis=0, concat_axis=0, tiled=True)
    other, attended = project_other(at, parts, w_out)
    other = swap(other)
    mine = project_mine(at, attended, w_out)
    summed = (mine.astype(F32) + other.astype(F32)).astype(BF).reshape(16, 4, HALF)
    summed = lax.all_to_all(summed, ("z", "y"), split_axis=0, concat_axis=0, tiled=True)
    residual = hidden + jnp.sum(summed.astype(F32), axis=0)
    square = jnp.sum(residual * residual, axis=-1, keepdims=True)
    mean_square = (square + swap(square)) * (1.0 / D)
    normed = (residual * lax.rsqrt(mean_square + EPS) * gain).astype(BF)
    wide = wide_groups()
    sent = jnp.broadcast_to(normed[None], (16, 4, HALF))
    own = lax.all_to_all(
        sent, ALL, split_axis=0, concat_axis=0, tiled=True, axis_index_groups=wide
    ).reshape(64, HALF)
    pieces = [own] + [lax.ppermute(own, PLANE, line_shift(s)) for s in (1, 2, 3)]
    w_gate, w_up, w_down = fetch(own, w_gate[0], w_up[0], w_down[0])
    pieces_b = [swap(piece) for piece in pieces]
    gate, up = expert_first(at, pieces, w_gate, w_up)
    inner, other_out = expert_second(at, pieces_b, w_gate, w_up, gate, up, w_down)
    other_out = swap(other_out)
    mine_out = expert_third(at, inner, w_down)
    out = [(mine_out[s].astype(F32) + other_out[s].astype(F32)).astype(BF) for s in range(4)]
    out = [out[0]] + [lax.ppermute(out[s], PLANE, line_shift(4 - s)) for s in (1, 2, 3)]
    out = functools.reduce(jnp.add, [piece.astype(F32) for piece in out]).astype(BF)
    out = lax.all_to_all(
        out.reshape(16, 4, HALF), ALL, split_axis=0, concat_axis=0, tiled=True, axis_index_groups=wide
    )
    out = out.reshape(4, 4, 4, HALF).astype(F32)
    mixed = residual + jnp.sum(out * weights.T[None, :, :, None], axis=(0, 1))
    mixed = mixed.astype(BF)
    kept = lax.dynamic_slice_in_dim(mixed, 2 * c, 2, 0)
    got = swap(lax.dynamic_slice_in_dim(mixed, 2 * (1 - c), 2, 0))
    return in_order(kept, got, 1)


def solution(mesh):
    grid = Mesh(mesh.devices.reshape(4, 4, 4, 2), ALL)
    placed = (
        P(ALL, None),
        P(PLANE, None),
        P(PLANE, None),
        P("x", PLANE, None),
        P("x", PLANE, None),
        P("x"),
        P(ALL, None),
        P(PLANE, None),
        P(),
        P(ALL, None),
        P(ALL, None),
        P("x", None, PLANE),
        P("x", None, PLANE),
        P("x", PLANE, None),
    )
    return jax.shard_map(
        local, mesh=grid, in_specs=placed, out_specs=P(ALL, None), check_vma=False
    )
```

time: 186 us -> 160 us (0.86)
  blocking collectives: 51.7 us -> 15.6 us
  local copies, waits for them, and re-layouts: 26.1 us -> 6.3 us
  starting transfers between devices: 21.1 us -> 39.8 us
  Pallas kernels: 24.9 us -> 33.9 us
  waiting for transfers between devices: 54.9 us -> 57.3 us
    all_to_all x2 -> x1, blocking collectives: 51.7 us -> 15.6 us  [local(): lax.all_to_all(sent, ALL, split_axis=0, concat_axis=0, tiled=True, axis_i...]
    ppermute x6 -> x20, waiting for transfers between devices: 1.55 us -> 19.4 us  [the longest x3 13.9 us: local(): lax.ppermute(out[s], PLANE, line_shift(4 - s))]
    ppermute x6 -> x20, starting transfers between devices: 4.82 us -> 20 us  [the longest x14 14.6 us: swap(): return lax.ppermute(value, 'c', SWAP)]
    unnamed x32 -> x11, local copies, waits for them, and re-layouts: 14 us -> 1.05 us
    all_to_all x2 -> x3, waiting for transfers between devices: 42 us -> 30.5 us  [the longest x1 12.2 us: local(): lax.all_to_all(parts, ('z', 'y'), split_axis=0, concat_axis=0, tiled=True)]
    pallas_call x1 -> x3, Pallas kernels: 2.92 us -> 11.5 us  [the longest x1 6.52 us: fetch(): pl.pallas_call(fetch_kernel, in_specs=[pl.BlockSpec(memory_space=pl.ANY)]...]
    reshape x4, local copies, waits for them, and re-layouts: 8.1 us -> 2.36 us  [the longest x1 1.02 us: local(): (mine.astype(F32) + other.astype(F32)).astype(BF).reshape(16, 4, HALF)]
    all_to_all x1, waiting for transfers between devices: 11.4 us -> 7.39 us  [local(): lax.all_to_all(q, PLANE, split_axis=0, concat_axis=0, tiled=True)]
  transfers between devices with their start and end apart: 9 -> 24, of which waited for: 4 -> 12; matrix products, arithmetic and copies ran while one was open for 2% -> 4% of each run, Pallas kernels for 3% -> 10%
where the time goes in v2:
time: 160 us
  waiting for transfers between devices  57.3 us (36%)
  starting transfers between devices  39.8 us (25%)
  Pallas kernels  33.9 us (21%)
  blocking collectives  15.6 us (10%)
  local copies, waits for them, and re-layouts  6.3 us (4%)
  other arithmetic  6.28 us (4%)
    all_to_all x1, blocking collectives, local(): lax.all_to_all(sent, ALL, split_axis=0, concat_axis=0, tiled=True, axis_i...  15.6 us
    ppermute x14, starting transfers between devices, swap(): return lax.ppermute(value, 'c', SWAP)  14.6 us
    ppermute x3, waiting for transfers between devices, local(): lax.ppermute(out[s], PLANE, line_shift(4 - s))  13.9 us
    all_to_all x1, waiting for transfers between devices, local(): lax.all_to_all(parts, ('z', 'y'), split_axis=0, concat_axis=0, tiled=True)  12.2 us
    all_to_all x1, waiting for transfers between devices, local(): lax.all_to_all(summed, ('z', 'y'), split_axis=0, concat_axis=0, tiled=True)  11.2 us
    pallas_call x1, Pallas kernels, attend(): pl.pallas_call(attend_kernel, grid=(KV,), in_specs=[pl.BlockSpec((64, 4 *...  9.63 us
    all_to_all x1, starting transfers between devices, local(): lax.all_to_all(q, PLANE, split_axis=0, concat_axis=0, tiled=True)  8.69 us
    all_to_all x1, waiting for transfers between devices, local(): lax.all_to_all(q, PLANE, split_axis=0, concat_axis=0, tiled=True)  7.39 us
  transfers between devices with their start and end apart: 24, of which 12 were waited for; matrix products, arithmetic and copies ran while one was open for 4% of the time, Pallas kernels for 10%

profile of v2, /device:TPU:1, one launch (start us, length us, event | category | flops | bytes accessed | tf_op | source)
XLA Modules:
  0.0 159.6 jit_solution(2221744883868928435)
XLA Ops:
  0.0 1.4 collective-permute-start.1
  1.4 0.5 collective-permute-start.3
  1.9 0.8 reshape.117
  2.8 1.3 broadcast_in_dim.34
  4.1 8.7 %all-to-all-start = ((bf16[32,2,4096]{2,1,0:T(2,128)(2,1)}), bf16[32,2,4096]{2,1,0:T(2,128)(2,1)S(1)}, u32[]{:S(2)}, u32[]{:S(2)}) async-start(bf16[32,2,4096]{2,1,0:T(2,128)(2,1)} %bitcast.4), calls=%async_computation | async-start | bytes 1048576 | tf_op jit(solution)/shard_map/all_to_all | solution.py:398
  12.8 0.7 subtract_bitcast_fusion.1
  13.4 0.1 copy.21
  13.5 1.5 pad_maximum_fusion
  15.1 0.2 reshape.120.ska_ref.sva_ref
  15.3 1.4 pad_maximum_fusion.1
  16.7 0.2 reshape.121.skb_ref.svb_ref
  16.9 7.4 %all-to-all-done = bf16[32,2,4096]{2,1,0:T(2,128)(2,1)S(1)} async-done(((bf16[32,2,4096]{2,1,0:T(2,128)(2,1)}), bf16[32,2,4096]{2,1,0:T(2,128)(2,1)S(1)}, u32[]{:S(2)}, u32[]{:S(2)}) %all-to-all-start) | async-done | bytes 524320 | tf_op jit(solution)/shard_map/all_to_all | solution.py:398
  24.3 0.2 reshape.119.q_ref
  24.6 0.9 copy-done
  25.5 9.6 %shard_map.136 = bf16[16,80,256]{2,1,0:T(8,128)(2,1)} custom-call(bf16[64,4096]{1,0:T(8,128)(2,1)S(1)} %reshape.119.q_ref, bf16[512,1024]{1,0:T(8,128)(2,1)} %ka_ref.1, bf16[512,1024]{1,0:T(8,128)(2,1)} %copy-done, bf16[512,1024]{1,0:T(8,128)(2,1)} %va_ref.1, bf16[512,1024]{1,0:T(8,128)(2,1)} %collective-permute-done.2.vb_ref, ...), custom_call_target="tpu_custom_call" | custom-call | flops 1400000000 | bytes 6291456 | tf_op jit(solution)/shard_map/pallas_call | solution.py:133
  35.1 3.6 %all-to-all-start.1 = ((bf16[16,80,256]{2,1,0:T(8,128)(2,1)}), bf16[16,80,256]{2,1,0:T(8,128)(2,1)S(1)}, u32[]{:S(2)}, u32[]{:S(2)}) async-start(bf16[16,80,256]{2,1,0:T(8,128)(2,1)} %shard_map.136), calls=%async_computation.1 | async-start | bytes 1310720 | tf_op jit(solution)/shard_map/all_to_all | solution.py:415
  38.8 12.2 %all-to-all-done.1.got_ref = bf16[16,80,256]{2,1,0:T(8,128)(2,1)S(1)} async-done(((bf16[16,80,256]{2,1,0:T(8,128)(2,1)}), bf16[16,80,256]{2,1,0:T(8,128)(2,1)S(1)}, u32[]{:S(2)}, u32[]{:S(2)}) %all-to-all-start.1) | async-done | bytes 655392 | tf_op jit(solution)/shard_map/all_to_all | solution.py:415
  51.0 2.5 %shard_map.137 = (bf16[64,4096]{1,0:T(8,128)(2,1)S(1)}, bf16[64,256]{1,0:T(8,128)(2,1)S(1)}) custom-call(s32[3]{0:T(128)S(1)} %pad_add_fusion.1.at_ref, bf16[16,80,256]{2,1,0:T(8,128)(2,1)S(1)} %all-to-all-done.1.got_ref, bf16[256,8192]{1,0:T(8,128)(2,1)} %w_ref.3), custom_call_target="tpu_custom_call" | custom-call | flops 140000000 | bytes 3145728 | tf_op jit(solution)/shard_map/pallas_call | solution.py:202
  53.5 1.7 %collective-permute-start.5 = (bf16[64,4096]{1,0:T(8,128)(2,1)S(1)}, bf16[64,4096]{1,0:T(8,128)(2,1)S(1)}, u32[]{:S(2)}, u32[]{:S(2)}) collective-permute-start(bf16[64,4096]{1,0:T(8,128)(2,1)S(1)} %get-tuple-element.15), channel_id=1, source_target_pairs={{0,1},{1,0},{2,3},{3,2},{4,5},{5,4},{6,7},{7,6},{8,9},{9,8},{10,11... | collective-permute-start | bytes 1572872 | tf_op jit(solution)/shard_map/ppermute | solution.py:362
  55.1 2.5 %shard_map.138 = bf16[64,4096]{1,0:T(8,128)(2,1)S(1)} custom-call(s32[3]{0:T(128)S(1)} %pad_add_fusion.1.at_ref, bf16[64,256]{1,0:T(8,128)(2,1)S(1)} %get-tuple-element.14.att_ref, bf16[256,8192]{1,0:T(8,128)(2,1)} %w_ref.3), custom_call_target="tpu_custom_call" | custom-call | flops 140000000 | bytes 3145728 | tf_op jit(solution)/shard_map/pallas_call | solution.py:225
  57.6 0.1 add_convert_fusion.4
  57.7 1.0 reshape.122
  58.8 3.6 %all-to-all-start.2 = ((bf16[16,4,4096]{2,1,0:T(4,128)(2,1)}), bf16[16,4,4096]{2,1,0:T(4,128)(2,1)S(1)}, u32[]{:S(2)}, u32[]{:S(2)}) async-start(bf16[16,4,4096]{2,1,0:T(4,128)(2,1)} %reshape.122), calls=%async_computation.2 | async-start | bytes 1048576 | tf_op jit(solution)/shard_map/all_to_all | solution.py:420
  62.4 0.1 collective-permute-start
  62.5 11.2 %all-to-all-done.2 = bf16[16,4,4096]{2,1,0:T(4,128)(2,1)S(1)} async-done(((bf16[16,4,4096]{2,1,0:T(4,128)(2,1)}), bf16[16,4,4096]{2,1,0:T(4,128)(2,1)S(1)}, u32[]{:S(2)}, u32[]{:S(2)}) %all-to-all-start.2) | async-done | bytes 524320 | tf_op jit(solution)/shard_map/all_to_all | solution.py:420
  73.7 0.2 convert_reduce_fusion
  73.9 0.2 multiply_reduce_fusion.1
  74.1 1.2 collective-permute-start.6
  75.3 0.8 collective-permute-done.6
  76.1 0.1 multiply_convert_fusion
  76.2 0.2 broadcast_in_dim.36
  76.4 15.6 %all_to_all.25 = bf16[16,4,4096]{2,1,0:T(4,128)(2,1)S(1)} all-to-all(bf16[16,4,4096]{2,1,0:T(4,128)(2,1)S(1)} %broadcast_in_dim.36), channel_id=1, replica_groups={{0,32,64,96,8,40,72,104,16,48,80,112,24,56,88,120},{2,34,66,98,10,42,74..., dimensions={0} | all-to-all | bytes 1048576 | tf_op jit(solution)/shard_map/all_to_all | solution.py:427
  92.0 0.1 reshape.123.refs_0_.p0
  92.2 0.7 collective-permute-start.10
  92.9 2.3 %collective-permute-start.12 = (bf16[64,4096]{1,0:T(8,128)(2,1)S(1)}, bf16[64,4096]{1,0:T(8,128)(2,1)S(1)}, u32[]{:S(2)}, u32[]{:S(2)}) collective-permute-start(bf16[64,4096]{1,0:T(8,128)(2,1)S(1)} %reshape.123.refs_0_.p0), channel_id=1, source_target_pairs={{0,6},{1,25},{2,0},{3,27},{4,2},{5,29},{6,4},{7,31},{8,14},{9,1},{... | collective-permute-start | bytes 1572872 | tf_op jit(solution)/shard_map/ppermute | solution.py:430
  95.2 1.6 %collective-permute-start.7 = (bf16[64,4096]{1,0:T(8,128)(2,1)S(1)}, bf16[64,4096]{1,0:T(8,128)(2,1)S(1)}, u32[]{:S(2)}, u32[]{:S(2)}) collective-permute-start(bf16[64,4096]{1,0:T(8,128)(2,1)S(1)} %reshape.123.refs_0_.p0), channel_id=1, source_target_pairs={{0,1},{1,0},{2,3},{3,2},{4,5},{5,4},{6,7},{7,6},{8,9},{9,8},{10,11... | collective-permute-start | bytes 1572872 | tf_op jit(solution)/shard_map/ppermute | solution.py:362
  96.8 6.5 %shard_map.139 = (bf16[8192,384]{1,0:T(8,128)(2,1)S(1)}, bf16[8192,384]{1,0:T(8,128)(2,1)S(1)}, bf16[384,8192]{1,0:T(8,128)(2,1)S(1)}) custom-call(bf16[64,4096]{1,0:T(8,128)(2,1)S(1)} %reshape.123.refs_0_.p0, bf16[8192,384]{1,0:T(8,128)(2,1)} %bitcast.36, bf16[8192,384]{1,0:T(8,128)(2,1)} %bitcast.37, bf16[384,8192]{1,0:T(8,128)(2,1)} %bitcast.38), custom_call_target="tpu_custom_call" | custom-call | bytes 23068672 | tf_op jit(solution)/shard_map/pallas_call | solution.py:69
  103.3 0.1 collective-permute-start.11
  103.4 2.1 %collective-permute-done.12.p3 = bf16[64,4096]{1,0:T(8,128)(2,1)S(1)} collective-permute-done((bf16[64,4096]{1,0:T(8,128)(2,1)S(1)}, bf16[64,4096]{1,0:T(8,128)(2,1)S(1)}, u32[]{:S(2)}, u32[]{:S(2)}) %collective-permute-start.12) | collective-permute-done | bytes 524320 | tf_op jit(solution)/shard_map/ppermute | solution.py:430
  105.5 2.7 %collective-permute-start.13 = (bf16[64,4096]{1,0:T(8,128)(2,1)S(1)}, bf16[64,4096]{1,0:T(8,128)(2,1)S(1)}, u32[]{:S(2)}, u32[]{:S(2)}) collective-permute-start(bf16[64,4096]{1,0:T(8,128)(2,1)S(1)} %collective-permute-done.12.p3), channel_id=1, source_target_pairs={{0,1},{1,0},{2,3},{3,2},{4,5},{5,4},{6,7},{7,6},{8,9},{9,8},{10,11... | collective-permute-start | bytes 1572872 | tf_op jit(solution)/shard_map/ppermute | solution.py:362
  108.2 3.7 %shard_map.140 = (f32[256,384]{1,0:T(8,128)S(1)}, f32[256,384]{1,0:T(8,128)S(1)}) custom-call(s32[3]{0:T(128)S(1)} %pad_add_fusion.1.at_ref, bf16[64,4096]{1,0:T(8,128)(2,1)S(1)} %reshape.123.refs_0_.p0, bf16[64,4096]{1,0:T(8,128)(2,1)S(1)} %collective-permute-done.8.p1, bf16[64,4096]{1,0:T(8,128)(2,1)S(1)} %collective-permute-done.10.p2, ...), custom_call_target="tpu_custom_call" | custom-call | flops 16000000000 | bytes 9437184 | tf_op jit(solution)/shard_map/pallas_call | solution.py:261
  111.9 6.4 %shard_map.141 = (bf16[256,384]{1,0:T(8,128)(2,1)S(1)}, bf16[4,64,4096]{2,1,0:T(8,128)(2,1)S(1)}) custom-call(s32[3]{0:T(128)S(1)} %pad_add_fusion.1.at_ref, bf16[64,4096]{1,0:T(8,128)(2,1)S(1)} %collective-permute-done.7.p0, bf16[64,4096]{1,0:T(8,128)(2,1)S(1)} %collective-permute-done.9.p1, bf16[64,4096]{1,0:T(8,128)(2,1)S(1)} %collective-permute-done.11.p2, ...), custom_call_target="tpu_custom_call" | custom-call | flops 2400000000 | bytes 15728640 | tf_op jit(solution)/shard_map/pallas_call | solution.py:313
  118.3 0.6 collective-permute-start.14
  118.8 2.7 %shard_map.142 = bf16[4,64,4096]{2,1,0:T(8,128)(2,1)S(1)} custom-call(s32[3]{0:T(128)S(1)} %pad_add_fusion.1.at_ref, bf16[256,384]{1,0:T(8,128)(2,1)S(1)} %get-tuple-element.21.inner_ref, bf16[384,8192]{1,0:T(8,128)(2,1)S(1)} %get-tuple-element.20.wd_ref), custom_call_target="tpu_custom_call" | custom-call | flops 800000000 | bytes 6291456 | tf_op jit(solution)/shard_map/pallas_call | solution.py:344
  121.6 1.0 collective-permute-done.14
  122.6 0.5 fusion.4
  123.2 0.7 collective-permute-start.15
  123.9 1.4 collective-permute-start.16
  125.3 0.2 collective-permute-start.17
  125.5 6.1 %collective-permute-done.15 = bf16[64,4096]{1,0:T(8,128)(2,1)S(1)} collective-permute-done((bf16[64,4096]{1,0:T(8,128)(2,1)S(1)}, bf16[64,4096]{1,0:T(8,128)(2,1)S(1)}, u32[]{:S(2)}, u32[]{:S(2)}) %collective-permute-start.15) | collective-permute-done | bytes 524320 | tf_op jit(solution)/shard_map/ppermute | solution.py:438
  131.5 2.2 %collective-permute-done.16 = bf16[64,4096]{1,0:T(8,128)(2,1)S(1)} collective-permute-done((bf16[64,4096]{1,0:T(8,128)(2,1)S(1)}, bf16[64,4096]{1,0:T(8,128)(2,1)S(1)}, u32[]{:S(2)}, u32[]{:S(2)}) %collective-permute-start.16) | collective-permute-done | bytes 524320 | tf_op jit(solution)/shard_map/ppermute | solution.py:438
  133.8 5.6 %collective-permute-done.17 = bf16[64,4096]{1,0:T(8,128)(2,1)S(1)} collective-permute-done((bf16[64,4096]{1,0:T(8,128)(2,1)S(1)}, bf16[64,4096]{1,0:T(8,128)(2,1)S(1)}, u32[]{:S(2)}, u32[]{:S(2)}) %collective-permute-start.17) | collective-permute-done | bytes 524320 | tf_op jit(solution)/shard_map/ppermute | solution.py:438
  139.3 0.3 fusion.2
  139.7 1.0 reshape.124
  140.7 4.0 %all-to-all-start.4 = ((bf16[16,4,4096]{2,1,0:T(4,128)(2,1)}), bf16[16,4,4096]{2,1,0:T(4,128)(2,1)S(1)}, u32[]{:S(2)}, u32[]{:S(2)}) async-start(bf16[16,4,4096]{2,1,0:T(4,128)(2,1)} %reshape.124), calls=%async_computation.4 | async-start | bytes 1048576 | tf_op jit(solution)/shard_map/all_to_all | solution.py:440
  144.7 0.1 fusion.7
  144.8 2.9 %collective-permute-start.18 = (f32[2,4]{1,0:T(2,128)S(1)}, f32[2,4]{1,0:T(2,128)S(1)}, u32[]{:S(2)}, u32[]{:S(2)}) collective-permute-start(f32[2,4]{1,0:T(2,128)S(1)} %fusion.7), channel_id=1, source_target_pairs={{0,1},{1,0},{2,3},{3,2},{4,5},{5,4},{6,7},{7,6},{8,9},{9,8},{10,11... | collective-permute-start | bytes 104 | tf_op jit(solution)/shard_map/ppermute | solution.py:362
  147.7 0.8 collective-permute-done.18
  148.5 0.1 copy.24
  148.6 7.2 %all-to-all-done.4 = bf16[16,4,4096]{2,1,0:T(4,128)(2,1)S(1)} async-done(((bf16[16,4,4096]{2,1,0:T(4,128)(2,1)}), bf16[16,4,4096]{2,1,0:T(4,128)(2,1)S(1)}, u32[]{:S(2)}, u32[]{:S(2)}) %all-to-all-start.4) | async-done | bytes 524320 | tf_op jit(solution)/shard_map/all_to_all | solution.py:440
  155.8 0.3 multiply_reduce_fusion
  156.2 1.9 %collective-permute-start.19 = (bf16[2,4096]{1,0:T(2,128)(2,1)S(1)}, bf16[2,4096]{1,0:T(2,128)(2,1)S(1)}, u32[]{:S(2)}, u32[]{:S(2)}) collective-permute-start(bf16[2,4096]{1,0:T(2,128)(2,1)S(1)} %get-tuple-element.29), channel_id=1, source_target_pairs={{0,1},{1,0},{2,3},{3,2},{4,5},{5,4},{6,7},{7,6},{8,9},{9,8},{10,11... | collective-permute-start | bytes 49160 | tf_op jit(solution)/shard_map/ppermute | solution.py:362
  158.1 0.8 collective-permute-done.19
  158.9 0.7 broadcast_select_fusion
  (37 shorter events, 0.3 us)
Async XLA Ops:
  0.0 24.5 %collective-permute-start.1 = (bf16[512,1024]{1,0:T(8,128)(2,1)}, bf16[512,1024]{1,0:T(8,128)(2,1)S(1)}, u32[]{:S(2)}, u32[]{:S(2)}) collective-permute-start(bf16[512,1024]{1,0:T(8,128)(2,1)} %ka_ref.1), channel_id=1, source_target_pairs={{0,1},{1,0},{2,3},{3,2},{4,5},{5,4},{6,7},{7,6},{8,9},{9,8},{10,11... | collective-permute-start | bytes 3145736 | tf_op jit(solution)/shard_map/ppermute | solution.py:362
  1.4 23.1 %collective-permute-start.2 = (bf16[512,1024]{1,0:T(8,128)(2,1)}, bf16[512,1024]{1,0:T(8,128)(2,1)}, u32[]{:S(2)}, u32[]{:S(2)}) collective-permute-start(bf16[512,1024]{1,0:T(8,128)(2,1)} %va_ref.1), channel_id=1, source_target_pairs={{0,1},{1,0},{2,3},{3,2},{4,5},{5,4},{6,7},{7,6},{8,9},{9,8},{10,11... | collective-permute-start | bytes 3145736 | tf_op jit(solution)/shard_map/ppermute | solution.py:362
  1.4 13.8 %collective-permute-start.3 = (bf16[64,2,1024]{2,1,0:T(2,128)(2,1)}, bf16[64,2,1024]{2,1,0:T(2,128)(2,1)S(1)}, u32[]{:S(2)}, u32[]{:S(2)}) collective-permute-start(bf16[64,2,1024]{2,1,0:T(2,128)(2,1)} %param.17), channel_id=1, source_target_pairs={{0,1},{1,0},{2,3},{3,2},{4,5},{5,4},{6,7},{7,6},{8,9},{9,8},{10,11... | collective-permute-start | bytes 786440 | tf_op jit(solution)/shard_map/ppermute | solution.py:362
  1.9 13.3 %collective-permute-start.4 = (bf16[64,2,1024]{2,1,0:T(2,128)(2,1)}, bf16[64,2,1024]{2,1,0:T(2,128)(2,1)}, u32[]{:S(2)}, u32[]{:S(2)}) collective-permute-start(bf16[64,2,1024]{2,1,0:T(2,128)(2,1)} %param.18), channel_id=1, source_target_pairs={{0,1},{1,0},{2,3},{3,2},{4,5},{5,4},{6,7},{7,6},{8,9},{9,8},{10,11... | collective-permute-start | bytes 786440 | tf_op jit(solution)/shard_map/ppermute | solution.py:362
  4.1 20.2 %all-to-all-start = ((bf16[32,2,4096]{2,1,0:T(2,128)(2,1)}), bf16[32,2,4096]{2,1,0:T(2,128)(2,1)S(1)}, u32[]{:S(2)}, u32[]{:S(2)}) async-start(bf16[32,2,4096]{2,1,0:T(2,128)(2,1)} %bitcast.4), calls=%async_computation | async-start | bytes 1048576 | tf_op jit(solution)/shard_map/all_to_all | solution.py:398
  24.5 1.0 copy-start
  35.1 15.9 %all-to-all-start.1 = ((bf16[16,80,256]{2,1,0:T(8,128)(2,1)}), bf16[16,80,256]{2,1,0:T(8,128)(2,1)S(1)}, u32[]{:S(2)}, u32[]{:S(2)}) async-start(bf16[16,80,256]{2,1,0:T(8,128)(2,1)} %shard_map.136), calls=%async_computation.1 | async-start | bytes 1310720 | tf_op jit(solution)/shard_map/all_to_all | solution.py:415
  53.5 4.1 %collective-permute-start.5 = (bf16[64,4096]{1,0:T(8,128)(2,1)S(1)}, bf16[64,4096]{1,0:T(8,128)(2,1)S(1)}, u32[]{:S(2)}, u32[]{:S(2)}) collective-permute-start(bf16[64,4096]{1,0:T(8,128)(2,1)S(1)} %get-tuple-element.15), channel_id=1, source_target_pairs={{0,1},{1,0},{2,3},{3,2},{4,5},{5,4},{6,7},{7,6},{8,9},{9,8},{10,11... | collective-permute-start | bytes 1572872 | tf_op jit(solution)/shard_map/ppermute | solution.py:362
  55.1 7.2 %copy-start.1 = (bf16[2,8192]{1,0:T(2,128)(2,1)S(1)}, bf16[2,8192]{1,0:T(2,128)(2,1)}, u32[]{:S(2)}) copy-start(bf16[2,8192]{1,0:T(2,128)(2,1)} %param.20) | copy-start | bytes 98308
  55.1 7.4 %copy-start.2 = (bf16[8192]{0:T(1024)(128)(2,1)S(1)}, bf16[8192]{0:T(1024)(128)(2,1)}, u32[]{:S(2)}) copy-start(bf16[8192]{0:T(1024)(128)(2,1)} %param.22) | copy-start | bytes 49156
  58.8 14.9 %all-to-all-start.2 = ((bf16[16,4,4096]{2,1,0:T(4,128)(2,1)}), bf16[16,4,4096]{2,1,0:T(4,128)(2,1)S(1)}, u32[]{:S(2)}, u32[]{:S(2)}) async-start(bf16[16,4,4096]{2,1,0:T(4,128)(2,1)} %reshape.122), calls=%async_computation.2 | async-start | bytes 1048576 | tf_op jit(solution)/shard_map/all_to_all | solution.py:420
  62.4 11.5 %collective-permute-start = (bf16[2,4096]{1,0:T(2,128)(2,1)S(1)}, bf16[2,4096]{1,0:T(2,128)(2,1)S(1)}, u32[]{:S(2)}, u32[]{:S(2)}) collective-permute-start(bf16[2,4096]{1,0:T(2,128)(2,1)S(1)} %get-tuple-element.30), channel_id=1, source_target_pairs={{0,1},{1,0},{2,3},{3,2},{4,5},{5,4},{6,7},{7,6},{8,9},{9,8},{10,11... | collective-permute-start | bytes 49160 | tf_op jit(solution)/shard_map/ppermute | solution.py:362
  74.1 2.0 %collective-permute-start.6 = (f32[4,1]{0,1:T(1,128)S(1)}, f32[4,1]{0,1:T(1,128)S(1)}, u32[]{:S(2)}, u32[]{:S(2)}) collective-permute-start(f32[4,1]{0,1:T(1,128)S(1)} %bitcast.41), channel_id=1, source_target_pairs={{0,1},{1,0},{2,3},{3,2},{4,5},{5,4},{6,7},{7,6},{8,9},{9,8},{10,11... | collective-permute-start | bytes 56 | tf_op jit(solution)/shard_map/ppermute | solution.py:362
  92.2 11.2 %collective-permute-start.10 = (bf16[64,4096]{1,0:T(8,128)(2,1)S(1)}, bf16[64,4096]{1,0:T(8,128)(2,1)S(1)}, u32[]{:S(2)}, u32[]{:S(2)}) collective-permute-start(bf16[64,4096]{1,0:T(8,128)(2,1)S(1)} %reshape.123.refs_0_.p0), channel_id=1, source_target_pairs={{0,4},{1,17},{2,6},{3,19},{4,0},{5,21},{6,2},{7,23},{8,12},{9,25},... | collective-permute-start | bytes 1572872 | tf_op jit(solution)/shard_map/ppermute | solution.py:430
  92.9 12.6 %collective-permute-start.12 = (bf16[64,4096]{1,0:T(8,128)(2,1)S(1)}, bf16[64,4096]{1,0:T(8,128)(2,1)S(1)}, u32[]{:S(2)}, u32[]{:S(2)}) collective-permute-start(bf16[64,4096]{1,0:T(8,128)(2,1)S(1)} %reshape.123.refs_0_.p0), channel_id=1, source_target_pairs={{0,6},{1,25},{2,0},{3,27},{4,2},{5,29},{6,4},{7,31},{8,14},{9,1},{... | collective-permute-start | bytes 1572872 | tf_op jit(solution)/shard_map/ppermute | solution.py:430
  95.2 13.0 %collective-permute-start.8 = (bf16[64,4096]{1,0:T(8,128)(2,1)S(1)}, bf16[64,4096]{1,0:T(8,128)(2,1)S(1)}, u32[]{:S(2)}, u32[]{:S(2)}) collective-permute-start(bf16[64,4096]{1,0:T(8,128)(2,1)S(1)} %reshape.123.refs_0_.p0), channel_id=1, source_target_pairs={{0,2},{1,9},{2,4},{3,11},{4,6},{5,13},{6,0},{7,15},{8,10},{9,17},{... | collective-permute-start | bytes 1572872 | tf_op jit(solution)/shard_map/ppermute | solution.py:430
  95.2 16.7 %collective-permute-start.7 = (bf16[64,4096]{1,0:T(8,128)(2,1)S(1)}, bf16[64,4096]{1,0:T(8,128)(2,1)S(1)}, u32[]{:S(2)}, u32[]{:S(2)}) collective-permute-start(bf16[64,4096]{1,0:T(8,128)(2,1)S(1)} %reshape.123.refs_0_.p0), channel_id=1, source_target_pairs={{0,1},{1,0},{2,3},{3,2},{4,5},{5,4},{6,7},{7,6},{8,9},{9,8},{10,11... | collective-permute-start | bytes 1572872 | tf_op jit(solution)/shard_map/ppermute | solution.py:362
  103.3 8.5 %collective-permute-start.11 = (bf16[64,4096]{1,0:T(8,128)(2,1)S(1)}, bf16[64,4096]{1,0:T(8,128)(2,1)S(1)}, u32[]{:S(2)}, u32[]{:S(2)}) collective-permute-start(bf16[64,4096]{1,0:T(8,128)(2,1)S(1)} %collective-permute-done.10.p2), channel_id=1, source_target_pairs={{0,1},{1,0},{2,3},{3,2},{4,5},{5,4},{6,7},{7,6},{8,9},{9,8},{10,11... | collective-permute-start | bytes 1572872 | tf_op jit(solution)/shard_map/ppermute | solution.py:362
  105.5 6.4 %collective-permute-start.13 = (bf16[64,4096]{1,0:T(8,128)(2,1)S(1)}, bf16[64,4096]{1,0:T(8,128)(2,1)S(1)}, u32[]{:S(2)}, u32[]{:S(2)}) collective-permute-start(bf16[64,4096]{1,0:T(8,128)(2,1)S(1)} %collective-permute-done.12.p3), channel_id=1, source_target_pairs={{0,1},{1,0},{2,3},{3,2},{4,5},{5,4},{6,7},{7,6},{8,9},{9,8},{10,11... | collective-permute-start | bytes 1572872 | tf_op jit(solution)/shard_map/ppermute | solution.py:362
  108.1 3.7 %collective-permute-start.9 = (bf16[64,4096]{1,0:T(8,128)(2,1)S(1)}, bf16[64,4096]{1,0:T(8,128)(2,1)S(1)}, u32[]{:S(2)}, u32[]{:S(2)}) collective-permute-start(bf16[64,4096]{1,0:T(8,128)(2,1)S(1)} %collective-permute-done.8.p1), channel_id=1, source_target_pairs={{0,1},{1,0},{2,3},{3,2},{4,5},{5,4},{6,7},{7,6},{8,9},{9,8},{10,11... | collective-permute-start | bytes 1572872 | tf_op jit(solution)/shard_map/ppermute | solution.py:362
  118.3 4.4 %collective-permute-start.14 = (bf16[4,64,4096]{2,1,0:T(8,128)(2,1)S(1)}, bf16[4,64,4096]{2,1,0:T(8,128)(2,1)S(1)}, u32[]{:S(2)}, u32[]{:S(2)}) collective-permute-start(bf16[4,64,4096]{2,1,0:T(8,128)(2,1)S(1)} %get-tuple-element.22), channel_id=1, source_target_pairs={{0,1},{1,0},{2,3},{3,2},{4,5},{5,4},{6,7},{7,6},{8,9},{9,8},{10,11... | collective-permute-start | bytes 6291464 | tf_op jit(solution)/shard_map/ppermute | solution.py:362
  121.6 23.1 %copy-start.3 = (f32[2,2]{1,0:T(2,128)S(1)}, f32[2,2]{1,0:T(2,128)}, u32[]{:S(2)}) copy-start(f32[2,2]{1,0:T(2,128)} %param.24) | copy-start | bytes 52
  121.6 23.1 %copy-start.4 = (s32[2,2]{1,0:T(2,128)S(1)}, s32[2,2]{1,0:T(2,128)}, u32[]{:S(2)}) copy-start(s32[2,2]{1,0:T(2,128)} %param.23) | copy-start | bytes 52
  123.2 8.4 %collective-permute-start.15 = (bf16[64,4096]{1,0:T(8,128)(2,1)S(1)}, bf16[64,4096]{1,0:T(8,128)(2,1)S(1)}, u32[]{:S(2)}, u32[]{:S(2)}) collective-permute-start(bf16[64,4096]{1,0:T(8,128)(2,1)S(1)} %get-tuple-element.25), channel_id=1, source_target_pairs={{0,6},{1,25},{2,0},{3,27},{4,2},{5,29},{6,4},{7,31},{8,14},{9,1},{... | collective-permute-start | bytes 1572872 | tf_op jit(solution)/shard_map/ppermute | solution.py:438
  123.9 9.9 %collective-permute-start.16 = (bf16[64,4096]{1,0:T(8,128)(2,1)S(1)}, bf16[64,4096]{1,0:T(8,128)(2,1)S(1)}, u32[]{:S(2)}, u32[]{:S(2)}) collective-permute-start(bf16[64,4096]{1,0:T(8,128)(2,1)S(1)} %get-tuple-element.27), channel_id=1, source_target_pairs={{0,4},{1,17},{2,6},{3,19},{4,0},{5,21},{6,2},{7,23},{8,12},{9,25},... | collective-permute-start | bytes 1572872 | tf_op jit(solution)/shard_map/ppermute | solution.py:438
  125.3 14.0 %collective-permute-start.17 = (bf16[64,4096]{1,0:T(8,128)(2,1)S(1)}, bf16[64,4096]{1,0:T(8,128)(2,1)S(1)}, u32[]{:S(2)}, u32[]{:S(2)}) collective-permute-start(bf16[64,4096]{1,0:T(8,128)(2,1)S(1)} %get-tuple-element.26), channel_id=1, source_target_pairs={{0,2},{1,9},{2,4},{3,11},{4,6},{5,13},{6,0},{7,15},{8,10},{9,17},{... | collective-permute-start | bytes 1572872 | tf_op jit(solution)/shard_map/ppermute | solution.py:438
  140.7 15.0 %all-to-all-start.4 = ((bf16[16,4,4096]{2,1,0:T(4,128)(2,1)}), bf16[16,4,4096]{2,1,0:T(4,128)(2,1)S(1)}, u32[]{:S(2)}, u32[]{:S(2)}) async-start(bf16[16,4,4096]{2,1,0:T(4,128)(2,1)} %reshape.124), calls=%async_computation.4 | async-start | bytes 1048576 | tf_op jit(solution)/shard_map/all_to_all | solution.py:440
  144.8 3.7 %collective-permute-start.18 = (f32[2,4]{1,0:T(2,128)S(1)}, f32[2,4]{1,0:T(2,128)S(1)}, u32[]{:S(2)}, u32[]{:S(2)}) collective-permute-start(f32[2,4]{1,0:T(2,128)S(1)} %fusion.7), channel_id=1, source_target_pairs={{0,1},{1,0},{2,3},{3,2},{4,5},{5,4},{6,7},{7,6},{8,9},{9,8},{10,11... | collective-permute-start | bytes 104 | tf_op jit(solution)/shard_map/ppermute | solution.py:362
  156.2 2.7 %collective-permute-start.19 = (bf16[2,4096]{1,0:T(2,128)(2,1)S(1)}, bf16[2,4096]{1,0:T(2,128)(2,1)S(1)}, u32[]{:S(2)}, u32[]{:S(2)}) collective-permute-start(bf16[2,4096]{1,0:T(2,128)(2,1)S(1)} %get-tuple-element.29), channel_id=1, source_target_pairs={{0,1},{1,0},{2,3},{3,2},{4,5},{5,4},{6,7},{7,6},{8,9},{9,8},{10,11... | collective-permute-start | bytes 49160 | tf_op jit(solution)/shard_map/ppermute | solution.py:362

commit v3 on v2

v3 whole, which is shorter than its diff:
```python
import functools

import jax
import jax.numpy as jnp
from jax import lax
from jax.experimental import pallas as pl
from jax.experimental.pallas import tpu as pltpu
from jax.sharding import Mesh, PartitionSpec as P

HEADS = 64
KV = 8
HD = 128
D = 8192
HALF = D // 2
EPS = 1e-05
NEG = -1e30
LOG2E = 1.4426950408889634
SCALE = LOG2E / HD**0.5
BF = jnp.bfloat16
F32 = jnp.float32
ALL = ("x", "z", "y", "c")
PLANE = ("z", "y", "c")
SWAP = [(0, 1), (1, 0)]
MB = 1 << 20
WHOLE = pl.BlockSpec(memory_space=pltpu.VMEM)
SCALARS = pl.BlockSpec(memory_space=pltpu.SMEM)


def device(x, z, y, c):
    return ((x * 4 + z) * 4 + y) * 2 + c


def wide_groups():
    four = range(4)
    zeros = [[device(x, z, y, 0) for z in four for x in four] for y in four]
    return zeros + [[device(x, z, y, 1) for y in four for x in four] for z in four]


def line_shift(step):
    pairs = []
    for z in range(4):
        for y in range(4):
            pairs.append(((z * 4 + y) * 2, (z * 4 + (y + step) % 4) * 2))
            pairs.append(((z * 4 + y) * 2 + 1, (((z + step) % 4) * 4 + y) * 2 + 1))
    return pairs


def dot(a, b):
    return jnp.dot(a, b, preferred_element_type=F32)


def dot_t(a, b):
    return lax.dot_general(a, b, (((1,), (1,)), ((), ())), preferred_element_type=F32)


def fetch_kernel(at_ref, after_ref, wg_ref, wu_ref, wd_ref, wdb_ref, gate_up_ref, down_ref, sems):
    units = wg_ref.shape[1]
    pairs = []
    for part in range(4):
        rows = pl.ds(part * D // 4, D // 4)
        pairs.append((wg_ref.at[rows], gate_up_ref.at[rows, pl.ds(0, units)]))
        pairs.append((wu_ref.at[rows], gate_up_ref.at[rows, pl.ds(units, units)]))
    columns = pl.ds(pl.multiple_of(at_ref[0] * HALF, HALF), HALF)
    for part in range(2):
        rows = pl.ds(part * units // 2, units // 2)
        pairs.append((wd_ref.at[rows, columns], down_ref.at[rows]))
        rows_b = pl.ds(units + part * units // 2, units // 2)
        pairs.append((wdb_ref.at[rows, columns], down_ref.at[rows_b]))
    copies = [pltpu.make_async_copy(src, dst, sems.at[i]) for i, (src, dst) in enumerate(pairs)]
    for copy in copies:
        copy.start()
    for copy in copies:
        copy.wait()


def fetch(at, after, w_gate, w_up, w_down, w_down_b):
    units = w_gate.shape[1]
    return pl.pallas_call(
        fetch_kernel,
        in_specs=[SCALARS] + [pl.BlockSpec(memory_space=pl.ANY)] * 5,
        out_specs=[WHOLE] * 2,
        out_shape=[pltpu.VMEM((D, 2 * units), BF), pltpu.VMEM((2 * units, HALF), BF)],
        scratch_shapes=[pltpu.SemaphoreType.DMA((12,))],
        compiler_params=pltpu.CompilerParams(vmem_limit_bytes=4 * MB),
        cost_estimate=pl.CostEstimate(flops=0, bytes_accessed=22 * MB, transcendentals=0),
    )(at, after, in_hbm(w_gate), in_hbm(w_up), in_hbm(w_down), in_hbm(w_down_b))


def in_vmem(array):
    return pltpu.with_memory_space_constraint(array, pltpu.VMEM)


def in_hbm(array):
    return pltpu.with_memory_space_constraint(array, pltpu.HBM)


def spread_kernel(q_ref, out_ref):
    for half in range(2):
        value = jnp.concatenate(
            [q_ref[:, (2 * k + half) * 2 * HD : (2 * k + half + 1) * 2 * HD] for k in range(16)], axis=1
        )
        for chip in range(16):
            out_ref[2 * chip + half] = value


def spread(queries):
    return pl.pallas_call(
        spread_kernel,
        in_specs=[WHOLE],
        out_specs=WHOLE,
        out_shape=jax.ShapeDtypeStruct((32, 2, HALF), BF),
        compiler_params=pltpu.CompilerParams(vmem_limit_bytes=4 * MB),
        cost_estimate=pl.CostEstimate(flops=0, bytes_accessed=MB, transcendentals=0),
    )(queries)


def attend_kernel(q_ref, ka_ref, kb_ref, va_ref, vb_ref, sa_ref, sb_ref, left_ref, out_ref):
    rows = 64
    row = lax.broadcasted_iota(jnp.int32, (4 * rows, 4 * rows), 0)
    col = lax.broadcasted_iota(jnp.int32, (4 * rows, 4 * rows), 1)
    left = left_ref[...]
    live = (row % rows == col % (2 * rows) // 2) & (
        col % 2 < jnp.where(col < 2 * rows, left[:, 0:1], left[:, 1:2])
    )
    eye = row == col
    line = lax.broadcasted_iota(jnp.int32, (16, 4 * rows), 0)
    for h in range(KV):
        at = slice(h * HD, (h + 1) * HD)
        at_v = slice((KV + h) * HD, (KV + h + 1) * HD)
        q = jnp.concatenate(
            [q_ref[:, (4 * h + g) * HD : (4 * h + g + 1) * HD] for g in range(4)], axis=0
        )
        suffix_k = jnp.concatenate([sa_ref[:, at], sb_ref[:, at]], axis=0)
        suffix_v = jnp.concatenate([sa_ref[:, at_v], sb_ref[:, at_v]], axis=0)
        scores = [
            dot_t(q, ka_ref[:, at]),
            dot_t(q, kb_ref[:, at]),
            jnp.where(live, dot_t(q, suffix_k), NEG),
        ]
        top = functools.reduce(jnp.maximum, [jnp.max(s, axis=1, keepdims=True) for s in scores])
        top = (top * SCALE).astype(BF).astype(F32)
        total = jnp.zeros((4 * rows, 1), F32)
        acc = jnp.zeros((4 * rows, HD), F32)
        for s, v in zip(scores, (va_ref[:, at], vb_ref[:, at], suffix_v)):
            prob = jnp.exp2(s * SCALE - top)
            total = total + jnp.sum(prob, axis=1, keepdims=True)
            acc = acc + dot(prob.astype(BF), v)
        top_row = jnp.sum(jnp.where(eye, top, 0.0), axis=0, keepdims=True)
        total_row = jnp.sum(jnp.where(eye, total, 0.0), axis=0, keepdims=True)
        total_high = total_row.astype(BF).astype(F32)
        total_low = total_row - total_high
        for k in range(2):
            for j in range(2):
                g = 2 * k + j
                out_ref[2 * h + k, 0:rows, j * HD : (j + 1) * HD] = acc[
                    g * rows : (g + 1) * rows
                ].astype(BF)
            part = slice(k * 2 * rows, (k + 1) * 2 * rows)
            high = jnp.concatenate([top_row[:, part], total_high[:, part]], axis=1)
            low = jnp.concatenate([top_row[:, part], total_low[:, part]], axis=1)
            tail = jnp.where(line == 0, high, jnp.where(line == 1, low, 0.0))
            out_ref[2 * h + k, rows : rows + 16, :] = tail.astype(BF)


def attend(q, ka, kb, va, vb, sa, sb, left):
    arrays = (q, ka, kb, va, vb, sa, sb, left)
    return pl.pallas_call(
        attend_kernel,
        grid=(1,),
        in_specs=[pl.BlockSpec(a.shape, lambda i: (0, 0)) for a in arrays],
        out_specs=pl.BlockSpec((16, 80, 2 * HD), lambda i: (0, 0, 0)),
        out_shape=jax.ShapeDtypeStruct((16, 80, 2 * HD), BF),
        compiler_params=pltpu.CompilerParams(vmem_limit_bytes=24 * MB),
        cost_estimate=pl.CostEstimate(flops=1400000000, bytes_accessed=6 * MB, transcendentals=2700000),
    )(q, in_hbm(ka), kb, in_hbm(va), vb, sa, sb, left)


def columns_of(w_ref, half, buffer, sems):
    width = HALF // 4
    return [
        pltpu.make_async_copy(
            w_ref.at[:, pl.ds(pl.multiple_of(half * HALF + part * width, width), width)],
            buffer.at[:, pl.ds(part * width, width)],
            sems.at[part],
        )
        for part in range(4)
    ]


def project_parts(copies, attended, buffer, out_ref):
    width = HALF // 4
    for part, copy in enumerate(copies):
        copy.wait()
        at = slice(part * width, (part + 1) * width)
        out_ref[:, at] = dot(attended, buffer[:, at]).astype(BF)


def project_kernel(at_ref, got_ref, w_ref, early_ref, out_ref, att_ref, buffer, sems):
    rows = 64
    copies = columns_of(w_ref, 1 - at_ref[0], buffer, sems)
    for copy in copies:
        copy.start()
    tops = [got_ref[s, rows : rows + 1, 0 : 2 * rows].astype(F32) for s in range(16)]
    sums = [
        got_ref[s, rows : rows + 1, 2 * rows :].astype(F32)
        + got_ref[s, rows + 1 : rows + 2, 2 * rows :].astype(F32)
        for s in range(16)
    ]
    top = functools.reduce(jnp.maximum, tops)
    factors = [jnp.exp2(t - top) for t in tops]
    total = functools.reduce(jnp.add, [f * s for f, s in zip(factors, sums)])
    lane = lax.broadcasted_iota(jnp.int32, (rows, 2 * rows), 1)
    line = lax.broadcasted_iota(jnp.int32, (rows, 2 * rows), 0)
    for j in range(2):
        here = lane == line + j * rows
        acc = jnp.zeros((rows, HD), F32)
        for s in range(16):
            share = jnp.sum(jnp.where(here, factors[s] / total, 0.0), axis=1, keepdims=True)
            acc = acc + got_ref[s, 0:rows, j * HD : (j + 1) * HD].astype(F32) * share
        att_ref[:, j * HD : (j + 1) * HD] = acc.astype(BF)
    project_parts(copies, att_ref[...], buffer, out_ref)


def project_other(at, got, w_out, early):
    return pl.pallas_call(
        project_kernel,
        in_specs=[
            pl.BlockSpec(memory_space=pltpu.SMEM),
            pl.BlockSpec(memory_space=pltpu.VMEM),
            pl.BlockSpec(memory_space=pl.ANY),
            pl.BlockSpec(memory_space=pl.ANY),
        ],
        out_specs=[pl.BlockSpec(memory_space=pltpu.VMEM)] * 2,
        out_shape=[jax.ShapeDtypeStruct((64, HALF), BF), jax.ShapeDtypeStruct((64, 256), BF)],
        scratch_shapes=[pltpu.VMEM((256, HALF), BF), pltpu.SemaphoreType.DMA((4,))],
        compiler_params=pltpu.CompilerParams(vmem_limit_bytes=16 * MB),
        cost_estimate=pl.CostEstimate(flops=140000000, bytes_accessed=3 * MB, transcendentals=0),
    )(at, got, in_hbm(w_out), in_hbm(early))


def project_mine_kernel(at_ref, att_ref, w_ref, out_ref, buffer, sems):
    copies = columns_of(w_ref, at_ref[0], buffer, sems)
    for copy in copies:
        copy.start()
    project_parts(copies, att_ref[...], buffer, out_ref)


def project_mine(at, attended, w_out):
    return pl.pallas_call(
        project_mine_kernel,
        in_specs=[
            pl.BlockSpec(memory_space=pltpu.SMEM),
            pl.BlockSpec(memory_space=pltpu.VMEM),
            pl.BlockSpec(memory_space=pl.ANY),
        ],
        out_specs=pl.BlockSpec(memory_space=pltpu.VMEM),
        out_shape=jax.ShapeDtypeStruct((64, HALF), BF),
        scratch_shapes=[pltpu.VMEM((256, HALF), BF), pltpu.SemaphoreType.DMA((4,))],
        compiler_params=pltpu.CompilerParams(vmem_limit_bytes=16 * MB),
        cost_estimate=pl.CostEstimate(flops=140000000, bytes_accessed=3 * MB, transcendentals=0),
    )(at, attended, in_hbm(w_out))


def rolled(place, back):
    return pl.multiple_of(((place + 4 - back) & 3) * 16, 16)


def gathered(x_ref, pieces, place, own):
    for a in range(4):
        for b in range(4):
            piece, back = (a, b) if own else (b, a)
            line = (4 * a + b) * 16
            x_ref[line : line + 16, :] = pieces[piece][pl.ds(rolled(place, back), 16), :]


def multiplied(x_ref, w_ref, half, acc_ref):
    width = HALF // 4
    for part in range(4):
        rows = pl.ds(pl.multiple_of(half * HALF + part * width, width), width)
        value = dot(x_ref[:, part * width : (part + 1) * width], w_ref[rows, :])
        if part == 0:
            acc_ref[...] = value
        else:
            acc_ref[...] += value


def first_kernel(at_ref, p0, p1, p2, p3, w_ref, acc_ref, x_ref):
    gathered(x_ref, (p0, p1, p2, p3), at_ref[1], True)
    multiplied(x_ref, w_ref, at_ref[0], acc_ref)


def expert_first(at, pieces, gate_up):
    units = gate_up.shape[1]
    return pl.pallas_call(
        first_kernel,
        in_specs=[SCALARS] + [WHOLE] * 5,
        out_specs=WHOLE,
        out_shape=jax.ShapeDtypeStruct((256, units), F32),
        scratch_shapes=[pltpu.VMEM((256, HALF), BF)],
        compiler_params=pltpu.CompilerParams(vmem_limit_bytes=12 * MB),
        cost_estimate=pl.CostEstimate(flops=16000000000, bytes_accessed=9 * MB, transcendentals=0),
    )(at, *pieces, in_vmem(gate_up))


def second_kernel(at_ref, p0, p1, p2, p3, w_ref, acc_ref, inner_ref, x_ref, more_ref):
    units = inner_ref.shape[1]
    gathered(x_ref, (p0, p1, p2, p3), at_ref[2], False)
    multiplied(x_ref, w_ref, 1 - at_ref[0], more_ref)
    gate = acc_ref[:, :units] + more_ref[:, :units]
    up = acc_ref[:, units:] + more_ref[:, units:]
    inner_ref[...] = (gate / (1.0 + jnp.exp(-gate)) * up).astype(BF)


def expert_second(at, pieces, gate_up, acc):
    units = gate_up.shape[1]
    return pl.pallas_call(
        second_kernel,
        in_specs=[SCALARS] + [WHOLE] * 6,
        out_specs=WHOLE,
        out_shape=jax.ShapeDtypeStruct((256, units // 2), BF),
        scratch_shapes=[pltpu.VMEM((256, HALF), BF), pltpu.VMEM((256, units), F32)],
        compiler_params=pltpu.CompilerParams(vmem_limit_bytes=12 * MB),
        cost_estimate=pl.CostEstimate(flops=1600000000, bytes_accessed=9 * MB, transcendentals=0),
    )(at, *pieces, in_vmem(gate_up), acc)


def third_kernel(at_ref, inner_ref, other_ref, w_ref, o0, o1, o2, o3, x_ref):
    units = inner_ref.shape[1]
    x_ref[:, :units] = inner_ref[...]
    for a in range(4):
        for b in range(4):
            line, line_b = (4 * a + b) * 16, (4 * b + a) * 16
            x_ref[line : line + 16, units:] = other_ref[line_b : line_b + 16, :]
    outs = (o0, o1, o2, o3)
    width = HALF // 4
    for part in range(4):
        cols = slice(part * width, (part + 1) * width)
        value = dot(x_ref[...], w_ref[:, cols]).astype(BF)
        for a in range(4):
            for b in range(4):
                line = (4 * a + b) * 16
                outs[a][pl.ds(rolled(at_ref[1], b), 16), cols] = value[line : line + 16]


def expert_third(at, inner, other, down):
    units = inner.shape[1]
    return pl.pallas_call(
        third_kernel,
        in_specs=[SCALARS] + [WHOLE] * 3,
        out_specs=[WHOLE] * 4,
        out_shape=[jax.ShapeDtypeStruct((64, HALF), BF)] * 4,
        scratch_shapes=[pltpu.VMEM((256, 2 * units), BF)],
        compiler_params=pltpu.CompilerParams(vmem_limit_bytes=12 * MB),
        cost_estimate=pl.CostEstimate(flops=1600000000, bytes_accessed=9 * MB, transcendentals=0),
    )(at, inner, other, in_vmem(down))


def swap(value):
    return lax.ppermute(value, "c", SWAP)


def local(
    queries,
    prefix_keys,
    prefix_values,
    suffix_keys,
    suffix_values,
    suffix_lengths,
    hidden_in,
    w_out,
    norm_gain,
    expert_ids,
    expert_weights,
    w_gate,
    w_up,
    w_down,
):
    c = lax.axis_index("c").astype(jnp.int32)
    z = lax.axis_index("z").astype(jnp.int32)
    y = lax.axis_index("y").astype(jnp.int32)
    chip = 4 * z + y
    at = jnp.stack([c, jnp.where(c == 0, z, y), jnp.where(c == 0, y, z)])

    def in_order(own, got, axis):
        return jnp.where(
            c == 0, jnp.concatenate([own, got], axis=axis), jnp.concatenate([got, own], axis=axis)
        )

    q = spread(queries)
    keys_b = swap(prefix_keys)
    values_b = swap(prefix_values)
    suffix_keys_b = swap(suffix_keys)
    suffix_values_b = swap(suffix_values)
    w_down_b = swap(w_down[0])
    q = lax.all_to_all(q, PLANE, split_axis=0, concat_axis=0, tiled=True).reshape(64, HALF)
    suffix = jnp.concatenate([suffix_keys, suffix_values], axis=-1).reshape(128, 2 * KV * HD)
    suffix_b = jnp.concatenate([suffix_keys_b, suffix_values_b], axis=-1).reshape(128, 2 * KV * HD)
    first = 4 * chip
    left = jnp.stack([suffix_lengths - (first + 2 * c), suffix_lengths - (first + 2 * (1 - c))], axis=1)
    left = jnp.tile(left.astype(jnp.int32), (4, 1))
    hidden = in_order(
        lax.dynamic_slice_in_dim(hidden_in, c * HALF, HALF, 1),
        swap(lax.dynamic_slice_in_dim(hidden_in, (1 - c) * HALF, HALF, 1)),
        0,
    ).astype(F32)
    match = expert_ids[:, :, None] == jnp.arange(4, dtype=jnp.int32)[None, None, :]
    weights = jnp.sum(jnp.where(match, expert_weights[:, :, None], 0.0), axis=1)
    weights = in_order(weights, swap(weights), 0)
    gain = lax.dynamic_slice_in_dim(norm_gain, c * HALF, HALF, 0).astype(F32)

    parts = attend(q, prefix_keys, keys_b, prefix_values, values_b, suffix, suffix_b, left)
    parts = lax.all_to_all(parts, ("z", "y"), split_axis=0, concat_axis=0, tiled=True)
    other, attended = project_other(at, parts, w_out, w_down_b)
    other = swap(other)
    mine = project_mine(at, attended, w_out)
    summed = (mine.astype(F32) + other.astype(F32)).astype(BF).reshape(16, 4, HALF)
    summed = lax.all_to_all(summed, ("z", "y"), split_axis=0, concat_axis=0, tiled=True)
    residual = hidden + jnp.sum(summed.astype(F32), axis=0)
    square = jnp.sum(residual * residual, axis=-1, keepdims=True)
    mean_square = (square + swap(square)) * (1.0 / D)
    normed = (residual * lax.rsqrt(mean_square + EPS) * gain).astype(BF)
    wide = wide_groups()
    sent = jnp.broadcast_to(normed[None], (16, 4, HALF))
    own = lax.all_to_all(
        sent, ALL, split_axis=0, concat_axis=0, tiled=True, axis_index_groups=wide
    ).reshape(64, HALF)
    pieces = [own] + [lax.ppermute(own, PLANE, line_shift(s)) for s in (1, 2, 3)]
    gate_up, down = fetch(at, own, w_gate[0], w_up[0], w_down[0], w_down_b)
    pieces_b = [swap(piece) for piece in pieces]
    acc = expert_first(at, pieces, gate_up)
    inner = expert_second(at, pieces_b, gate_up, acc)
    out = expert_third(at, inner, swap(inner), down)
    out = [out[0]] + [lax.ppermute(out[s], PLANE, line_shift(4 - s)) for s in (1, 2, 3)]
    out = functools.reduce(jnp.add, [piece.astype(F32) for piece in out]).astype(BF)
    out = lax.all_to_all(
        out.reshape(16, 4, HALF), ALL, split_axis=0, concat_axis=0, tiled=True, axis_index_groups=wide
    )
    out = out.reshape(4, 4, 4, HALF).astype(F32)
    mixed = residual + jnp.sum(out * weights.T[None, :, :, None], axis=(0, 1))
    mixed = mixed.astype(BF)
    kept = lax.dynamic_slice_in_dim(mixed, 2 * c, 2, 0)
    got = swap(lax.dynamic_slice_in_dim(mixed, 2 * (1 - c), 2, 0))
    return in_order(kept, got, 1)


def solution(mesh):
    grid = Mesh(mesh.devices.reshape(4, 4, 4, 2), ALL)
    placed = (
        P(ALL, None),
        P(PLANE, None),
        P(PLANE, None),
        P("x", PLANE, None),
        P("x", PLANE, None),
        P("x"),
        P(ALL, None),
        P(PLANE, None),
        P(),
        P(ALL, None),
        P(ALL, None),
        P("x", None, PLANE),
        P("x", None, PLANE),
        P("x", PLANE, None),
    )
    return jax.shard_map(
        local, mesh=grid, in_specs=placed, out_specs=P(ALL, None), check_vma=False
    )
```

time: 160 us -> 151 us (0.944)
  Pallas kernels: 33.9 us -> 27.6 us
  starting transfers between devices: 39.8 us -> 36.6 us
  waiting for transfers between devices: 57.3 us -> 60.4 us
  local copies, waits for them, and re-layouts: 6.3 us -> 3.99 us
    pallas_call x5 -> x6, Pallas kernels: 28.9 us -> 22.7 us  [the longest x1 7.6 us: attend(): pl.pallas_call(attend_kernel, grid=(1,), in_specs=[pl.BlockSpec(a.shape,...]
    ppermute x14 -> x15, starting transfers between devices: 14.6 us -> 11.9 us  [swap(): return lax.ppermute(value, 'c', SWAP)]
    ppermute x14 -> x15, waiting for transfers between devices: 3.52 us -> 4.01 us  [swap(): return lax.ppermute(value, 'c', SWAP)]
  transfers between devices with their start and end apart: 24 -> 25, of which waited for: 12 -> 13; matrix products, arithmetic and copies ran while one was open for 4% -> 3% of each run, Pallas kernels for 10% -> 14%
where the time goes in v3:
time: 151 us; the launch traced here: 150 us
  waiting for transfers between devices  60.4 us (40%)
  starting transfers between devices  36.6 us (24%)
  Pallas kernels  27.6 us (18%)
  blocking collectives  15.7 us (10%)
  other arithmetic  5.69 us (4%)
  local copies, waits for them, and re-layouts  3.99 us (3%)
    all_to_all x1, blocking collectives, local(): lax.all_to_all(sent, ALL, split_axis=0, concat_axis=0, tiled=True, axis_i...  15.7 us
    ppermute x3, waiting for transfers between devices, local(): lax.ppermute(out[s], PLANE, line_shift(4 - s))  14.5 us
    all_to_all x1, waiting for transfers between devices, local(): lax.all_to_all(parts, ('z', 'y'), split_axis=0, concat_axis=0, tiled=True)  12.2 us
    ppermute x15, starting transfers between devices, swap(): return lax.ppermute(value, 'c', SWAP)  11.9 us
    all_to_all x1, waiting for transfers between devices, local(): lax.all_to_all(summed, ('z', 'y'), split_axis=0, concat_axis=0, tiled=True)  11.2 us
    all_to_all x1, waiting for transfers between devices, local(): lax.all_to_all(out.reshape(16, 4, HALF), ALL, split_axis=0, concat_axis=0...  8.6 us
    all_to_all x1, starting transfers between devices, local(): lax.all_to_all(q, PLANE, split_axis=0, concat_axis=0, tiled=True)  8.3 us
    pallas_call x1, Pallas kernels, attend(): pl.pallas_call(attend_kernel, grid=(1,), in_specs=[pl.BlockSpec(a.shape,...  7.6 us
  transfers between devices with their start and end apart: 25, of which 13 were waited for; matrix products, arithmetic and copies ran while one was open for 3% of the time, Pallas kernels for 14%

profile of v3, /device:TPU:1, one launch (start us, length us, event | category | flops | bytes accessed | tf_op | source)
XLA Modules:
  0.0 150.3 jit_solution(17955546325705017154)
XLA Ops:
  0.0 1.4 collective-permute-start.5
  1.4 0.5 collective-permute-start.2
  1.9 0.5 collective-permute-start.4
  2.4 0.8 copy-done
  3.2 0.9 shard_map.136
  4.1 8.3 %all-to-all-start = ((bf16[32,2,4096]{2,1,0:T(2,128)(2,1)}), bf16[32,2,4096]{2,1,0:T(2,128)(2,1)S(1)}, u32[]{:S(2)}, u32[]{:S(2)}) async-start(bf16[32,2,4096]{2,1,0:T(2,128)(2,1)} %shard_map.136), calls=%async_computation | async-start | bytes 1048576 | tf_op jit(solution)/shard_map/all_to_all | solution.py:395
  12.4 0.7 subtract_bitcast_fusion.1
  13.1 0.1 copy.17
  13.2 1.5 %pad_maximum_fusion = bf16[64,2,2048]{2,1,0:T(2,128)(2,1)S(1)} fusion(bf16[64,2,1024]{2,1,0:T(2,128)(2,1)} %param.18, bf16[64,2,1024]{2,1,0:T(2,128)(2,1)} %param.17), kind=kLoop, calls=%fused_computation.4 | loop fusion | flops 1048576 | bytes 1048576 | tf_op jit(solution)/shard_map/concatenate | solution.py:396
  14.7 0.2 reshape.92.sa_ref
  14.9 0.4 collective-permute-done.4
  15.3 1.4 pad_maximum_fusion.1
  16.7 0.2 reshape.93.sb_ref
  17.0 7.0 %all-to-all-done = bf16[32,2,4096]{2,1,0:T(2,128)(2,1)S(1)} async-done(((bf16[32,2,4096]{2,1,0:T(2,128)(2,1)}), bf16[32,2,4096]{2,1,0:T(2,128)(2,1)S(1)}, u32[]{:S(2)}, u32[]{:S(2)}) %all-to-all-start) | async-done | bytes 524320 | tf_op jit(solution)/shard_map/all_to_all | solution.py:395
  23.9 0.2 reshape.91.q_ref
  24.2 7.6 %shard_map.137 = bf16[16,80,256]{2,1,0:T(8,128)(2,1)} custom-call(bf16[64,4096]{1,0:T(8,128)(2,1)S(1)} %reshape.91.q_ref, bf16[512,1024]{1,0:T(8,128)(2,1)} %ka_ref.1, bf16[512,1024]{1,0:T(8,128)(2,1)S(1)} %collective-permute-done.1.kb_ref, bf16[512,1024]{1,0:T(8,128)(2,1)} %va_ref.1, bf16[512,1024]{1,0:T(8,128)(2,1)} %collective-permute-done.2.vb_ref, ...), custom_call_target="tpu_custom_call" | custom-call | flops 1400000000 | bytes 6291456 | tf_op jit(solution)/shard_map/pallas_call | solution.py:167
  31.8 3.6 %all-to-all-start.1 = ((bf16[16,80,256]{2,1,0:T(8,128)(2,1)}), bf16[16,80,256]{2,1,0:T(8,128)(2,1)S(1)}, u32[]{:S(2)}, u32[]{:S(2)}) async-start(bf16[16,80,256]{2,1,0:T(8,128)(2,1)} %shard_map.137), calls=%async_computation.1 | async-start | bytes 1310720 | tf_op jit(solution)/shard_map/all_to_all | solution.py:412
  35.5 12.2 %all-to-all-done.1.got_ref = bf16[16,80,256]{2,1,0:T(8,128)(2,1)S(1)} async-done(((bf16[16,80,256]{2,1,0:T(8,128)(2,1)}), bf16[16,80,256]{2,1,0:T(8,128)(2,1)S(1)}, u32[]{:S(2)}, u32[]{:S(2)}) %all-to-all-start.1) | async-done | bytes 655392 | tf_op jit(solution)/shard_map/all_to_all | solution.py:412
  47.7 2.5 %shard_map.138 = (bf16[64,4096]{1,0:T(8,128)(2,1)S(1)}, bf16[64,256]{1,0:T(8,128)(2,1)S(1)}) custom-call(s32[3]{0:T(128)S(1)} %pad_add_fusion.1.at_ref, bf16[16,80,256]{2,1,0:T(8,128)(2,1)S(1)} %all-to-all-done.1.got_ref, bf16[256,8192]{1,0:T(8,128)(2,1)} %w_ref.3, bf16[384,8192]{1,0:T(8,128)(2,1)} %collective-permute-done.5.early_ref.wdb_ref), custom_call_target="tpu_custom_call" | custom-call | flops 140000000 | bytes 3145728 | tf_op jit(solution)/shard_map/pallas_call | solution.py:225
  50.2 1.7 %collective-permute-start.6 = (bf16[64,4096]{1,0:T(8,128)(2,1)S(1)}, bf16[64,4096]{1,0:T(8,128)(2,1)S(1)}, u32[]{:S(2)}, u32[]{:S(2)}) collective-permute-start(bf16[64,4096]{1,0:T(8,128)(2,1)S(1)} %get-tuple-element.14), channel_id=1, source_target_pairs={{0,1},{1,0},{2,3},{3,2},{4,5},{5,4},{6,7},{7,6},{8,9},{9,8},{10,11... | collective-permute-start | bytes 1572872 | tf_op jit(solution)/shard_map/ppermute | solution.py:359
  51.8 2.5 %shard_map.139 = bf16[64,4096]{1,0:T(8,128)(2,1)S(1)} custom-call(s32[3]{0:T(128)S(1)} %pad_add_fusion.1.at_ref, bf16[64,256]{1,0:T(8,128)(2,1)S(1)} %get-tuple-element.13.att_ref, bf16[256,8192]{1,0:T(8,128)(2,1)} %w_ref.3), custom_call_target="tpu_custom_call" | custom-call | flops 140000000 | bytes 3145728 | tf_op jit(solution)/shard_map/pallas_call | solution.py:249
  54.3 0.1 add_convert_fusion.1
  54.4 1.0 reshape.94
  55.4 3.6 %all-to-all-start.2 = ((bf16[16,4,4096]{2,1,0:T(4,128)(2,1)}), bf16[16,4,4096]{2,1,0:T(4,128)(2,1)S(1)}, u32[]{:S(2)}, u32[]{:S(2)}) async-start(bf16[16,4,4096]{2,1,0:T(4,128)(2,1)} %reshape.94), calls=%async_computation.2 | async-start | bytes 1048576 | tf_op jit(solution)/shard_map/all_to_all | solution.py:417
  59.1 0.1 collective-permute-start
  59.2 11.2 %all-to-all-done.2 = bf16[16,4,4096]{2,1,0:T(4,128)(2,1)S(1)} async-done(((bf16[16,4,4096]{2,1,0:T(4,128)(2,1)}), bf16[16,4,4096]{2,1,0:T(4,128)(2,1)S(1)}, u32[]{:S(2)}, u32[]{:S(2)}) %all-to-all-start.2) | async-done | bytes 524320 | tf_op jit(solution)/shard_map/all_to_all | solution.py:417
  70.4 0.2 convert_reduce_fusion
  70.6 0.2 multiply_reduce_fusion.1
  70.8 1.2 collective-permute-start.7
  72.0 0.8 collective-permute-done.7
  72.8 0.1 multiply_convert_fusion
  72.9 0.2 broadcast_in_dim.17
  73.1 15.7 %all_to_all.25 = bf16[16,4,4096]{2,1,0:T(4,128)(2,1)S(1)} all-to-all(bf16[16,4,4096]{2,1,0:T(4,128)(2,1)S(1)} %broadcast_in_dim.17), channel_id=1, replica_groups={{0,32,64,96,8,40,72,104,16,48,80,112,24,56,88,120},{2,34,66,98,10,42,74..., dimensions={0} | all-to-all | bytes 1048576 | tf_op jit(solution)/shard_map/all_to_all | solution.py:424
  88.8 0.1 reshape.95.after_ref.p0
  88.9 0.6 collective-permute-start.9
  89.5 0.8 collective-permute-start.11
  90.3 1.7 %collective-permute-start.13 = (bf16[64,4096]{1,0:T(8,128)(2,1)S(1)}, bf16[64,4096]{1,0:T(8,128)(2,1)S(1)}, u32[]{:S(2)}, u32[]{:S(2)}) collective-permute-start(bf16[64,4096]{1,0:T(8,128)(2,1)S(1)} %reshape.95.after_ref.p0), channel_id=1, source_target_pairs={{0,6},{1,25},{2,0},{3,27},{4,2},{5,29},{6,4},{7,31},{8,14},{9,1},{... | collective-permute-start | bytes 1572872 | tf_op jit(solution)/shard_map/ppermute | solution.py:427
  92.0 2.1 %collective-permute-start.8 = (bf16[64,4096]{1,0:T(8,128)(2,1)S(1)}, bf16[64,4096]{1,0:T(8,128)(2,1)S(1)}, u32[]{:S(2)}, u32[]{:S(2)}) collective-permute-start(bf16[64,4096]{1,0:T(8,128)(2,1)S(1)} %reshape.95.after_ref.p0), channel_id=1, source_target_pairs={{0,1},{1,0},{2,3},{3,2},{4,5},{5,4},{6,7},{7,6},{8,9},{9,8},{10,11... | collective-permute-start | bytes 1572872 | tf_op jit(solution)/shard_map/ppermute | solution.py:359
  94.1 7.1 %shard_map.140 = (bf16[8192,768]{1,0:T(8,128)(2,1)S(1)}, bf16[768,4096]{1,0:T(8,128)(2,1)S(1)}) custom-call(s32[3]{0:T(128)S(1)} %pad_add_fusion.1.at_ref, bf16[64,4096]{1,0:T(8,128)(2,1)S(1)} %reshape.95.after_ref.p0, bf16[8192,384]{1,0:T(8,128)(2,1)} %bitcast.21, bf16[8192,384]{1,0:T(8,128)(2,1)} %bitcast.22, bf16[384,8192]{1,0:T(8,128)(2,1)} %bitcast.20, ...), custom_call_target="tpu_custom_call" | custom-call | bytes 23068672 | tf_op jit(solution)/shard_map/pallas_call | solution.py:78
  101.2 2.9 %collective-permute-done.9.p1 = bf16[64,4096]{1,0:T(8,128)(2,1)S(1)} collective-permute-done((bf16[64,4096]{1,0:T(8,128)(2,1)S(1)}, bf16[64,4096]{1,0:T(8,128)(2,1)S(1)}, u32[]{:S(2)}, u32[]{:S(2)}) %collective-permute-start.9) | collective-permute-done | bytes 524320 | tf_op jit(solution)/shard_map/ppermute | solution.py:427
  104.1 1.3 collective-permute-start.12
  105.5 2.4 %shard_map.141.acc_ref = f32[256,768]{1,0:T(8,128)S(1)} custom-call(s32[3]{0:T(128)S(1)} %pad_add_fusion.1.at_ref, bf16[64,4096]{1,0:T(8,128)(2,1)S(1)} %reshape.95.after_ref.p0, bf16[64,4096]{1,0:T(8,128)(2,1)S(1)} %collective-permute-done.9.p1, bf16[64,4096]{1,0:T(8,128)(2,1)S(1)} %collective-permute-done.11.p2, ...), custom_call_target="tpu_custom_call" | custom-call | flops 16000000000 | bytes 9437184 | tf_op jit(solution)/shard_map/pallas_call | solution.py:294
  107.9 2.4 %shard_map.142.inner_ref = bf16[256,384]{1,0:T(8,128)(2,1)S(1)} custom-call(s32[3]{0:T(128)S(1)} %pad_add_fusion.1.at_ref, bf16[64,4096]{1,0:T(8,128)(2,1)S(1)} %collective-permute-done.8.p0, bf16[64,4096]{1,0:T(8,128)(2,1)S(1)} %collective-permute-done.10.p1, bf16[64,4096]{1,0:T(8,128)(2,1)S(1)} %collective-permute-done.12.p2, ...), custom_call_target="tpu_custom_call" | custom-call | flops 1600000000 | bytes 9437184 | tf_op jit(solution)/shard_map/pallas_call | solution.py:316
  110.3 0.6 collective-permute-start.15
  110.9 1.1 collective-permute-done.15.other_ref
  111.9 2.4 %shard_map.143 = (bf16[64,4096]{1,0:T(8,128)(2,1)S(1)}, bf16[64,4096]{1,0:T(8,128)(2,1)S(1)}, bf16[64,4096]{1,0:T(8,128)(2,1)S(1)}, bf16[64,4096]{1,0:T(8,128)(2,1)S(1)}) custom-call(s32[3]{0:T(128)S(1)} %pad_add_fusion.1.at_ref, bf16[256,384]{1,0:T(8,128)(2,1)S(1)} %shard_map.142.inner_ref, bf16[256,384]{1,0:T(8,128)(2,1)S(1)} %collective-permute-done.15.other_ref, ...), custom_call_target="tpu_custom_call" | custom-call | flops 1600000000 | bytes 9437184 | tf_op jit(solution)/shard_map/pallas_call | solution.py:347
  114.3 1.4 collective-permute-start.16
  115.7 0.7 collective-permute-start.17
  116.5 0.2 collective-permute-start.18
  116.6 6.1 %collective-permute-done.16 = bf16[64,4096]{1,0:T(8,128)(2,1)S(1)} collective-permute-done((bf16[64,4096]{1,0:T(8,128)(2,1)S(1)}, bf16[64,4096]{1,0:T(8,128)(2,1)S(1)}, u32[]{:S(2)}, u32[]{:S(2)}) %collective-permute-start.16) | collective-permute-done | bytes 524320 | tf_op jit(solution)/shard_map/ppermute | solution.py:433
  122.7 2.9 %collective-permute-done.17 = bf16[64,4096]{1,0:T(8,128)(2,1)S(1)} collective-permute-done((bf16[64,4096]{1,0:T(8,128)(2,1)S(1)}, bf16[64,4096]{1,0:T(8,128)(2,1)S(1)}, u32[]{:S(2)}, u32[]{:S(2)}) %collective-permute-start.17) | collective-permute-done | bytes 524320 | tf_op jit(solution)/shard_map/ppermute | solution.py:433
  125.6 5.6 %collective-permute-done.18 = bf16[64,4096]{1,0:T(8,128)(2,1)S(1)} collective-permute-done((bf16[64,4096]{1,0:T(8,128)(2,1)S(1)}, bf16[64,4096]{1,0:T(8,128)(2,1)S(1)}, u32[]{:S(2)}, u32[]{:S(2)}) %collective-permute-start.18) | collective-permute-done | bytes 524320 | tf_op jit(solution)/shard_map/ppermute | solution.py:433
  131.2 0.3 add_convert_fusion
  131.4 1.0 reshape.96
  132.5 3.8 %all-to-all-start.4 = ((bf16[16,4,4096]{2,1,0:T(4,128)(2,1)}), bf16[16,4,4096]{2,1,0:T(4,128)(2,1)S(1)}, u32[]{:S(2)}, u32[]{:S(2)}) async-start(bf16[16,4,4096]{2,1,0:T(4,128)(2,1)} %reshape.96), calls=%async_computation.4 | async-start | bytes 1048576 | tf_op jit(solution)/shard_map/all_to_all | solution.py:435
  136.3 0.1 fusion
  136.4 2.0 %collective-permute-start.19 = (f32[2,4]{1,0:T(2,128)S(1)}, f32[2,4]{1,0:T(2,128)S(1)}, u32[]{:S(2)}, u32[]{:S(2)}) collective-permute-start(f32[2,4]{1,0:T(2,128)S(1)} %fusion), channel_id=1, source_target_pairs={{0,1},{1,0},{2,3},{3,2},{4,5},{5,4},{6,7},{7,6},{8,9},{9,8},{10,11... | collective-permute-start | bytes 104 | tf_op jit(solution)/shard_map/ppermute | solution.py:359
  138.4 0.8 collective-permute-done.19
  139.2 0.1 copy.20
  139.3 8.6 %all-to-all-done.4 = bf16[16,4,4096]{2,1,0:T(4,128)(2,1)S(1)} async-done(((bf16[16,4,4096]{2,1,0:T(4,128)(2,1)}), bf16[16,4,4096]{2,1,0:T(4,128)(2,1)S(1)}, u32[]{:S(2)}, u32[]{:S(2)}) %all-to-all-start.4) | async-done | bytes 524320 | tf_op jit(solution)/shard_map/all_to_all | solution.py:435
  147.9 0.3 multiply_reduce_fusion
  148.3 0.5 collective-permute-start.20
  148.8 0.8 collective-permute-done.20
  149.7 0.7 broadcast_select_fusion
  (35 shorter events, 0.3 us)
Async XLA Ops:
  0.0 47.6 %collective-permute-start.5 = (bf16[384,8192]{1,0:T(8,128)(2,1)}, bf16[384,8192]{1,0:T(8,128)(2,1)}, u32[]{:S(2)}, u32[]{:S(2)}) collective-permute-start(bf16[384,8192]{1,0:T(8,128)(2,1)} %bitcast.19), channel_id=1, source_target_pairs={{0,1},{1,0},{2,3},{3,2},{4,5},{5,4},{6,7},{7,6},{8,9},{9,8},{10,11... | collective-permute-start | bytes 18874376 | tf_op jit(solution)/shard_map/ppermute | solution.py:359
  1.4 22.7 %collective-permute-start.1 = (bf16[512,1024]{1,0:T(8,128)(2,1)}, bf16[512,1024]{1,0:T(8,128)(2,1)S(1)}, u32[]{:S(2)}, u32[]{:S(2)}) collective-permute-start(bf16[512,1024]{1,0:T(8,128)(2,1)} %ka_ref.1), channel_id=1, source_target_pairs={{0,1},{1,0},{2,3},{3,2},{4,5},{5,4},{6,7},{7,6},{8,9},{9,8},{10,11... | collective-permute-start | bytes 3145736 | tf_op jit(solution)/shard_map/ppermute | solution.py:359
  1.4 22.7 %collective-permute-start.2 = (bf16[512,1024]{1,0:T(8,128)(2,1)}, bf16[512,1024]{1,0:T(8,128)(2,1)}, u32[]{:S(2)}, u32[]{:S(2)}) collective-permute-start(bf16[512,1024]{1,0:T(8,128)(2,1)} %va_ref.1), channel_id=1, source_target_pairs={{0,1},{1,0},{2,3},{3,2},{4,5},{5,4},{6,7},{7,6},{8,9},{9,8},{10,11... | collective-permute-start | bytes 3145736 | tf_op jit(solution)/shard_map/ppermute | solution.py:359
  1.9 12.9 %collective-permute-start.3 = (bf16[64,2,1024]{2,1,0:T(2,128)(2,1)}, bf16[64,2,1024]{2,1,0:T(2,128)(2,1)S(1)}, u32[]{:S(2)}, u32[]{:S(2)}) collective-permute-start(bf16[64,2,1024]{2,1,0:T(2,128)(2,1)} %param.17), channel_id=1, source_target_pairs={{0,1},{1,0},{2,3},{3,2},{4,5},{5,4},{6,7},{7,6},{8,9},{9,8},{10,11... | collective-permute-start | bytes 786440 | tf_op jit(solution)/shard_map/ppermute | solution.py:359
  1.9 13.4 %collective-permute-start.4 = (bf16[64,2,1024]{2,1,0:T(2,128)(2,1)}, bf16[64,2,1024]{2,1,0:T(2,128)(2,1)}, u32[]{:S(2)}, u32[]{:S(2)}) collective-permute-start(bf16[64,2,1024]{2,1,0:T(2,128)(2,1)} %param.18), channel_id=1, source_target_pairs={{0,1},{1,0},{2,3},{3,2},{4,5},{5,4},{6,7},{7,6},{8,9},{9,8},{10,11... | collective-permute-start | bytes 786440 | tf_op jit(solution)/shard_map/ppermute | solution.py:359
  2.4 0.8 copy-start
  4.1 19.9 %all-to-all-start = ((bf16[32,2,4096]{2,1,0:T(2,128)(2,1)}), bf16[32,2,4096]{2,1,0:T(2,128)(2,1)S(1)}, u32[]{:S(2)}, u32[]{:S(2)}) async-start(bf16[32,2,4096]{2,1,0:T(2,128)(2,1)} %shard_map.136), calls=%async_computation | async-start | bytes 1048576 | tf_op jit(solution)/shard_map/all_to_all | solution.py:395
  31.8 15.9 %all-to-all-start.1 = ((bf16[16,80,256]{2,1,0:T(8,128)(2,1)}), bf16[16,80,256]{2,1,0:T(8,128)(2,1)S(1)}, u32[]{:S(2)}, u32[]{:S(2)}) async-start(bf16[16,80,256]{2,1,0:T(8,128)(2,1)} %shard_map.137), calls=%async_computation.1 | async-start | bytes 1310720 | tf_op jit(solution)/shard_map/all_to_all | solution.py:412
  50.1 8.9 %copy-start.1 = (bf16[2,8192]{1,0:T(2,128)(2,1)S(1)}, bf16[2,8192]{1,0:T(2,128)(2,1)}, u32[]{:S(2)}) copy-start(bf16[2,8192]{1,0:T(2,128)(2,1)} %param.20) | copy-start | bytes 98308
  50.1 9.0 %copy-start.2 = (bf16[8192]{0:T(1024)(128)(2,1)S(1)}, bf16[8192]{0:T(1024)(128)(2,1)}, u32[]{:S(2)}) copy-start(bf16[8192]{0:T(1024)(128)(2,1)} %param.22) | copy-start | bytes 49156
  50.2 4.1 %collective-permute-start.6 = (bf16[64,4096]{1,0:T(8,128)(2,1)S(1)}, bf16[64,4096]{1,0:T(8,128)(2,1)S(1)}, u32[]{:S(2)}, u32[]{:S(2)}) collective-permute-start(bf16[64,4096]{1,0:T(8,128)(2,1)S(1)} %get-tuple-element.14), channel_id=1, source_target_pairs={{0,1},{1,0},{2,3},{3,2},{4,5},{5,4},{6,7},{7,6},{8,9},{9,8},{10,11... | collective-permute-start | bytes 1572872 | tf_op jit(solution)/shard_map/ppermute | solution.py:359
  55.4 14.9 %all-to-all-start.2 = ((bf16[16,4,4096]{2,1,0:T(4,128)(2,1)}), bf16[16,4,4096]{2,1,0:T(4,128)(2,1)S(1)}, u32[]{:S(2)}, u32[]{:S(2)}) async-start(bf16[16,4,4096]{2,1,0:T(4,128)(2,1)} %reshape.94), calls=%async_computation.2 | async-start | bytes 1048576 | tf_op jit(solution)/shard_map/all_to_all | solution.py:417
  59.1 11.5 %collective-permute-start = (bf16[2,4096]{1,0:T(2,128)(2,1)S(1)}, bf16[2,4096]{1,0:T(2,128)(2,1)S(1)}, u32[]{:S(2)}, u32[]{:S(2)}) collective-permute-start(bf16[2,4096]{1,0:T(2,128)(2,1)S(1)} %get-tuple-element.25), channel_id=1, source_target_pairs={{0,1},{1,0},{2,3},{3,2},{4,5},{5,4},{6,7},{7,6},{8,9},{9,8},{10,11... | collective-permute-start | bytes 49160 | tf_op jit(solution)/shard_map/ppermute | solution.py:359
  70.8 2.0 %collective-permute-start.7 = (f32[4,1]{0,1:T(1,128)S(1)}, f32[4,1]{0,1:T(1,128)S(1)}, u32[]{:S(2)}, u32[]{:S(2)}) collective-permute-start(f32[4,1]{0,1:T(1,128)S(1)} %bitcast.24), channel_id=1, source_target_pairs={{0,1},{1,0},{2,3},{3,2},{4,5},{5,4},{6,7},{7,6},{8,9},{9,8},{10,11... | collective-permute-start | bytes 56 | tf_op jit(solution)/shard_map/ppermute | solution.py:359
  88.9 15.2 %collective-permute-start.9 = (bf16[64,4096]{1,0:T(8,128)(2,1)S(1)}, bf16[64,4096]{1,0:T(8,128)(2,1)S(1)}, u32[]{:S(2)}, u32[]{:S(2)}) collective-permute-start(bf16[64,4096]{1,0:T(8,128)(2,1)S(1)} %reshape.95.after_ref.p0), channel_id=1, source_target_pairs={{0,2},{1,9},{2,4},{3,11},{4,6},{5,13},{6,0},{7,15},{8,10},{9,17},{... | collective-permute-start | bytes 1572872 | tf_op jit(solution)/shard_map/ppermute | solution.py:427
  89.5 14.6 %collective-permute-start.11 = (bf16[64,4096]{1,0:T(8,128)(2,1)S(1)}, bf16[64,4096]{1,0:T(8,128)(2,1)S(1)}, u32[]{:S(2)}, u32[]{:S(2)}) collective-permute-start(bf16[64,4096]{1,0:T(8,128)(2,1)S(1)} %reshape.95.after_ref.p0), channel_id=1, source_target_pairs={{0,4},{1,17},{2,6},{3,19},{4,0},{5,21},{6,2},{7,23},{8,12},{9,25},... | collective-permute-start | bytes 1572872 | tf_op jit(solution)/shard_map/ppermute | solution.py:427
  90.3 15.1 %collective-permute-start.13 = (bf16[64,4096]{1,0:T(8,128)(2,1)S(1)}, bf16[64,4096]{1,0:T(8,128)(2,1)S(1)}, u32[]{:S(2)}, u32[]{:S(2)}) collective-permute-start(bf16[64,4096]{1,0:T(8,128)(2,1)S(1)} %reshape.95.after_ref.p0), channel_id=1, source_target_pairs={{0,6},{1,25},{2,0},{3,27},{4,2},{5,29},{6,4},{7,31},{8,14},{9,1},{... | collective-permute-start | bytes 1572872 | tf_op jit(solution)/shard_map/ppermute | solution.py:427
  92.0 15.9 %collective-permute-start.8 = (bf16[64,4096]{1,0:T(8,128)(2,1)S(1)}, bf16[64,4096]{1,0:T(8,128)(2,1)S(1)}, u32[]{:S(2)}, u32[]{:S(2)}) collective-permute-start(bf16[64,4096]{1,0:T(8,128)(2,1)S(1)} %reshape.95.after_ref.p0), channel_id=1, source_target_pairs={{0,1},{1,0},{2,3},{3,2},{4,5},{5,4},{6,7},{7,6},{8,9},{9,8},{10,11... | collective-permute-start | bytes 1572872 | tf_op jit(solution)/shard_map/ppermute | solution.py:359
  104.1 3.8 %collective-permute-start.10 = (bf16[64,4096]{1,0:T(8,128)(2,1)S(1)}, bf16[64,4096]{1,0:T(8,128)(2,1)S(1)}, u32[]{:S(2)}, u32[]{:S(2)}) collective-permute-start(bf16[64,4096]{1,0:T(8,128)(2,1)S(1)} %collective-permute-done.9.p1), channel_id=1, source_target_pairs={{0,1},{1,0},{2,3},{3,2},{4,5},{5,4},{6,7},{7,6},{8,9},{9,8},{10,11... | collective-permute-start | bytes 1572872 | tf_op jit(solution)/shard_map/ppermute | solution.py:359
  104.1 3.8 %collective-permute-start.12 = (bf16[64,4096]{1,0:T(8,128)(2,1)S(1)}, bf16[64,4096]{1,0:T(8,128)(2,1)S(1)}, u32[]{:S(2)}, u32[]{:S(2)}) collective-permute-start(bf16[64,4096]{1,0:T(8,128)(2,1)S(1)} %collective-permute-done.11.p2), channel_id=1, source_target_pairs={{0,1},{1,0},{2,3},{3,2},{4,5},{5,4},{6,7},{7,6},{8,9},{9,8},{10,11... | collective-permute-start | bytes 1572872 | tf_op jit(solution)/shard_map/ppermute | solution.py:359
  105.4 2.5 %collective-permute-start.14 = (bf16[64,4096]{1,0:T(8,128)(2,1)S(1)}, bf16[64,4096]{1,0:T(8,128)(2,1)S(1)}, u32[]{:S(2)}, u32[]{:S(2)}) collective-permute-start(bf16[64,4096]{1,0:T(8,128)(2,1)S(1)} %collective-permute-done.13.p3), channel_id=1, source_target_pairs={{0,1},{1,0},{2,3},{3,2},{4,5},{5,4},{6,7},{7,6},{8,9},{9,8},{10,11... | collective-permute-start | bytes 1572872 | tf_op jit(solution)/shard_map/ppermute | solution.py:359
  110.3 26.0 %copy-start.3 = (f32[2,2]{1,0:T(2,128)S(1)}, f32[2,2]{1,0:T(2,128)}, u32[]{:S(2)}) copy-start(f32[2,2]{1,0:T(2,128)} %param.24) | copy-start | bytes 52
  110.3 26.0 %copy-start.4 = (s32[2,2]{1,0:T(2,128)S(1)}, s32[2,2]{1,0:T(2,128)}, u32[]{:S(2)}) copy-start(s32[2,2]{1,0:T(2,128)} %param.23) | copy-start | bytes 52
  110.3 1.6 %collective-permute-start.15 = (bf16[256,384]{1,0:T(8,128)(2,1)S(1)}, bf16[256,384]{1,0:T(8,128)(2,1)S(1)}, u32[]{:S(2)}, u32[]{:S(2)}) collective-permute-start(bf16[256,384]{1,0:T(8,128)(2,1)S(1)} %shard_map.142.inner_ref), channel_id=1, source_target_pairs={{0,1},{1,0},{2,3},{3,2},{4,5},{5,4},{6,7},{7,6},{8,9},{9,8},{10,11... | collective-permute-start | bytes 589832 | tf_op jit(solution)/shard_map/ppermute | solution.py:359
  114.3 8.4 %collective-permute-start.16 = (bf16[64,4096]{1,0:T(8,128)(2,1)S(1)}, bf16[64,4096]{1,0:T(8,128)(2,1)S(1)}, u32[]{:S(2)}, u32[]{:S(2)}) collective-permute-start(bf16[64,4096]{1,0:T(8,128)(2,1)S(1)} %get-tuple-element.18), channel_id=1, source_target_pairs={{0,6},{1,25},{2,0},{3,27},{4,2},{5,29},{6,4},{7,31},{8,14},{9,1},{... | collective-permute-start | bytes 1572872 | tf_op jit(solution)/shard_map/ppermute | solution.py:433
  115.7 9.9 %collective-permute-start.17 = (bf16[64,4096]{1,0:T(8,128)(2,1)S(1)}, bf16[64,4096]{1,0:T(8,128)(2,1)S(1)}, u32[]{:S(2)}, u32[]{:S(2)}) collective-permute-start(bf16[64,4096]{1,0:T(8,128)(2,1)S(1)} %get-tuple-element.19), channel_id=1, source_target_pairs={{0,4},{1,17},{2,6},{3,19},{4,0},{5,21},{6,2},{7,23},{8,12},{9,25},... | collective-permute-start | bytes 1572872 | tf_op jit(solution)/shard_map/ppermute | solution.py:433
  116.5 14.7 %collective-permute-start.18 = (bf16[64,4096]{1,0:T(8,128)(2,1)S(1)}, bf16[64,4096]{1,0:T(8,128)(2,1)S(1)}, u32[]{:S(2)}, u32[]{:S(2)}) collective-permute-start(bf16[64,4096]{1,0:T(8,128)(2,1)S(1)} %get-tuple-element.20), channel_id=1, source_target_pairs={{0,2},{1,9},{2,4},{3,11},{4,6},{5,13},{6,0},{7,15},{8,10},{9,17},{... | collective-permute-start | bytes 1572872 | tf_op jit(solution)/shard_map/ppermute | solution.py:433
  132.5 15.5 %all-to-all-start.4 = ((bf16[16,4,4096]{2,1,0:T(4,128)(2,1)}), bf16[16,4,4096]{2,1,0:T(4,128)(2,1)S(1)}, u32[]{:S(2)}, u32[]{:S(2)}) async-start(bf16[16,4,4096]{2,1,0:T(4,128)(2,1)} %reshape.96), calls=%async_computation.4 | async-start | bytes 1048576 | tf_op jit(solution)/shard_map/all_to_all | solution.py:435
  136.4 2.8 %collective-permute-start.19 = (f32[2,4]{1,0:T(2,128)S(1)}, f32[2,4]{1,0:T(2,128)S(1)}, u32[]{:S(2)}, u32[]{:S(2)}) collective-permute-start(f32[2,4]{1,0:T(2,128)S(1)} %fusion), channel_id=1, source_target_pairs={{0,1},{1,0},{2,3},{3,2},{4,5},{5,4},{6,7},{7,6},{8,9},{9,8},{10,11... | collective-permute-start | bytes 104 | tf_op jit(solution)/shard_map/ppermute | solution.py:359
  148.3 1.3 collective-permute-start.20

commit v4 on v3

--- a/solution.py
+++ b/solution.py
@@ -94,7 +94,8 @@
     return pltpu.with_memory_space_constraint(array, pltpu.HBM)
 
 
-def spread_kernel(q_ref, out_ref):
+def spread_kernel(q_ref, hidden_ref, out_ref, copy_ref):
+    copy_ref[...] = hidden_ref[...]
     for half in range(2):
         value = jnp.concatenate(
             [q_ref[:, (2 * k + half) * 2 * HD : (2 * k + half + 1) * 2 * HD] for k in range(16)], axis=1
@@ -103,18 +104,41 @@
             out_ref[2 * chip + half] = value
 
 
-def spread(queries):
+def spread(queries, hidden):
+    whole = pl.BlockSpec((2, D), lambda i: (0, 0))
     return pl.pallas_call(
         spread_kernel,
-        in_specs=[WHOLE],
-        out_specs=WHOLE,
-        out_shape=jax.ShapeDtypeStruct((32, 2, HALF), BF),
+        grid=(1,),
+        in_specs=[whole] * 2,
+        out_specs=[pl.BlockSpec((32, 2, HALF), lambda i: (0, 0, 0)), whole],
+        out_shape=[jax.ShapeDtypeStruct((32, 2, HALF), BF), jax.ShapeDtypeStruct((2, D), BF)],
         compiler_params=pltpu.CompilerParams(vmem_limit_bytes=4 * MB),
         cost_estimate=pl.CostEstimate(flops=0, bytes_accessed=MB, transcendentals=0),
-    )(queries)
-
-
-def attend_kernel(q_ref, ka_ref, kb_ref, va_ref, vb_ref, sa_ref, sb_ref, left_ref, out_ref):
+    )(in_hbm(queries), in_hbm(hidden))
+
+
+def store_part(out_ref, first, acc, top, total):
+    rows = 64
+    size = (4 * rows, 4 * rows)
+    eye = lax.broadcasted_iota(jnp.int32, size, 0) == lax.broadcasted_iota(jnp.int32, size, 1)
+    top_row = jnp.sum(jnp.where(eye, top, 0.0), axis=0, keepdims=True)
+    total_row = jnp.sum(jnp.where(eye, total, 0.0), axis=0, keepdims=True)
+    total_high = total_row.astype(BF).astype(F32)
+    total_low = total_row - total_high
+    line = lax.broadcasted_iota(jnp.int32, (8, 4 * rows), 0)
+    for k in range(2):
+        for j in range(2):
+            g = 2 * k + j
+            out_ref[first + k, 0:rows, j * HD : (j + 1) * HD] = acc[g * rows : (g + 1) * rows].astype(BF)
+        part = slice(k * 2 * rows, (k + 1) * 2 * rows)
+        high = jnp.concatenate([top_row[:, part], total_high[:, part]], axis=1)
+        low = jnp.concatenate([top_row[:, part], total_low[:, part]], axis=1)
+        tail = jnp.where(line == 0, high, jnp.where(line == 1, low, 0.0))
+        out_ref[first + k, rows : rows + 8, :] = tail.astype(BF)
+
+
+def attend_kernel(q_ref, ka_ref, kb_ref, va_ref, vb_ref, sa_ref, sb_ref, left_ref, *refs):
+    out_ref = refs[-1]
     rows = 64
     row = lax.broadcasted_iota(jnp.int32, (4 * rows, 4 * rows), 0)
     col = lax.broadcasted_iota(jnp.int32, (4 * rows, 4 * rows), 1)
@@ -122,8 +146,6 @@
     live = (row % rows == col % (2 * rows) // 2) & (
         col % 2 < jnp.where(col < 2 * rows, left[:, 0:1], left[:, 1:2])
     )
-    eye = row == col
-    line = lax.broadcasted_iota(jnp.int32, (16, 4 * rows), 0)
     for h in range(KV):
         at = slice(h * HD, (h + 1) * HD)
         at_v = slice((KV + h) * HD, (KV + h + 1) * HD)
@@ -139,67 +161,37 @@
         ]
         top = functools.reduce(jnp.maximum, [jnp.max(s, axis=1, keepdims=True) for s in scores])
         top = (top * SCALE).astype(BF).astype(F32)
-        total = jnp.zeros((4 * rows, 1), F32)
-        acc = jnp.zeros((4 * rows, HD), F32)
+        total, acc = 0.0, 0.0
         for s, v in zip(scores, (va_ref[:, at], vb_ref[:, at], suffix_v)):
             prob = jnp.exp2(s * SCALE - top)
             total = total + jnp.sum(prob, axis=1, keepdims=True)
             acc = acc + dot(prob.astype(BF), v)
-        top_row = jnp.sum(jnp.where(eye, top, 0.0), axis=0, keepdims=True)
-        total_row = jnp.sum(jnp.where(eye, total, 0.0), axis=0, keepdims=True)
-        total_high = total_row.astype(BF).astype(F32)
-        total_low = total_row - total_high
-        for k in range(2):
-            for j in range(2):
-                g = 2 * k + j
-                out_ref[2 * h + k, 0:rows, j * HD : (j + 1) * HD] = acc[
-                    g * rows : (g + 1) * rows
-                ].astype(BF)
-            part = slice(k * 2 * rows, (k + 1) * 2 * rows)
-            high = jnp.concatenate([top_row[:, part], total_high[:, part]], axis=1)
-            low = jnp.concatenate([top_row[:, part], total_low[:, part]], axis=1)
-            tail = jnp.where(line == 0, high, jnp.where(line == 1, low, 0.0))
-            out_ref[2 * h + k, rows : rows + 16, :] = tail.astype(BF)
-
-
-def attend(q, ka, kb, va, vb, sa, sb, left):
+        store_part(out_ref, 2 * h, acc, top, total)
+
+
+def attend(q, ka, kb, va, vb, sa, sb, left, early):
     arrays = (q, ka, kb, va, vb, sa, sb, left)
     return pl.pallas_call(
         attend_kernel,
         grid=(1,),
-        in_specs=[pl.BlockSpec(a.shape, lambda i: (0, 0)) for a in arrays],
-        out_specs=pl.BlockSpec((16, 80, 2 * HD), lambda i: (0, 0, 0)),
-        out_shape=jax.ShapeDtypeStruct((16, 80, 2 * HD), BF),
+        in_specs=[pl.BlockSpec(a.shape, lambda i: (0, 0)) for a in arrays]
+        + [pl.BlockSpec(memory_space=pl.ANY)] * len(early),
+        out_specs=pl.BlockSpec((16, 72, 2 * HD), lambda i: (0, 0, 0)),
+        out_shape=jax.ShapeDtypeStruct((16, 72, 2 * HD), BF),
         compiler_params=pltpu.CompilerParams(vmem_limit_bytes=24 * MB),
         cost_estimate=pl.CostEstimate(flops=1400000000, bytes_accessed=6 * MB, transcendentals=2700000),
-    )(q, in_hbm(ka), kb, in_hbm(va), vb, sa, sb, left)
-
-
-def columns_of(w_ref, half, buffer, sems):
+    )(q, in_hbm(ka), kb, in_hbm(va), vb, sa, sb, left, *early)
+
+
+def half_product(attended, w_ref, half, out_ref):
     width = HALF // 4
-    return [
-        pltpu.make_async_copy(
-            w_ref.at[:, pl.ds(pl.multiple_of(half * HALF + part * width, width), width)],
-            buffer.at[:, pl.ds(part * width, width)],
-            sems.at[part],
-        )
-        for part in range(4)
-    ]
-
-
-def project_parts(copies, attended, buffer, out_ref):
-    width = HALF // 4
-    for part, copy in enumerate(copies):
-        copy.wait()
-        at = slice(part * width, (part + 1) * width)
-        out_ref[:, at] = dot(attended, buffer[:, at]).astype(BF)
-
-
-def project_kernel(at_ref, got_ref, w_ref, early_ref, out_ref, att_ref, buffer, sems):
+    for part in range(4):
+        cols = pl.ds(pl.multiple_of(half * HALF + part * width, width), width)
+        out_ref[:, part * width : (part + 1) * width] = dot(attended, w_ref[:, cols]).astype(BF)
+
+
+def project_kernel(at_ref, got_ref, w_ref, early_ref, out_ref, att_ref):
     rows = 64
-    copies = columns_of(w_ref, 1 - at_ref[0], buffer, sems)
-    for copy in copies:
-        copy.start()
     tops = [got_ref[s, rows : rows + 1, 0 : 2 * rows].astype(F32) for s in range(16)]
     sums = [
         got_ref[s, rows : rows + 1, 2 * rows :].astype(F32)
@@ -218,47 +210,33 @@
             share = jnp.sum(jnp.where(here, factors[s] / total, 0.0), axis=1, keepdims=True)
             acc = acc + got_ref[s, 0:rows, j * HD : (j + 1) * HD].astype(F32) * share
         att_ref[:, j * HD : (j + 1) * HD] = acc.astype(BF)
-    project_parts(copies, att_ref[...], buffer, out_ref)
+    half_product(att_ref[...], w_ref, 1 - at_ref[0], out_ref)
 
 
 def project_other(at, got, w_out, early):
     return pl.pallas_call(
         project_kernel,
-        in_specs=[
-            pl.BlockSpec(memory_space=pltpu.SMEM),
-            pl.BlockSpec(memory_space=pltpu.VMEM),
-            pl.BlockSpec(memory_space=pl.ANY),
-            pl.BlockSpec(memory_space=pl.ANY),
-        ],
-        out_specs=[pl.BlockSpec(memory_space=pltpu.VMEM)] * 2,
+        in_specs=[SCALARS, WHOLE, WHOLE, pl.BlockSpec(memory_space=pl.ANY)],
+        out_specs=[WHOLE] * 2,
         out_shape=[jax.ShapeDtypeStruct((64, HALF), BF), jax.ShapeDtypeStruct((64, 256), BF)],
-        scratch_shapes=[pltpu.VMEM((256, HALF), BF), pltpu.SemaphoreType.DMA((4,))],
         compiler_params=pltpu.CompilerParams(vmem_limit_bytes=16 * MB),
         cost_estimate=pl.CostEstimate(flops=140000000, bytes_accessed=3 * MB, transcendentals=0),
-    )(at, got, in_hbm(w_out), in_hbm(early))
-
-
-def project_mine_kernel(at_ref, att_ref, w_ref, out_ref, buffer, sems):
-    copies = columns_of(w_ref, at_ref[0], buffer, sems)
-    for copy in copies:
-        copy.start()
-    project_parts(copies, att_ref[...], buffer, out_ref)
+    )(at, got, in_vmem(w_out), in_hbm(early))
+
+
+def project_mine_kernel(at_ref, att_ref, w_ref, out_ref):
+    half_product(att_ref[...], w_ref, at_ref[0], out_ref)
 
 
 def project_mine(at, attended, w_out):
     return pl.pallas_call(
         project_mine_kernel,
-        in_specs=[
-            pl.BlockSpec(memory_space=pltpu.SMEM),
-            pl.BlockSpec(memory_space=pltpu.VMEM),
-            pl.BlockSpec(memory_space=pl.ANY),
-        ],
-        out_specs=pl.BlockSpec(memory_space=pltpu.VMEM),
+        in_specs=[SCALARS, WHOLE, WHOLE],
+        out_specs=WHOLE,
         out_shape=jax.ShapeDtypeStruct((64, HALF), BF),
-        scratch_shapes=[pltpu.VMEM((256, HALF), BF), pltpu.SemaphoreType.DMA((4,))],
         compiler_params=pltpu.CompilerParams(vmem_limit_bytes=16 * MB),
         cost_estimate=pl.CostEstimate(flops=140000000, bytes_accessed=3 * MB, transcendentals=0),
-    )(at, attended, in_hbm(w_out))
+    )(at, attended, in_vmem(w_out))
 
 
 def rolled(place, back):
@@ -284,22 +262,22 @@
             acc_ref[...] += value
 
 
-def first_kernel(at_ref, p0, p1, p2, p3, w_ref, acc_ref, x_ref):
+def first_kernel(at_ref, p0, p1, p2, p3, w_ref, early_ref, acc_ref, x_ref):
     gathered(x_ref, (p0, p1, p2, p3), at_ref[1], True)
     multiplied(x_ref, w_ref, at_ref[0], acc_ref)
 
 
-def expert_first(at, pieces, gate_up):
+def expert_first(at, pieces, gate_up, early):
     units = gate_up.shape[1]
     return pl.pallas_call(
         first_kernel,
-        in_specs=[SCALARS] + [WHOLE] * 5,
+        in_specs=[SCALARS] + [WHOLE] * 5 + [pl.BlockSpec(memory_space=pl.ANY)],
         out_specs=WHOLE,
         out_shape=jax.ShapeDtypeStruct((256, units), F32),
         scratch_shapes=[pltpu.VMEM((256, HALF), BF)],
         compiler_params=pltpu.CompilerParams(vmem_limit_bytes=12 * MB),
         cost_estimate=pl.CostEstimate(flops=16000000000, bytes_accessed=9 * MB, transcendentals=0),
-    )(at, *pieces, in_vmem(gate_up))
+    )(at, *pieces, in_vmem(gate_up), early)
 
 
 def second_kernel(at_ref, p0, p1, p2, p3, w_ref, acc_ref, inner_ref, x_ref, more_ref):
@@ -353,6 +331,28 @@
         compiler_params=pltpu.CompilerParams(vmem_limit_bytes=12 * MB),
         cost_estimate=pl.CostEstimate(flops=1600000000, bytes_accessed=9 * MB, transcendentals=0),
     )(at, inner, other, in_vmem(down))
+
+
+def mix_kernel(at_ref, got_ref, residual_ref, weights_ref, kept_ref, sent_ref):
+    mixed = residual_ref[...]
+    weights = weights_ref[...]
+    for expert in range(4):
+        value = functools.reduce(jnp.add, [got_ref[4 * line + expert].astype(F32) for line in range(4)])
+        mixed = mixed + value * weights[:, expert : expert + 1]
+    first = at_ref[0] == 0
+    kept_ref[...] = jnp.where(first, mixed[0:2], mixed[2:4]).astype(BF)
+    sent_ref[...] = jnp.where(first, mixed[2:4], mixed[0:2]).astype(BF)
+
+
+def mix(at, got, residual, weights):
+    return pl.pallas_call(
+        mix_kernel,
+        in_specs=[SCALARS] + [WHOLE] * 3,
+        out_specs=[WHOLE] * 2,
+        out_shape=[jax.ShapeDtypeStruct((2, HALF), BF)] * 2,
+        compiler_params=pltpu.CompilerParams(vmem_limit_bytes=8 * MB),
+        cost_estimate=pl.CostEstimate(flops=1000000, bytes_accessed=MB, transcendentals=0),
+    )(at, got, residual, weights)
 
 
 def swap(value):
@@ -386,7 +386,7 @@
             c == 0, jnp.concatenate([own, got], axis=axis), jnp.concatenate([got, own], axis=axis)
         )
 
-    q = spread(queries)
+    q, hidden_in = spread(queries, hidden_in)
     keys_b = swap(prefix_keys)
     values_b = swap(prefix_values)
     suffix_keys_b = swap(suffix_keys)
@@ -408,7 +408,8 @@
     weights = in_order(weights, swap(weights), 0)
     gain = lax.dynamic_slice_in_dim(norm_gain, c * HALF, HALF, 0).astype(F32)
 
-    parts = attend(q, prefix_keys, keys_b, prefix_values, values_b, suffix, suffix_b, left)
+    early = (hidden, gain, at)
+    parts = attend(q, prefix_keys, keys_b, prefix_values, values_b, suffix, suffix_b, left, early)
     parts = lax.all_to_all(parts, ("z", "y"), split_axis=0, concat_axis=0, tiled=True)
     other, attended = project_other(at, parts, w_out, w_down_b)
     other = swap(other)
@@ -427,7 +428,7 @@
     pieces = [own] + [lax.ppermute(own, PLANE, line_shift(s)) for s in (1, 2, 3)]
     gate_up, down = fetch(at, own, w_gate[0], w_up[0], w_down[0], w_down_b)
     pieces_b = [swap(piece) for piece in pieces]
-    acc = expert_first(at, pieces, gate_up)
+    acc = expert_first(at, pieces, gate_up, weights)
     inner = expert_second(at, pieces_b, gate_up, acc)
     out = expert_third(at, inner, swap(inner), down)
     out = [out[0]] + [lax.ppermute(out[s], PLANE, line_shift(4 - s)) for s in (1, 2, 3)]
@@ -435,11 +436,8 @@
     out = lax.all_to_all(
         out.reshape(16, 4, HALF), ALL, split_axis=0, concat_axis=0, tiled=True, axis_index_groups=wide
     )
-    out = out.reshape(4, 4, 4, HALF).astype(F32)
-    mixed = residual + jnp.sum(out * weights.T[None, :, :, None], axis=(0, 1))
-    mixed = mixed.astype(BF)
-    kept = lax.dynamic_slice_in_dim(mixed, 2 * c, 2, 0)
-    got = swap(lax.dynamic_slice_in_dim(mixed, 2 * (1 - c), 2, 0))
+    kept, sent = mix(at, out, residual, weights)
+    got = swap(sent)
     return in_order(kept, got, 1)
 
 

time: 151 us -> 144 us (0.954)
  blocking collectives: 15.7 us -> 59 us
  waiting for transfers between devices: 60.4 us -> 26.3 us
  starting transfers between devices: 36.6 us -> 25.4 us
  local copies, waits for them, and re-layouts: 3.99 us -> 1.63 us
  Pallas kernels: 27.6 us -> 25.7 us
    all_to_all x0 -> x3, blocking collectives: none -> 43.5 us  [the longest x1 15.3 us: local(): lax.all_to_all(out.reshape(16, 4, HALF), ALL, split_axis=0, concat_axis=0...]
    all_to_all x3 -> x0, waiting for transfers between devices: 32 us -> none  [the longest x1 12.2 us: local(): lax.all_to_all(parts, ('z', 'y'), split_axis=0, concat_axis=0, tiled=True)]
    all_to_all x3 -> x0, starting transfers between devices: 11 us -> none  [the longest x1 3.85 us: local(): lax.all_to_all(out.reshape(16, 4, HALF), ALL, split_axis=0, concat_axis=0...]
    all_to_all x1, waiting for transfers between devices: 6.97 us -> 4.94 us  [local(): lax.all_to_all(q, PLANE, split_axis=0, concat_axis=0, tiled=True)]
    pallas_call x4 -> x5, Pallas kernels: 8.17 us -> 7.03 us  [the longest x1 2.37 us: expert_first(): pl.pallas_call(first_kernel, in_specs=[SCALARS] + [WHOLE] * 5 + [pl.Block...]
  transfers between devices with their start and end apart: 25 -> 22, of which waited for: 13 -> 11; matrix products, arithmetic and copies ran while one was open for 3% -> 3% of each run, Pallas kernels for 14% -> 13%
where the time goes in v4:
time: 144 us; the launch traced here: 143 us
  blocking collectives  59 us (41%)
  waiting for transfers between devices  26.3 us (18%)
  Pallas kernels  25.7 us (18%)
  starting transfers between devices  25.4 us (18%)
  other arithmetic  5.11 us (4%)
  local copies, waits for them, and re-layouts  1.63 us (1%)
    all_to_all x1, blocking collectives, local(): lax.all_to_all(sent, ALL, split_axis=0, concat_axis=0, tiled=True, axis_i...  15.6 us
    all_to_all x1, blocking collectives, local(): lax.all_to_all(out.reshape(16, 4, HALF), ALL, split_axis=0, concat_axis=0...  15.3 us
    all_to_all x1, blocking collectives, local(): lax.all_to_all(parts, ('z', 'y'), split_axis=0, concat_axis=0, tiled=True)  14.6 us
    ppermute x3, waiting for transfers between devices, local(): lax.ppermute(out[s], PLANE, line_shift(4 - s))  14.5 us
    all_to_all x1, blocking collectives, local(): lax.all_to_all(summed, ('z', 'y'), split_axis=0, concat_axis=0, tiled=True)  13.6 us
    ppermute x15, starting transfers between devices, swap(): return lax.ppermute(value, 'c', SWAP)  11.3 us
    all_to_all x1, starting transfers between devices, local(): lax.all_to_all(q, PLANE, split_axis=0, concat_axis=0, tiled=True)  8.68 us
    pallas_call x1, Pallas kernels, fetch(): pl.pallas_call(fetch_kernel, in_specs=[SCALARS] + [pl.BlockSpec(memory_sp...  7.07 us
  transfers between devices with their start and end apart: 22, of which 11 were waited for; matrix products, arithmetic and copies ran while one was open for 3% of the time, Pallas kernels for 13%

profile of v4, /device:TPU:1, one launch (start us, length us, event | category | flops | bytes accessed | tf_op | source)
XLA Modules:
  0.0 143.5 jit_solution(2489492749609531953)
XLA Ops:
  0.0 1.4 collective-permute-start.5
  1.4 1.6 %shard_map.136 = (bf16[32,2,4096]{2,1,0:T(2,128)(2,1)}, bf16[2,8192]{1,0:T(2,128)(2,1)S(1)}) custom-call(bf16[2,8192]{1,0:T(2,128)(2,1)} %q_ref.1, bf16[2,8192]{1,0:T(2,128)(2,1)} %hidden_ref.1), custom_call_target="tpu_custom_call" | custom-call | bytes 1048576 | tf_op jit(solution)/shard_map/pallas_call | solution.py:109
  3.1 0.1 collective-permute-start
  3.2 8.7 %all-to-all-start = ((bf16[32,2,4096]{2,1,0:T(2,128)(2,1)}), bf16[32,2,4096]{2,1,0:T(2,128)(2,1)S(1)}, u32[]{:S(2)}, u32[]{:S(2)}) async-start(bf16[32,2,4096]{2,1,0:T(2,128)(2,1)} %get-tuple-element.18), calls=%async_computation | async-start | bytes 1048576 | tf_op jit(solution)/shard_map/all_to_all | solution.py:395
  11.9 0.3 collective-permute-start.3
  12.2 0.3 collective-permute-start.1
  12.4 0.2 collective-permute-start.2
  12.7 0.7 dynamic-slice_convert_fusion.refs_1_
  13.4 0.7 subtract_bitcast_fusion.1
  14.1 1.5 %pad_maximum_fusion = bf16[64,2,2048]{2,1,0:T(2,128)(2,1)S(1)} fusion(bf16[64,2,1024]{2,1,0:T(2,128)(2,1)} %param.18, bf16[64,2,1024]{2,1,0:T(2,128)(2,1)} %param.17), kind=kLoop, calls=%fused_computation.3 | loop fusion | flops 1048576 | bytes 1048576 | tf_op jit(solution)/shard_map/concatenate | solution.py:396
  15.6 0.1 pad_add_fusion.1.refs_2_.at_ref
  15.7 0.1 copy.16
  15.8 0.2 reshape.89.sa_ref
  16.0 0.4 collective-permute-start.4
  16.4 0.2 copy-done.1
  16.6 1.2 collective-permute-done.4
  17.8 0.5 pad_maximum_fusion.1
  18.3 0.2 reshape.90.sb_ref
  18.5 4.9 %all-to-all-done = bf16[32,2,4096]{2,1,0:T(2,128)(2,1)S(1)} async-done(((bf16[32,2,4096]{2,1,0:T(2,128)(2,1)}), bf16[32,2,4096]{2,1,0:T(2,128)(2,1)S(1)}, u32[]{:S(2)}, u32[]{:S(2)}) %all-to-all-start) | async-done | bytes 524320 | tf_op jit(solution)/shard_map/all_to_all | solution.py:395
  23.4 0.2 reshape.88.q_ref
  23.7 6.9 %shard_map.137 = bf16[16,72,256]{2,1,0:T(8,128)(2,1)S(1)} custom-call(bf16[64,4096]{1,0:T(8,128)(2,1)S(1)} %reshape.88.q_ref, bf16[512,1024]{1,0:T(8,128)(2,1)} %ka_ref.1, bf16[512,1024]{1,0:T(8,128)(2,1)S(1)} %collective-permute-done.1.kb_ref, bf16[512,1024]{1,0:T(8,128)(2,1)} %va_ref.1, bf16[512,1024]{1,0:T(8,128)(2,1)} %collective-permute-done.2.vb_ref, ...), custom_call_target="tpu_custom_call" | custom-call | flops 1400000000 | bytes 6291456 | tf_op jit(solution)/shard_map/pallas_call | solution.py:174
  30.5 14.6 %all_to_all.25.got_ref = bf16[16,72,256]{2,1,0:T(8,128)(2,1)S(1)} all-to-all(bf16[16,72,256]{2,1,0:T(8,128)(2,1)S(1)} %shard_map.137), channel_id=1, replica_groups=mesh['x'=4,'z'=4,'y'=4,'c'=2] {'z','y'}, dimensions={0} | all-to-all | bytes 1179648 | tf_op jit(solution)/shard_map/all_to_all | solution.py:413
  45.2 1.4 shard_map.138
  46.6 1.8 %collective-permute-start.6 = (bf16[64,4096]{1,0:T(8,128)(2,1)S(1)}, bf16[64,4096]{1,0:T(8,128)(2,1)S(1)}, u32[]{:S(2)}, u32[]{:S(2)}) collective-permute-start(bf16[64,4096]{1,0:T(8,128)(2,1)S(1)} %get-tuple-element.20), channel_id=1, source_target_pairs={{0,1},{1,0},{2,3},{3,2},{4,5},{5,4},{6,7},{7,6},{8,9},{9,8},{10,11... | collective-permute-start | bytes 1572872 | tf_op jit(solution)/shard_map/ppermute | solution.py:359
  48.3 1.0 shard_map.139
  49.4 0.5 collective-permute-done.6
  49.9 0.1 add_convert_fusion.1
  50.0 0.2 reshape.91
  50.2 13.6 %all_to_all.26 = bf16[16,4,4096]{2,1,0:T(4,128)(2,1)S(1)} all-to-all(bf16[16,4,4096]{2,1,0:T(4,128)(2,1)S(1)} %reshape.91), channel_id=1, replica_groups=mesh['x'=4,'z'=4,'y'=4,'c'=2] {'z','y'}, dimensions={0} | all-to-all | bytes 1048576 | tf_op jit(solution)/shard_map/all_to_all | solution.py:418
  63.8 0.2 convert_reduce_fusion
  64.0 0.2 multiply_reduce_fusion
  64.2 1.8 %collective-permute-start.7 = (f32[4,1]{0,1:T(1,128)S(1)}, f32[4,1]{0,1:T(1,128)S(1)}, u32[]{:S(2)}, u32[]{:S(2)}) collective-permute-start(f32[4,1]{0,1:T(1,128)S(1)} %bitcast.20), channel_id=1, source_target_pairs={{0,1},{1,0},{2,3},{3,2},{4,5},{5,4},{6,7},{7,6},{8,9},{9,8},{10,11... | collective-permute-start | bytes 56 | tf_op jit(solution)/shard_map/ppermute | solution.py:359
  66.0 0.8 collective-permute-done.7
  66.8 0.1 multiply_convert_fusion
  66.9 0.2 broadcast_in_dim.26
  67.2 15.6 %all_to_all.27 = bf16[16,4,4096]{2,1,0:T(4,128)(2,1)S(1)} all-to-all(bf16[16,4,4096]{2,1,0:T(4,128)(2,1)S(1)} %broadcast_in_dim.26), channel_id=1, replica_groups={{0,32,64,96,8,40,72,104,16,48,80,112,24,56,88,120},{2,34,66,98,10,42,74..., dimensions={0} | all-to-all | bytes 1048576 | tf_op jit(solution)/shard_map/all_to_all | solution.py:425
  82.7 0.1 reshape.92.after_ref.p0
  82.8 0.6 collective-permute-start.9
  83.4 0.8 collective-permute-start.11
  84.2 1.7 %collective-permute-start.13 = (bf16[64,4096]{1,0:T(8,128)(2,1)S(1)}, bf16[64,4096]{1,0:T(8,128)(2,1)S(1)}, u32[]{:S(2)}, u32[]{:S(2)}) collective-permute-start(bf16[64,4096]{1,0:T(8,128)(2,1)S(1)} %reshape.92.after_ref.p0), channel_id=1, source_target_pairs={{0,6},{1,25},{2,0},{3,27},{4,2},{5,29},{6,4},{7,31},{8,14},{9,1},{... | collective-permute-start | bytes 1572872 | tf_op jit(solution)/shard_map/ppermute | solution.py:428
  85.9 0.1 fusion.1
  86.0 2.3 %collective-permute-start.15 = (f32[2,4]{1,0:T(2,128)S(1)}, f32[2,4]{1,0:T(2,128)S(1)}, u32[]{:S(2)}, u32[]{:S(2)}) collective-permute-start(f32[2,4]{1,0:T(2,128)S(1)} %fusion.1), channel_id=1, source_target_pairs={{0,1},{1,0},{2,3},{3,2},{4,5},{5,4},{6,7},{7,6},{8,9},{9,8},{10,11... | collective-permute-start | bytes 104 | tf_op jit(solution)/shard_map/ppermute | solution.py:359
  88.2 0.8 collective-permute-done.15
  89.0 0.4 collective-permute-start.8
  89.4 7.1 %shard_map.140 = (bf16[8192,768]{1,0:T(8,128)(2,1)S(1)}, bf16[768,4096]{1,0:T(8,128)(2,1)S(1)}) custom-call(s32[3]{0:T(128)S(1)} %pad_add_fusion.1.refs_2_.at_ref, bf16[64,4096]{1,0:T(8,128)(2,1)S(1)} %reshape.92.after_ref.p0, bf16[8192,384]{1,0:T(8,128)(2,1)} %bitcast.18, bf16[8192,384]{1,0:T(8,128)(2,1)} %bitcast.19, bf16[384,8192]{1,0:T(8,128)(2,1)} %bitcast.17, ...), custom_call_target="tpu_custom_call" | custom-call | bytes 23068672 | tf_op jit(solution)/shard_map/pallas_call | solution.py:78
  96.5 1.5 %collective-permute-done.9.p1 = bf16[64,4096]{1,0:T(8,128)(2,1)S(1)} collective-permute-done((bf16[64,4096]{1,0:T(8,128)(2,1)S(1)}, bf16[64,4096]{1,0:T(8,128)(2,1)S(1)}, u32[]{:S(2)}, u32[]{:S(2)}) %collective-permute-start.9) | collective-permute-done | bytes 524320 | tf_op jit(solution)/shard_map/ppermute | solution.py:428
  98.1 1.3 collective-permute-start.12
  99.4 2.4 %shard_map.141.acc_ref = f32[256,768]{1,0:T(8,128)S(1)} custom-call(s32[3]{0:T(128)S(1)} %pad_add_fusion.1.refs_2_.at_ref, bf16[64,4096]{1,0:T(8,128)(2,1)S(1)} %reshape.92.after_ref.p0, bf16[64,4096]{1,0:T(8,128)(2,1)S(1)} %collective-permute-done.9.p1, bf16[64,4096]{1,0:T(8,128)(2,1)S(1)} %collective-permute-done.11.p2, ...), custom_call_target="tpu_custom_call" | custom-call | flops 16000000000 | bytes 9437184 | tf_op jit(solution)/shard_map/pallas_call | solution.py:272
  101.8 2.4 %shard_map.142.inner_ref = bf16[256,384]{1,0:T(8,128)(2,1)S(1)} custom-call(s32[3]{0:T(128)S(1)} %pad_add_fusion.1.refs_2_.at_ref, bf16[64,4096]{1,0:T(8,128)(2,1)S(1)} %collective-permute-done.8.p0, bf16[64,4096]{1,0:T(8,128)(2,1)S(1)} %collective-permute-done.10.p1, bf16[64,4096]{1,0:T(8,128)(2,1)S(1)} %collective-permute-done.12.p2, ...), custom_call_target="tpu_custom_call" | custom-call | flops 1600000000 | bytes 9437184 | tf_op jit(solution)/shard_map/pallas_call | solution.py:294
  104.2 0.6 collective-permute-start.16
  104.8 1.1 collective-permute-done.16.other_ref
  105.9 2.4 %shard_map.143 = (bf16[64,4096]{1,0:T(8,128)(2,1)S(1)}, bf16[64,4096]{1,0:T(8,128)(2,1)S(1)}, bf16[64,4096]{1,0:T(8,128)(2,1)S(1)}, bf16[64,4096]{1,0:T(8,128)(2,1)S(1)}) custom-call(s32[3]{0:T(128)S(1)} %pad_add_fusion.1.refs_2_.at_ref, bf16[256,384]{1,0:T(8,128)(2,1)S(1)} %shard_map.142.inner_ref, bf16[256,384]{1,0:T(8,128)(2,1)S(1)} %collective-permute-done.16.other_ref, ...), custom_call_target="tpu_custom_call" | custom-call | flops 1600000000 | bytes 9437184 | tf_op jit(solution)/shard_map/pallas_call | solution.py:325
  108.2 1.4 %collective-permute-start.17 = (bf16[64,4096]{1,0:T(8,128)(2,1)S(1)}, bf16[64,4096]{1,0:T(8,128)(2,1)S(1)}, u32[]{:S(2)}, u32[]{:S(2)}) collective-permute-start(bf16[64,4096]{1,0:T(8,128)(2,1)S(1)} %get-tuple-element.24), channel_id=1, source_target_pairs={{0,6},{1,25},{2,0},{3,27},{4,2},{5,29},{6,4},{7,31},{8,14},{9,1},{... | collective-permute-start | bytes 1572872 | tf_op jit(solution)/shard_map/ppermute | solution.py:434
  109.7 0.9 collective-permute-start.18
  110.6 6.0 %collective-permute-done.17 = bf16[64,4096]{1,0:T(8,128)(2,1)S(1)} collective-permute-done((bf16[64,4096]{1,0:T(8,128)(2,1)S(1)}, bf16[64,4096]{1,0:T(8,128)(2,1)S(1)}, u32[]{:S(2)}, u32[]{:S(2)}) %collective-permute-start.17) | collective-permute-done | bytes 524320 | tf_op jit(solution)/shard_map/ppermute | solution.py:434
  116.6 2.9 %collective-permute-done.18 = bf16[64,4096]{1,0:T(8,128)(2,1)S(1)} collective-permute-done((bf16[64,4096]{1,0:T(8,128)(2,1)S(1)}, bf16[64,4096]{1,0:T(8,128)(2,1)S(1)}, u32[]{:S(2)}, u32[]{:S(2)}) %collective-permute-start.18) | collective-permute-done | bytes 524320 | tf_op jit(solution)/shard_map/ppermute | solution.py:434
  119.5 5.6 %collective-permute-done.19 = bf16[64,4096]{1,0:T(8,128)(2,1)S(1)} collective-permute-done((bf16[64,4096]{1,0:T(8,128)(2,1)S(1)}, bf16[64,4096]{1,0:T(8,128)(2,1)S(1)}, u32[]{:S(2)}, u32[]{:S(2)}) %collective-permute-start.19) | collective-permute-done | bytes 524320 | tf_op jit(solution)/shard_map/ppermute | solution.py:434
  125.1 0.3 add_convert_fusion
  125.4 0.2 reshape.93
  125.6 15.3 %all_to_all.28.got_ref = bf16[16,4,4096]{2,1,0:T(4,128)(2,1)S(1)} all-to-all(bf16[16,4,4096]{2,1,0:T(4,128)(2,1)S(1)} %reshape.93), channel_id=1, replica_groups={{0,32,64,96,8,40,72,104,16,48,80,112,24,56,88,120},{2,34,66,98,10,42,74..., dimensions={0} | all-to-all | bytes 1048576 | tf_op jit(solution)/shard_map/all_to_all | solution.py:436
  140.9 0.7 shard_map.144
  141.5 0.5 collective-permute-start.20
  142.0 0.8 collective-permute-done.20
  142.8 0.7 broadcast_select_fusion
  (29 shorter events, 0.2 us)
Async XLA Ops:
  0.0 45.2 %collective-permute-start.5 = (bf16[384,8192]{1,0:T(8,128)(2,1)}, bf16[384,8192]{1,0:T(8,128)(2,1)}, u32[]{:S(2)}, u32[]{:S(2)}) collective-permute-start(bf16[384,8192]{1,0:T(8,128)(2,1)} %bitcast.16), channel_id=1, source_target_pairs={{0,1},{1,0},{2,3},{3,2},{4,5},{5,4},{6,7},{7,6},{8,9},{9,8},{10,11... | collective-permute-start | bytes 18874376 | tf_op jit(solution)/shard_map/ppermute | solution.py:359
  3.1 12.9 %collective-permute-start = (bf16[2,4096]{1,0:T(2,128)(2,1)S(1)}, bf16[2,4096]{1,0:T(2,128)(2,1)S(1)}, u32[]{:S(2)}, u32[]{:S(2)}) collective-permute-start(bf16[2,4096]{1,0:T(2,128)(2,1)S(1)} %get-tuple-element.32), channel_id=1, source_target_pairs={{0,1},{1,0},{2,3},{3,2},{4,5},{5,4},{6,7},{7,6},{8,9},{9,8},{10,11... | collective-permute-start | bytes 49160 | tf_op jit(solution)/shard_map/ppermute | solution.py:359
  3.2 20.2 %all-to-all-start = ((bf16[32,2,4096]{2,1,0:T(2,128)(2,1)}), bf16[32,2,4096]{2,1,0:T(2,128)(2,1)S(1)}, u32[]{:S(2)}, u32[]{:S(2)}) async-start(bf16[32,2,4096]{2,1,0:T(2,128)(2,1)} %get-tuple-element.18), calls=%async_computation | async-start | bytes 1048576 | tf_op jit(solution)/shard_map/all_to_all | solution.py:395
  11.9 4.5 %collective-permute-start.3 = (bf16[64,2,1024]{2,1,0:T(2,128)(2,1)}, bf16[64,2,1024]{2,1,0:T(2,128)(2,1)S(1)}, u32[]{:S(2)}, u32[]{:S(2)}) collective-permute-start(bf16[64,2,1024]{2,1,0:T(2,128)(2,1)} %param.17), channel_id=1, source_target_pairs={{0,1},{1,0},{2,3},{3,2},{4,5},{5,4},{6,7},{7,6},{8,9},{9,8},{10,11... | collective-permute-start | bytes 786440 | tf_op jit(solution)/shard_map/ppermute | solution.py:359
  12.2 11.5 %collective-permute-start.1 = (bf16[512,1024]{1,0:T(8,128)(2,1)}, bf16[512,1024]{1,0:T(8,128)(2,1)S(1)}, u32[]{:S(2)}, u32[]{:S(2)}) collective-permute-start(bf16[512,1024]{1,0:T(8,128)(2,1)} %ka_ref.1), channel_id=1, source_target_pairs={{0,1},{1,0},{2,3},{3,2},{4,5},{5,4},{6,7},{7,6},{8,9},{9,8},{10,11... | collective-permute-start | bytes 3145736 | tf_op jit(solution)/shard_map/ppermute | solution.py:359
  12.4 11.2 %collective-permute-start.2 = (bf16[512,1024]{1,0:T(8,128)(2,1)}, bf16[512,1024]{1,0:T(8,128)(2,1)}, u32[]{:S(2)}, u32[]{:S(2)}) collective-permute-start(bf16[512,1024]{1,0:T(8,128)(2,1)} %va_ref.1), channel_id=1, source_target_pairs={{0,1},{1,0},{2,3},{3,2},{4,5},{5,4},{6,7},{7,6},{8,9},{9,8},{10,11... | collective-permute-start | bytes 3145736 | tf_op jit(solution)/shard_map/ppermute | solution.py:359
  16.0 0.6 copy-start.1
  16.0 1.8 %collective-permute-start.4 = (bf16[64,2,1024]{2,1,0:T(2,128)(2,1)}, bf16[64,2,1024]{2,1,0:T(2,128)(2,1)S(1)}, u32[]{:S(2)}, u32[]{:S(2)}) collective-permute-start(bf16[64,2,1024]{2,1,0:T(2,128)(2,1)} %param.18), channel_id=1, source_target_pairs={{0,1},{1,0},{2,3},{3,2},{4,5},{5,4},{6,7},{7,6},{8,9},{9,8},{10,11... | collective-permute-start | bytes 786440 | tf_op jit(solution)/shard_map/ppermute | solution.py:359
  23.6 21.6 %copy-start = (bf16[256,8192]{1,0:T(8,128)(2,1)S(1)}, bf16[256,8192]{1,0:T(8,128)(2,1)}, u32[]{:S(2)}) copy-start(bf16[256,8192]{1,0:T(8,128)(2,1)} %w_ref.3) | copy-start | bytes 12582916
  46.5 17.5 %copy-start.2 = (bf16[2,4096]{1,0:T(2,128)(2,1)S(1)}, bf16[2,4096]{1,0:T(2,128)(2,1)}, u32[]{:S(2)}) copy-start(bf16[2,4096]{1,0:T(2,128)(2,1)} %copy-done.1) | copy-start | bytes 49156
  46.5 39.3 %copy-start.3 = (f32[2,2]{1,0:T(2,128)S(1)}, f32[2,2]{1,0:T(2,128)}, u32[]{:S(2)}) copy-start(f32[2,2]{1,0:T(2,128)} %param.24) | copy-start | bytes 52
  46.6 39.3 %copy-start.4 = (s32[2,2]{1,0:T(2,128)S(1)}, s32[2,2]{1,0:T(2,128)}, u32[]{:S(2)}) copy-start(s32[2,2]{1,0:T(2,128)} %param.23) | copy-start | bytes 52
  46.6 3.3 %collective-permute-start.6 = (bf16[64,4096]{1,0:T(8,128)(2,1)S(1)}, bf16[64,4096]{1,0:T(8,128)(2,1)S(1)}, u32[]{:S(2)}, u32[]{:S(2)}) collective-permute-start(bf16[64,4096]{1,0:T(8,128)(2,1)S(1)} %get-tuple-element.20), channel_id=1, source_target_pairs={{0,1},{1,0},{2,3},{3,2},{4,5},{5,4},{6,7},{7,6},{8,9},{9,8},{10,11... | collective-permute-start | bytes 1572872 | tf_op jit(solution)/shard_map/ppermute | solution.py:359
  64.2 2.7 %collective-permute-start.7 = (f32[4,1]{0,1:T(1,128)S(1)}, f32[4,1]{0,1:T(1,128)S(1)}, u32[]{:S(2)}, u32[]{:S(2)}) collective-permute-start(f32[4,1]{0,1:T(1,128)S(1)} %bitcast.20), channel_id=1, source_target_pairs={{0,1},{1,0},{2,3},{3,2},{4,5},{5,4},{6,7},{7,6},{8,9},{9,8},{10,11... | collective-permute-start | bytes 56 | tf_op jit(solution)/shard_map/ppermute | solution.py:359
  82.8 15.2 %collective-permute-start.9 = (bf16[64,4096]{1,0:T(8,128)(2,1)S(1)}, bf16[64,4096]{1,0:T(8,128)(2,1)S(1)}, u32[]{:S(2)}, u32[]{:S(2)}) collective-permute-start(bf16[64,4096]{1,0:T(8,128)(2,1)S(1)} %reshape.92.after_ref.p0), channel_id=1, source_target_pairs={{0,2},{1,9},{2,4},{3,11},{4,6},{5,13},{6,0},{7,15},{8,10},{9,17},{... | collective-permute-start | bytes 1572872 | tf_op jit(solution)/shard_map/ppermute | solution.py:428
  83.4 14.7 %collective-permute-start.11 = (bf16[64,4096]{1,0:T(8,128)(2,1)S(1)}, bf16[64,4096]{1,0:T(8,128)(2,1)S(1)}, u32[]{:S(2)}, u32[]{:S(2)}) collective-permute-start(bf16[64,4096]{1,0:T(8,128)(2,1)S(1)} %reshape.92.after_ref.p0), channel_id=1, source_target_pairs={{0,4},{1,17},{2,6},{3,19},{4,0},{5,21},{6,2},{7,23},{8,12},{9,25},... | collective-permute-start | bytes 1572872 | tf_op jit(solution)/shard_map/ppermute | solution.py:428
  84.2 15.1 %collective-permute-start.13 = (bf16[64,4096]{1,0:T(8,128)(2,1)S(1)}, bf16[64,4096]{1,0:T(8,128)(2,1)S(1)}, u32[]{:S(2)}, u32[]{:S(2)}) collective-permute-start(bf16[64,4096]{1,0:T(8,128)(2,1)S(1)} %reshape.92.after_ref.p0), channel_id=1, source_target_pairs={{0,6},{1,25},{2,0},{3,27},{4,2},{5,29},{6,4},{7,31},{8,14},{9,1},{... | collective-permute-start | bytes 1572872 | tf_op jit(solution)/shard_map/ppermute | solution.py:428
  86.0 3.1 %collective-permute-start.15 = (f32[2,4]{1,0:T(2,128)S(1)}, f32[2,4]{1,0:T(2,128)S(1)}, u32[]{:S(2)}, u32[]{:S(2)}) collective-permute-start(f32[2,4]{1,0:T(2,128)S(1)} %fusion.1), channel_id=1, source_target_pairs={{0,1},{1,0},{2,3},{3,2},{4,5},{5,4},{6,7},{7,6},{8,9},{9,8},{10,11... | collective-permute-start | bytes 104 | tf_op jit(solution)/shard_map/ppermute | solution.py:359
  89.0 12.7 %collective-permute-start.8 = (bf16[64,4096]{1,0:T(8,128)(2,1)S(1)}, bf16[64,4096]{1,0:T(8,128)(2,1)S(1)}, u32[]{:S(2)}, u32[]{:S(2)}) collective-permute-start(bf16[64,4096]{1,0:T(8,128)(2,1)S(1)} %reshape.92.after_ref.p0), channel_id=1, source_target_pairs={{0,1},{1,0},{2,3},{3,2},{4,5},{5,4},{6,7},{7,6},{8,9},{9,8},{10,11... | collective-permute-start | bytes 1572872 | tf_op jit(solution)/shard_map/ppermute | solution.py:359
  98.1 3.7 %collective-permute-start.10 = (bf16[64,4096]{1,0:T(8,128)(2,1)S(1)}, bf16[64,4096]{1,0:T(8,128)(2,1)S(1)}, u32[]{:S(2)}, u32[]{:S(2)}) collective-permute-start(bf16[64,4096]{1,0:T(8,128)(2,1)S(1)} %collective-permute-done.9.p1), channel_id=1, source_target_pairs={{0,1},{1,0},{2,3},{3,2},{4,5},{5,4},{6,7},{7,6},{8,9},{9,8},{10,11... | collective-permute-start | bytes 1572872 | tf_op jit(solution)/shard_map/ppermute | solution.py:359
  98.1 3.7 %collective-permute-start.12 = (bf16[64,4096]{1,0:T(8,128)(2,1)S(1)}, bf16[64,4096]{1,0:T(8,128)(2,1)S(1)}, u32[]{:S(2)}, u32[]{:S(2)}) collective-permute-start(bf16[64,4096]{1,0:T(8,128)(2,1)S(1)} %collective-permute-done.11.p2), channel_id=1, source_target_pairs={{0,1},{1,0},{2,3},{3,2},{4,5},{5,4},{6,7},{7,6},{8,9},{9,8},{10,11... | collective-permute-start | bytes 1572872 | tf_op jit(solution)/shard_map/ppermute | solution.py:359
  99.4 2.4 %collective-permute-start.14 = (bf16[64,4096]{1,0:T(8,128)(2,1)S(1)}, bf16[64,4096]{1,0:T(8,128)(2,1)S(1)}, u32[]{:S(2)}, u32[]{:S(2)}) collective-permute-start(bf16[64,4096]{1,0:T(8,128)(2,1)S(1)} %collective-permute-done.13.p3), channel_id=1, source_target_pairs={{0,1},{1,0},{2,3},{3,2},{4,5},{5,4},{6,7},{7,6},{8,9},{9,8},{10,11... | collective-permute-start | bytes 1572872 | tf_op jit(solution)/shard_map/ppermute | solution.py:359
  104.2 1.6 %collective-permute-start.16 = (bf16[256,384]{1,0:T(8,128)(2,1)S(1)}, bf16[256,384]{1,0:T(8,128)(2,1)S(1)}, u32[]{:S(2)}, u32[]{:S(2)}) collective-permute-start(bf16[256,384]{1,0:T(8,128)(2,1)S(1)} %shard_map.142.inner_ref), channel_id=1, source_target_pairs={{0,1},{1,0},{2,3},{3,2},{4,5},{5,4},{6,7},{7,6},{8,9},{9,8},{10,11... | collective-permute-start | bytes 589832 | tf_op jit(solution)/shard_map/ppermute | solution.py:359
  108.2 8.4 %collective-permute-start.17 = (bf16[64,4096]{1,0:T(8,128)(2,1)S(1)}, bf16[64,4096]{1,0:T(8,128)(2,1)S(1)}, u32[]{:S(2)}, u32[]{:S(2)}) collective-permute-start(bf16[64,4096]{1,0:T(8,128)(2,1)S(1)} %get-tuple-element.24), channel_id=1, source_target_pairs={{0,6},{1,25},{2,0},{3,27},{4,2},{5,29},{6,4},{7,31},{8,14},{9,1},{... | collective-permute-start | bytes 1572872 | tf_op jit(solution)/shard_map/ppermute | solution.py:434
  109.7 9.9 %collective-permute-start.18 = (bf16[64,4096]{1,0:T(8,128)(2,1)S(1)}, bf16[64,4096]{1,0:T(8,128)(2,1)S(1)}, u32[]{:S(2)}, u32[]{:S(2)}) collective-permute-start(bf16[64,4096]{1,0:T(8,128)(2,1)S(1)} %get-tuple-element.25), channel_id=1, source_target_pairs={{0,4},{1,17},{2,6},{3,19},{4,0},{5,21},{6,2},{7,23},{8,12},{9,25},... | collective-permute-start | bytes 1572872 | tf_op jit(solution)/shard_map/ppermute | solution.py:434
  110.6 14.5 %collective-permute-start.19 = (bf16[64,4096]{1,0:T(8,128)(2,1)S(1)}, bf16[64,4096]{1,0:T(8,128)(2,1)S(1)}, u32[]{:S(2)}, u32[]{:S(2)}) collective-permute-start(bf16[64,4096]{1,0:T(8,128)(2,1)S(1)} %get-tuple-element.26), channel_id=1, source_target_pairs={{0,2},{1,9},{2,4},{3,11},{4,6},{5,13},{6,0},{7,15},{8,10},{9,17},{... | collective-permute-start | bytes 1572872 | tf_op jit(solution)/shard_map/ppermute | solution.py:434
  141.5 1.3 collective-permute-start.20

commit v5 on v4

--- a/solution.py
+++ b/solution.py
@@ -94,8 +94,7 @@
     return pltpu.with_memory_space_constraint(array, pltpu.HBM)
 
 
-def spread_kernel(q_ref, hidden_ref, out_ref, copy_ref):
-    copy_ref[...] = hidden_ref[...]
+def spread_kernel(q_ref, out_ref):
     for half in range(2):
         value = jnp.concatenate(
             [q_ref[:, (2 * k + half) * 2 * HD : (2 * k + half + 1) * 2 * HD] for k in range(16)], axis=1
@@ -104,17 +103,33 @@
             out_ref[2 * chip + half] = value
 
 
-def spread(queries, hidden):
-    whole = pl.BlockSpec((2, D), lambda i: (0, 0))
+def spread(queries):
     return pl.pallas_call(
         spread_kernel,
         grid=(1,),
-        in_specs=[whole] * 2,
-        out_specs=[pl.BlockSpec((32, 2, HALF), lambda i: (0, 0, 0)), whole],
-        out_shape=[jax.ShapeDtypeStruct((32, 2, HALF), BF), jax.ShapeDtypeStruct((2, D), BF)],
+        in_specs=[pl.BlockSpec((2, D), lambda i: (0, 0))],
+        out_specs=pl.BlockSpec((32, 2, HALF), lambda i: (0, 0, 0)),
+        out_shape=jax.ShapeDtypeStruct((32, 2, HALF), BF),
         compiler_params=pltpu.CompilerParams(vmem_limit_bytes=4 * MB),
         cost_estimate=pl.CostEstimate(flops=0, bytes_accessed=MB, transcendentals=0),
-    )(in_hbm(queries), in_hbm(hidden))
+    )(in_hbm(queries))
+
+
+def widen_kernel(gain_ref, out_ref):
+    out_ref[...] = gain_ref[...].astype(F32)
+
+
+def widen(gain):
+    whole = pl.BlockSpec((1, D), lambda i: (0, 0))
+    return pl.pallas_call(
+        widen_kernel,
+        grid=(1,),
+        in_specs=[whole],
+        out_specs=whole,
+        out_shape=jax.ShapeDtypeStruct((1, D), F32),
+        compiler_params=pltpu.CompilerParams(vmem_limit_bytes=4 * MB),
+        cost_estimate=pl.CostEstimate(flops=20000000000, bytes_accessed=MB, transcendentals=0),
+    )(gain)
 
 
 def store_part(out_ref, first, acc, top, total):
@@ -183,14 +198,19 @@
     )(q, in_hbm(ka), kb, in_hbm(va), vb, sa, sb, left, *early)
 
 
-def half_product(attended, w_ref, half, out_ref):
+def half_product(attended, w_ref, half, hidden_ref, first, out_ref):
     width = HALF // 4
+    line = lax.broadcasted_iota(jnp.int32, (out_ref.shape[0], 1), 0)
+    picks = [(line == first + i).astype(F32) for i in range(2)]
     for part in range(4):
         cols = pl.ds(pl.multiple_of(half * HALF + part * width, width), width)
-        out_ref[:, part * width : (part + 1) * width] = dot(attended, w_ref[:, cols]).astype(BF)
-
-
-def project_kernel(at_ref, got_ref, w_ref, early_ref, out_ref, att_ref):
+        value = dot(attended, w_ref[:, cols])
+        hidden = hidden_ref[:, cols].astype(F32)
+        value = value + picks[0] * hidden[0:1] + picks[1] * hidden[1:2]
+        out_ref[:, part * width : (part + 1) * width] = value.astype(BF)
+
+
+def project_kernel(at_ref, got_ref, w_ref, hidden_ref, out_ref, att_ref):
     rows = 64
     tops = [got_ref[s, rows : rows + 1, 0 : 2 * rows].astype(F32) for s in range(16)]
     sums = [
@@ -210,33 +230,51 @@
             share = jnp.sum(jnp.where(here, factors[s] / total, 0.0), axis=1, keepdims=True)
             acc = acc + got_ref[s, 0:rows, j * HD : (j + 1) * HD].astype(F32) * share
         att_ref[:, j * HD : (j + 1) * HD] = acc.astype(BF)
-    half_product(att_ref[...], w_ref, 1 - at_ref[0], out_ref)
-
-
-def project_other(at, got, w_out, early):
+    half_product(att_ref[...], w_ref, 1 - at_ref[0], hidden_ref, at_ref[3], out_ref)
+
+
+def project_other(at, got, w_out, hidden):
     return pl.pallas_call(
         project_kernel,
-        in_specs=[SCALARS, WHOLE, WHOLE, pl.BlockSpec(memory_space=pl.ANY)],
+        in_specs=[SCALARS] + [WHOLE] * 3,
         out_specs=[WHOLE] * 2,
         out_shape=[jax.ShapeDtypeStruct((64, HALF), BF), jax.ShapeDtypeStruct((64, 256), BF)],
         compiler_params=pltpu.CompilerParams(vmem_limit_bytes=16 * MB),
         cost_estimate=pl.CostEstimate(flops=140000000, bytes_accessed=3 * MB, transcendentals=0),
-    )(at, got, in_vmem(w_out), in_hbm(early))
-
-
-def project_mine_kernel(at_ref, att_ref, w_ref, out_ref):
-    half_product(att_ref[...], w_ref, at_ref[0], out_ref)
-
-
-def project_mine(at, attended, w_out):
+    )(at, got, in_vmem(w_out), in_vmem(hidden))
+
+
+def project_mine_kernel(at_ref, att_ref, w_ref, hidden_ref, out_ref):
+    half_product(att_ref[...], w_ref, at_ref[0], hidden_ref, at_ref[3], out_ref)
+
+
+def project_mine(at, attended, w_out, hidden):
     return pl.pallas_call(
         project_mine_kernel,
-        in_specs=[SCALARS, WHOLE, WHOLE],
+        in_specs=[SCALARS] + [WHOLE] * 3,
         out_specs=WHOLE,
         out_shape=jax.ShapeDtypeStruct((64, HALF), BF),
         compiler_params=pltpu.CompilerParams(vmem_limit_bytes=16 * MB),
         cost_estimate=pl.CostEstimate(flops=140000000, bytes_accessed=3 * MB, transcendentals=0),
-    )(at, attended, in_vmem(w_out))
+    )(at, attended, in_vmem(w_out), in_vmem(hidden))
+
+
+def settle_kernel(got_ref, early_ref, residual_ref, sent_ref):
+    residual = functools.reduce(jnp.add, [got_ref[i].astype(F32) for i in range(16)])
+    residual_ref[...] = residual
+    for i in range(16):
+        sent_ref[i] = residual.astype(BF)
+
+
+def settle(got, early):
+    return pl.pallas_call(
+        settle_kernel,
+        in_specs=[WHOLE, pl.BlockSpec(memory_space=pl.ANY)],
+        out_specs=[WHOLE] * 2,
+        out_shape=[jax.ShapeDtypeStruct((4, HALF), F32), jax.ShapeDtypeStruct((16, 4, HALF), BF)],
+        compiler_params=pltpu.CompilerParams(vmem_limit_bytes=8 * MB),
+        cost_estimate=pl.CostEstimate(flops=1000000, bytes_accessed=MB, transcendentals=0),
+    )(got, in_hbm(early))
 
 
 def rolled(place, back):
@@ -251,86 +289,109 @@
             x_ref[line : line + 16, :] = pieces[piece][pl.ds(rolled(place, back), 16), :]
 
 
-def multiplied(x_ref, w_ref, half, acc_ref):
+def multiplied(x_ref, gain_ref, w_ref, half, acc_ref):
     width = HALF // 4
+    square = 0.0
     for part in range(4):
         rows = pl.ds(pl.multiple_of(half * HALF + part * width, width), width)
-        value = dot(x_ref[:, part * width : (part + 1) * width], w_ref[rows, :])
+        x = x_ref[:, part * width : (part + 1) * width].astype(F32)
+        square = square + jnp.sum(x * x, axis=1, keepdims=True)
+        value = dot((x * gain_ref[:, rows]).astype(BF), w_ref[rows, :])
         if part == 0:
             acc_ref[...] = value
         else:
             acc_ref[...] += value
-
-
-def first_kernel(at_ref, p0, p1, p2, p3, w_ref, early_ref, acc_ref, x_ref):
+    return square
+
+
+def first_kernel(at_ref, p0, p1, p2, p3, w_ref, gain_ref, early_ref, acc_ref, square_ref, x_ref):
     gathered(x_ref, (p0, p1, p2, p3), at_ref[1], True)
-    multiplied(x_ref, w_ref, at_ref[0], acc_ref)
-
-
-def expert_first(at, pieces, gate_up, early):
+    square = multiplied(x_ref, gain_ref, w_ref, at_ref[0], acc_ref)
+    square_ref[...] = jnp.broadcast_to(square, square_ref.shape)
+
+
+def expert_first(at, pieces, gate_up, gain, early):
     units = gate_up.shape[1]
     return pl.pallas_call(
         first_kernel,
-        in_specs=[SCALARS] + [WHOLE] * 5 + [pl.BlockSpec(memory_space=pl.ANY)],
-        out_specs=WHOLE,
-        out_shape=jax.ShapeDtypeStruct((256, units), F32),
+        in_specs=[SCALARS] + [WHOLE] * 6 + [pl.BlockSpec(memory_space=pl.ANY)],
+        out_specs=[WHOLE] * 2,
+        out_shape=[jax.ShapeDtypeStruct((256, units), F32), jax.ShapeDtypeStruct((256, HD), F32)],
         scratch_shapes=[pltpu.VMEM((256, HALF), BF)],
         compiler_params=pltpu.CompilerParams(vmem_limit_bytes=12 * MB),
         cost_estimate=pl.CostEstimate(flops=16000000000, bytes_accessed=9 * MB, transcendentals=0),
-    )(at, *pieces, in_vmem(gate_up), early)
-
-
-def second_kernel(at_ref, p0, p1, p2, p3, w_ref, acc_ref, inner_ref, x_ref, more_ref):
+    )(at, *pieces, in_vmem(gate_up), gain, early)
+
+
+def second_kernel(at_ref, p0, p1, p2, p3, w_ref, gain_ref, acc_ref, square_ref, inner_ref, x_ref, more_ref):
     units = inner_ref.shape[1]
     gathered(x_ref, (p0, p1, p2, p3), at_ref[2], False)
-    multiplied(x_ref, w_ref, 1 - at_ref[0], more_ref)
-    gate = acc_ref[:, :units] + more_ref[:, :units]
-    up = acc_ref[:, units:] + more_ref[:, units:]
+    square = square_ref[:, 0:1] + multiplied(x_ref, gain_ref, w_ref, 1 - at_ref[0], more_ref)
+    scale = lax.rsqrt(square * (1.0 / D) + EPS)
+    gate = (acc_ref[:, :units] + more_ref[:, :units]) * scale
+    up = (acc_ref[:, units:] + more_ref[:, units:]) * scale
     inner_ref[...] = (gate / (1.0 + jnp.exp(-gate)) * up).astype(BF)
 
 
-def expert_second(at, pieces, gate_up, acc):
+def expert_second(at, pieces, gate_up, gain, acc, square):
     units = gate_up.shape[1]
     return pl.pallas_call(
         second_kernel,
-        in_specs=[SCALARS] + [WHOLE] * 6,
+        in_specs=[SCALARS] + [WHOLE] * 8,
         out_specs=WHOLE,
         out_shape=jax.ShapeDtypeStruct((256, units // 2), BF),
         scratch_shapes=[pltpu.VMEM((256, HALF), BF), pltpu.VMEM((256, units), F32)],
         compiler_params=pltpu.CompilerParams(vmem_limit_bytes=12 * MB),
         cost_estimate=pl.CostEstimate(flops=1600000000, bytes_accessed=9 * MB, transcendentals=0),
-    )(at, *pieces, in_vmem(gate_up), acc)
-
-
-def third_kernel(at_ref, inner_ref, other_ref, w_ref, o0, o1, o2, o3, x_ref):
+    )(at, *pieces, in_vmem(gate_up), gain, acc, square)
+
+
+def third_kernel(inner_ref, w_ref, out_ref):
     units = inner_ref.shape[1]
-    x_ref[:, :units] = inner_ref[...]
+    width = HALF // 4
+    for part in range(4):
+        cols = slice(part * width, (part + 1) * width)
+        out_ref[:, cols] = dot(inner_ref[...], w_ref[:units, cols])
+
+
+def expert_third(inner, down):
+    return pl.pallas_call(
+        third_kernel,
+        in_specs=[WHOLE] * 2,
+        out_specs=WHOLE,
+        out_shape=jax.ShapeDtypeStruct((inner.shape[0], HALF), F32),
+        compiler_params=pltpu.CompilerParams(vmem_limit_bytes=12 * MB),
+        cost_estimate=pl.CostEstimate(flops=8000000000, bytes_accessed=9 * MB, transcendentals=0),
+    )(inner, in_vmem(down))
+
+
+def fourth_kernel(at_ref, other_ref, w_ref, half_ref, o0, o1, o2, o3, x_ref):
+    units = other_ref.shape[1]
     for a in range(4):
         for b in range(4):
             line, line_b = (4 * a + b) * 16, (4 * b + a) * 16
-            x_ref[line : line + 16, units:] = other_ref[line_b : line_b + 16, :]
+            x_ref[line : line + 16, :] = other_ref[line_b : line_b + 16, :]
     outs = (o0, o1, o2, o3)
     width = HALF // 4
     for part in range(4):
         cols = slice(part * width, (part + 1) * width)
-        value = dot(x_ref[...], w_ref[:, cols]).astype(BF)
+        value = (half_ref[:, cols] + dot(x_ref[...], w_ref[units:, cols])).astype(BF)
         for a in range(4):
             for b in range(4):
                 line = (4 * a + b) * 16
                 outs[a][pl.ds(rolled(at_ref[1], b), 16), cols] = value[line : line + 16]
 
 
-def expert_third(at, inner, other, down):
-    units = inner.shape[1]
-    return pl.pallas_call(
-        third_kernel,
+def expert_fourth(at, other, down, half):
+    return pl.pallas_call(
+        fourth_kernel,
         in_specs=[SCALARS] + [WHOLE] * 3,
         out_specs=[WHOLE] * 4,
         out_shape=[jax.ShapeDtypeStruct((64, HALF), BF)] * 4,
-        scratch_shapes=[pltpu.VMEM((256, 2 * units), BF)],
+        scratch_shapes=[pltpu.VMEM(other.shape, BF)],
         compiler_params=pltpu.CompilerParams(vmem_limit_bytes=12 * MB),
-        cost_estimate=pl.CostEstimate(flops=1600000000, bytes_accessed=9 * MB, transcendentals=0),
-    )(at, inner, other, in_vmem(down))
+        cost_estimate=pl.CostEstimate(flops=800000000, bytes_accessed=9 * MB, transcendentals=0),
+    )(at, other, in_vmem(down), half)
 
 
 def mix_kernel(at_ref, got_ref, residual_ref, weights_ref, kept_ref, sent_ref):
@@ -379,14 +440,14 @@
     z = lax.axis_index("z").astype(jnp.int32)
     y = lax.axis_index("y").astype(jnp.int32)
     chip = 4 * z + y
-    at = jnp.stack([c, jnp.where(c == 0, z, y), jnp.where(c == 0, y, z)])
+    at = jnp.stack([c, jnp.where(c == 0, z, y), jnp.where(c == 0, y, z), 4 * chip + 2 * c])
 
     def in_order(own, got, axis):
         return jnp.where(
             c == 0, jnp.concatenate([own, got], axis=axis), jnp.concatenate([got, own], axis=axis)
         )
 
-    q, hidden_in = spread(queries, hidden_in)
+    q = spread(queries)
     keys_b = swap(prefix_keys)
     values_b = swap(prefix_values)
     suffix_keys_b = swap(suffix_keys)
@@ -398,39 +459,30 @@
     first = 4 * chip
     left = jnp.stack([suffix_lengths - (first + 2 * c), suffix_lengths - (first + 2 * (1 - c))], axis=1)
     left = jnp.tile(left.astype(jnp.int32), (4, 1))
-    hidden = in_order(
-        lax.dynamic_slice_in_dim(hidden_in, c * HALF, HALF, 1),
-        swap(lax.dynamic_slice_in_dim(hidden_in, (1 - c) * HALF, HALF, 1)),
-        0,
-    ).astype(F32)
     match = expert_ids[:, :, None] == jnp.arange(4, dtype=jnp.int32)[None, None, :]
     weights = jnp.sum(jnp.where(match, expert_weights[:, :, None], 0.0), axis=1)
     weights = in_order(weights, swap(weights), 0)
-    gain = lax.dynamic_slice_in_dim(norm_gain, c * HALF, HALF, 0).astype(F32)
-
-    early = (hidden, gain, at)
+    gain = widen(norm_gain.reshape(1, D))
+    early = (gain, at)
     parts = attend(q, prefix_keys, keys_b, prefix_values, values_b, suffix, suffix_b, left, early)
     parts = lax.all_to_all(parts, ("z", "y"), split_axis=0, concat_axis=0, tiled=True)
-    other, attended = project_other(at, parts, w_out, w_down_b)
+    other, attended = project_other(at, parts, w_out, hidden_in)
     other = swap(other)
-    mine = project_mine(at, attended, w_out)
+    mine = project_mine(at, attended, w_out, hidden_in)
     summed = (mine.astype(F32) + other.astype(F32)).astype(BF).reshape(16, 4, HALF)
     summed = lax.all_to_all(summed, ("z", "y"), split_axis=0, concat_axis=0, tiled=True)
-    residual = hidden + jnp.sum(summed.astype(F32), axis=0)
-    square = jnp.sum(residual * residual, axis=-1, keepdims=True)
-    mean_square = (square + swap(square)) * (1.0 / D)
-    normed = (residual * lax.rsqrt(mean_square + EPS) * gain).astype(BF)
+    residual, sent = settle(summed, w_down_b)
     wide = wide_groups()
-    sent = jnp.broadcast_to(normed[None], (16, 4, HALF))
     own = lax.all_to_all(
         sent, ALL, split_axis=0, concat_axis=0, tiled=True, axis_index_groups=wide
     ).reshape(64, HALF)
     pieces = [own] + [lax.ppermute(own, PLANE, line_shift(s)) for s in (1, 2, 3)]
     gate_up, down = fetch(at, own, w_gate[0], w_up[0], w_down[0], w_down_b)
     pieces_b = [swap(piece) for piece in pieces]
-    acc = expert_first(at, pieces, gate_up, weights)
-    inner = expert_second(at, pieces_b, gate_up, acc)
-    out = expert_third(at, inner, swap(inner), down)
+    acc, square = expert_first(at, pieces, gate_up, gain, weights)
+    inner = expert_second(at, pieces_b, gate_up, gain, acc, square)
+    other = swap(inner)
+    out = expert_fourth(at, other, down, expert_third(inner, down))
     out = [out[0]] + [lax.ppermute(out[s], PLANE, line_shift(4 - s)) for s in (1, 2, 3)]
     out = functools.reduce(jnp.add, [piece.astype(F32) for piece in out]).astype(BF)
     out = lax.all_to_all(

time: 144 us -> 141 us (0.979)
  waiting for transfers between devices: 26.3 us -> 23.1 us
  starting transfers between devices: 25.4 us -> 23.3 us
  other arithmetic: 5.11 us -> 3.11 us
  blocking collectives: 59 us -> 60.6 us
    ppermute x15 -> x13, waiting for transfers between devices: 5.31 us -> 2.29 us  [swap(): return lax.ppermute(value, 'c', SWAP)]
    all_to_all x1, waiting for transfers between devices: 4.94 us -> 6.77 us  [local(): lax.all_to_all(q, PLANE, split_axis=0, concat_axis=0, tiled=True)]
    pallas_call x6 -> x9, Pallas kernels: 11.1 us -> 12.4 us  [the longest x1 2.62 us: expert_second(): pl.pallas_call(second_kernel, in_specs=[SCALARS] + [WHOLE] * 8, out_specs...]
    ppermute x15 -> x13, starting transfers between devices: 11.3 us -> 10.9 us  [swap(): return lax.ppermute(value, 'c', SWAP)]
  transfers between devices with their start and end apart: 22 -> 20, of which waited for: 11 -> 9; matrix products, arithmetic and copies ran while one was open for 3% -> 3% of each run, Pallas kernels for 13% -> 16%
where the time goes in v5:
time: 141 us; the launch traced here: 140 us
  blocking collectives  60.6 us (43%)
  Pallas kernels  27 us (19%)
  starting transfers between devices  23.3 us (17%)
  waiting for transfers between devices  23.1 us (16%)
  other arithmetic  3.11 us (2%)
  local copies, waits for them, and re-layouts  2.85 us (2%)
    all_to_all x1, blocking collectives, local(): lax.all_to_all(sent, ALL, split_axis=0, concat_axis=0, tiled=True, axis_i...  16.7 us
    all_to_all x1, blocking collectives, local(): lax.all_to_all(out.reshape(16, 4, HALF), ALL, split_axis=0, concat_axis=0...  15.7 us
    all_to_all x1, blocking collectives, local(): lax.all_to_all(parts, ('z', 'y'), split_axis=0, concat_axis=0, tiled=True)  14.6 us
    ppermute x3, waiting for transfers between devices, local(): lax.ppermute(out[s], PLANE, line_shift(4 - s))  13.6 us
    all_to_all x1, blocking collectives, local(): lax.all_to_all(summed, ('z', 'y'), split_axis=0, concat_axis=0, tiled=True)  13.6 us
    ppermute x13, starting transfers between devices, swap(): return lax.ppermute(value, 'c', SWAP)  10.9 us
    all_to_all x1, starting transfers between devices, local(): lax.all_to_all(q, PLANE, split_axis=0, concat_axis=0, tiled=True)  8.3 us
    pallas_call x1, Pallas kernels, fetch(): pl.pallas_call(fetch_kernel, in_specs=[SCALARS] + [pl.BlockSpec(memory_sp...  7.07 us
  transfers between devices with their start and end apart: 20, of which 9 were waited for; matrix products, arithmetic and copies ran while one was open for 3% of the time, Pallas kernels for 16%

profile of v5, /device:TPU:1, one launch (start us, length us, event | category | flops | bytes accessed | tf_op | source)
XLA Modules:
  0.0 140.3 jit_solution(5720765605698672982)
XLA Ops:
  0.0 1.4 %collective-permute-start.5 = (bf16[384,8192]{1,0:T(8,128)(2,1)}, bf16[384,8192]{1,0:T(8,128)(2,1)}, u32[]{:S(2)}, u32[]{:S(2)}) collective-permute-start(bf16[384,8192]{1,0:T(8,128)(2,1)} %bitcast.13), channel_id=1, source_target_pairs={{0,1},{1,0},{2,3},{3,2},{4,5},{5,4},{6,7},{7,6},{8,9},{9,8},{10,11... | collective-permute-start | bytes 18874376 | tf_op jit(solution)/shard_map/ppermute | solution.py:420
  1.4 0.5 collective-permute-start.3
  1.9 1.6 %shard_map.136 = bf16[32,2,4096]{2,1,0:T(2,128)(2,1)} custom-call(bf16[2,8192]{1,0:T(2,128)(2,1)} %q_ref.1), custom_call_target="tpu_custom_call" | custom-call | bytes 1048576 | tf_op jit(solution)/shard_map/pallas_call | solution.py:107
  3.6 8.3 %all-to-all-start = ((bf16[32,2,4096]{2,1,0:T(2,128)(2,1)}), bf16[32,2,4096]{2,1,0:T(2,128)(2,1)S(1)}, u32[]{:S(2)}, u32[]{:S(2)}) async-start(bf16[32,2,4096]{2,1,0:T(2,128)(2,1)} %shard_map.136), calls=%async_computation | async-start | bytes 1048576 | tf_op jit(solution)/shard_map/all_to_all | solution.py:456
  11.9 0.3 collective-permute-start
  12.2 0.3 collective-permute-start.1
  12.5 0.7 reshape.30.gain_ref
  13.2 0.0 copy-start.6
  13.2 0.0 copy-start.3
  13.3 0.6 copy-done.6
  13.9 0.1 copy.16
  14.0 0.2 copy-done.2
  14.2 0.1 copy-done.3
  14.3 0.5 pad_maximum_fusion
  14.7 0.2 reshape.28.sa_ref
  14.9 0.1 pad_add_fusion.1.refs_1_.at_ref
  15.0 1.4 %pad_maximum_fusion.1 = bf16[64,2,2048]{2,1,0:T(2,128)(2,1)S(1)} fusion(bf16[64,2,1024]{2,1,0:T(2,128)(2,1)} %collective-permute-done.3, bf16[64,2,1024]{2,1,0:T(2,128)(2,1)S(1)} %collective-permute-done.2), kind=kLoop, calls=%fused_computation.3 | loop fusion | flops 1048576 | bytes 1048576 | tf_op jit(solution)/shard_map/concatenate | solution.py:458
  16.5 0.2 reshape.29.sb_ref
  16.7 6.8 %all-to-all-done = bf16[32,2,4096]{2,1,0:T(2,128)(2,1)S(1)} async-done(((bf16[32,2,4096]{2,1,0:T(2,128)(2,1)}), bf16[32,2,4096]{2,1,0:T(2,128)(2,1)S(1)}, u32[]{:S(2)}, u32[]{:S(2)}) %all-to-all-start) | async-done | bytes 524320 | tf_op jit(solution)/shard_map/all_to_all | solution.py:456
  23.4 0.2 reshape.27.q_ref
  23.7 6.9 %shard_map.138 = bf16[16,72,256]{2,1,0:T(8,128)(2,1)S(1)} custom-call(bf16[64,4096]{1,0:T(8,128)(2,1)S(1)} %reshape.27.q_ref, bf16[512,1024]{1,0:T(8,128)(2,1)} %ka_ref.1, bf16[512,1024]{1,0:T(8,128)(2,1)S(1)} %collective-permute-done.kb_ref, bf16[512,1024]{1,0:T(8,128)(2,1)} %va_ref.1, bf16[512,1024]{1,0:T(8,128)(2,1)} %collective-permute-done.1.vb_ref, ...), custom_call_target="tpu_custom_call" | custom-call | flops 1400000000 | bytes 6291456 | tf_op jit(solution)/shard_map/pallas_call | solution.py:189
  30.6 14.6 %all_to_all.25.got_ref = bf16[16,72,256]{2,1,0:T(8,128)(2,1)S(1)} all-to-all(bf16[16,72,256]{2,1,0:T(8,128)(2,1)S(1)} %shard_map.138), channel_id=1, replica_groups=mesh['x'=4,'z'=4,'y'=4,'c'=2] {'z','y'}, dimensions={0} | all-to-all | bytes 1179648 | tf_op jit(solution)/shard_map/all_to_all | solution.py:468
  45.2 1.4 shard_map.139
  46.6 1.8 %collective-permute-start.4 = (bf16[64,4096]{1,0:T(8,128)(2,1)S(1)}, bf16[64,4096]{1,0:T(8,128)(2,1)S(1)}, u32[]{:S(2)}, u32[]{:S(2)}) collective-permute-start(bf16[64,4096]{1,0:T(8,128)(2,1)S(1)} %get-tuple-element.20), channel_id=1, source_target_pairs={{0,1},{1,0},{2,3},{3,2},{4,5},{5,4},{6,7},{7,6},{8,9},{9,8},{10,11... | collective-permute-start | bytes 1572872 | tf_op jit(solution)/shard_map/ppermute | solution.py:420
  48.3 1.1 shard_map.140
  49.4 0.0 copy-start.4
  49.4 0.0 copy-start.5
  49.4 0.5 collective-permute-done.4
  49.9 0.1 add_convert_fusion.1
  50.0 0.2 reshape.31
  50.2 13.6 %all_to_all.26.got_ref = bf16[16,4,4096]{2,1,0:T(4,128)(2,1)S(1)} all-to-all(bf16[16,4,4096]{2,1,0:T(4,128)(2,1)S(1)} %reshape.31), channel_id=1, replica_groups=mesh['x'=4,'z'=4,'y'=4,'c'=2] {'z','y'}, dimensions={0} | all-to-all | bytes 1048576 | tf_op jit(solution)/shard_map/all_to_all | solution.py:473
  63.8 0.1 shard_map.141
  63.9 16.7 %all_to_all.27 = bf16[16,4,4096]{2,1,0:T(4,128)(2,1)S(1)} all-to-all(bf16[16,4,4096]{2,1,0:T(4,128)(2,1)S(1)} %get-tuple-element.21), channel_id=1, replica_groups={{0,32,64,96,8,40,72,104,16,48,80,112,24,56,88,120},{2,34,66,98,10,42,74..., dimensions={0} | all-to-all | bytes 1048576 | tf_op jit(solution)/shard_map/all_to_all | solution.py:476
  80.6 0.1 reshape.32.after_ref.p0
  80.7 0.1 collective-permute-start.9
  80.8 0.6 collective-permute-start.11
  81.4 0.9 collective-permute-start.7
  82.4 0.1 fusion
  82.4 2.2 %collective-permute-start.13 = (f32[2,4]{1,0:T(2,128)S(1)}, f32[2,4]{1,0:T(2,128)S(1)}, u32[]{:S(2)}, u32[]{:S(2)}) collective-permute-start(f32[2,4]{1,0:T(2,128)S(1)} %fusion), channel_id=1, source_target_pairs={{0,1},{1,0},{2,3},{3,2},{4,5},{5,4},{6,7},{7,6},{8,9},{9,8},{10,11... | collective-permute-start | bytes 104 | tf_op jit(solution)/shard_map/ppermute | solution.py:420
  84.7 0.8 collective-permute-done.13
  85.5 0.4 collective-permute-start.6
  85.9 7.1 %shard_map.142 = (bf16[8192,768]{1,0:T(8,128)(2,1)S(1)}, bf16[768,4096]{1,0:T(8,128)(2,1)S(1)}) custom-call(s32[4]{0:T(128)S(1)} %pad_add_fusion.1.refs_1_.at_ref, bf16[64,4096]{1,0:T(8,128)(2,1)S(1)} %reshape.32.after_ref.p0, bf16[8192,384]{1,0:T(8,128)(2,1)} %bitcast.15, bf16[8192,384]{1,0:T(8,128)(2,1)} %bitcast.16, bf16[384,8192]{1,0:T(8,128)(2,1)} %bitcast.14, ...), custom_call_target="tpu_custom_call" | custom-call | bytes 23068672 | tf_op jit(solution)/shard_map/pallas_call | solution.py:78
  93.0 0.2 collective-permute-start.10
  93.2 2.7 %collective-permute-start.12 = (bf16[64,4096]{1,0:T(8,128)(2,1)S(1)}, bf16[64,4096]{1,0:T(8,128)(2,1)S(1)}, u32[]{:S(2)}, u32[]{:S(2)}) collective-permute-start(bf16[64,4096]{1,0:T(8,128)(2,1)S(1)} %collective-permute-done.11.p3), channel_id=1, source_target_pairs={{0,1},{1,0},{2,3},{3,2},{4,5},{5,4},{6,7},{7,6},{8,9},{9,8},{10,11... | collective-permute-start | bytes 1572872 | tf_op jit(solution)/shard_map/ppermute | solution.py:420
  95.9 0.4 collective-permute-done.7.p1
  96.2 0.6 collective-permute-start.8
  96.8 2.5 %shard_map.143 = (f32[256,768]{1,0:T(8,128)S(1)}, f32[256,128]{1,0:T(8,128)S(1)}) custom-call(s32[4]{0:T(128)S(1)} %pad_add_fusion.1.refs_1_.at_ref, bf16[64,4096]{1,0:T(8,128)(2,1)S(1)} %reshape.32.after_ref.p0, bf16[64,4096]{1,0:T(8,128)(2,1)S(1)} %collective-permute-done.7.p1, bf16[64,4096]{1,0:T(8,128)(2,1)S(1)} %collective-permute-done.9.p2, ...), custom_call_target="tpu_custom_call" | custom-call | flops 16000000000 | bytes 9437184 | tf_op jit(solution)/shard_map/pallas_call | solution.py:315
  99.4 2.6 %shard_map.144.inner_ref = bf16[256,384]{1,0:T(8,128)(2,1)S(1)} custom-call(s32[4]{0:T(128)S(1)} %pad_add_fusion.1.refs_1_.at_ref, bf16[64,4096]{1,0:T(8,128)(2,1)S(1)} %collective-permute-done.6.p0, bf16[64,4096]{1,0:T(8,128)(2,1)S(1)} %collective-permute-done.8.p1, bf16[64,4096]{1,0:T(8,128)(2,1)S(1)} %collective-permute-done.10.p2, ...), custom_call_target="tpu_custom_call" | custom-call | flops 1600000000 | bytes 9437184 | tf_op jit(solution)/shard_map/pallas_call | solution.py:338
  102.0 0.1 collective-permute-start.14
  102.1 1.3 shard_map.145.half_ref
  103.4 0.2 collective-permute-done.14.other_ref
  103.5 1.8 %shard_map.146 = (bf16[64,4096]{1,0:T(8,128)(2,1)S(1)}, bf16[64,4096]{1,0:T(8,128)(2,1)S(1)}, bf16[64,4096]{1,0:T(8,128)(2,1)S(1)}, bf16[64,4096]{1,0:T(8,128)(2,1)S(1)}) custom-call(s32[4]{0:T(128)S(1)} %pad_add_fusion.1.refs_1_.at_ref, bf16[256,384]{1,0:T(8,128)(2,1)S(1)} %collective-permute-done.14.other_ref, ...), custom_call_target="tpu_custom_call" | custom-call | flops 800000000 | bytes 9437184 | tf_op jit(solution)/shard_map/pallas_call | solution.py:386
  105.3 0.6 collective-permute-start.15
  106.0 1.8 %collective-permute-start.16 = (bf16[64,4096]{1,0:T(8,128)(2,1)S(1)}, bf16[64,4096]{1,0:T(8,128)(2,1)S(1)}, u32[]{:S(2)}, u32[]{:S(2)}) collective-permute-start(bf16[64,4096]{1,0:T(8,128)(2,1)S(1)} %get-tuple-element.28), channel_id=1, source_target_pairs={{0,4},{1,17},{2,6},{3,19},{4,0},{5,21},{6,2},{7,23},{8,12},{9,25},... | collective-permute-start | bytes 1572872 | tf_op jit(solution)/shard_map/ppermute | solution.py:486
  107.8 5.9 %collective-permute-done.15 = bf16[64,4096]{1,0:T(8,128)(2,1)S(1)} collective-permute-done((bf16[64,4096]{1,0:T(8,128)(2,1)S(1)}, bf16[64,4096]{1,0:T(8,128)(2,1)S(1)}, u32[]{:S(2)}, u32[]{:S(2)}) %collective-permute-start.15) | collective-permute-done | bytes 524320 | tf_op jit(solution)/shard_map/ppermute | solution.py:486
  113.7 2.1 %collective-permute-done.16 = bf16[64,4096]{1,0:T(8,128)(2,1)S(1)} collective-permute-done((bf16[64,4096]{1,0:T(8,128)(2,1)S(1)}, bf16[64,4096]{1,0:T(8,128)(2,1)S(1)}, u32[]{:S(2)}, u32[]{:S(2)}) %collective-permute-start.16) | collective-permute-done | bytes 524320 | tf_op jit(solution)/shard_map/ppermute | solution.py:486
  115.9 5.6 %collective-permute-done.17 = bf16[64,4096]{1,0:T(8,128)(2,1)S(1)} collective-permute-done((bf16[64,4096]{1,0:T(8,128)(2,1)S(1)}, bf16[64,4096]{1,0:T(8,128)(2,1)S(1)}, u32[]{:S(2)}, u32[]{:S(2)}) %collective-permute-start.17) | collective-permute-done | bytes 524320 | tf_op jit(solution)/shard_map/ppermute | solution.py:486
  121.4 0.3 add_convert_fusion
  121.7 0.2 reshape.33
  121.9 15.7 %all_to_all.28.got_ref = bf16[16,4,4096]{2,1,0:T(4,128)(2,1)S(1)} all-to-all(bf16[16,4,4096]{2,1,0:T(4,128)(2,1)S(1)} %reshape.33), channel_id=1, replica_groups={{0,32,64,96,8,40,72,104,16,48,80,112,24,56,88,120},{2,34,66,98,10,42,74..., dimensions={0} | all-to-all | bytes 1048576 | tf_op jit(solution)/shard_map/all_to_all | solution.py:488
  137.6 0.7 shard_map.147
  138.3 0.5 collective-permute-start.18
  138.8 0.8 collective-permute-done.18
  139.6 0.7 broadcast_select_fusion
  (25 shorter events, 0.1 us)
Async XLA Ops:
  0.0 63.8 %collective-permute-start.5 = (bf16[384,8192]{1,0:T(8,128)(2,1)}, bf16[384,8192]{1,0:T(8,128)(2,1)}, u32[]{:S(2)}, u32[]{:S(2)}) collective-permute-start(bf16[384,8192]{1,0:T(8,128)(2,1)} %bitcast.13), channel_id=1, source_target_pairs={{0,1},{1,0},{2,3},{3,2},{4,5},{5,4},{6,7},{7,6},{8,9},{9,8},{10,11... | collective-permute-start | bytes 18874376 | tf_op jit(solution)/shard_map/ppermute | solution.py:420
  1.4 13.6 %collective-permute-start.2 = (bf16[64,2,1024]{2,1,0:T(2,128)(2,1)}, bf16[64,2,1024]{2,1,0:T(2,128)(2,1)S(1)}, u32[]{:S(2)}, u32[]{:S(2)}) collective-permute-start(bf16[64,2,1024]{2,1,0:T(2,128)(2,1)} %param.17), channel_id=1, source_target_pairs={{0,1},{1,0},{2,3},{3,2},{4,5},{5,4},{6,7},{7,6},{8,9},{9,8},{10,11... | collective-permute-start | bytes 786440 | tf_op jit(solution)/shard_map/ppermute | solution.py:420
  1.4 13.6 %collective-permute-start.3 = (bf16[64,2,1024]{2,1,0:T(2,128)(2,1)}, bf16[64,2,1024]{2,1,0:T(2,128)(2,1)}, u32[]{:S(2)}, u32[]{:S(2)}) collective-permute-start(bf16[64,2,1024]{2,1,0:T(2,128)(2,1)} %param.18), channel_id=1, source_target_pairs={{0,1},{1,0},{2,3},{3,2},{4,5},{5,4},{6,7},{7,6},{8,9},{9,8},{10,11... | collective-permute-start | bytes 786440 | tf_op jit(solution)/shard_map/ppermute | solution.py:420
  3.6 19.9 %all-to-all-start = ((bf16[32,2,4096]{2,1,0:T(2,128)(2,1)}), bf16[32,2,4096]{2,1,0:T(2,128)(2,1)S(1)}, u32[]{:S(2)}, u32[]{:S(2)}) async-start(bf16[32,2,4096]{2,1,0:T(2,128)(2,1)} %shard_map.136), calls=%async_computation | async-start | bytes 1048576 | tf_op jit(solution)/shard_map/all_to_all | solution.py:456
  11.9 11.8 %collective-permute-start = (bf16[512,1024]{1,0:T(8,128)(2,1)}, bf16[512,1024]{1,0:T(8,128)(2,1)S(1)}, u32[]{:S(2)}, u32[]{:S(2)}) collective-permute-start(bf16[512,1024]{1,0:T(8,128)(2,1)} %ka_ref.1), channel_id=1, source_target_pairs={{0,1},{1,0},{2,3},{3,2},{4,5},{5,4},{6,7},{7,6},{8,9},{9,8},{10,11... | collective-permute-start | bytes 3145736 | tf_op jit(solution)/shard_map/ppermute | solution.py:420
  12.2 11.5 %collective-permute-start.1 = (bf16[512,1024]{1,0:T(8,128)(2,1)}, bf16[512,1024]{1,0:T(8,128)(2,1)}, u32[]{:S(2)}, u32[]{:S(2)}) collective-permute-start(bf16[512,1024]{1,0:T(8,128)(2,1)} %va_ref.1), channel_id=1, source_target_pairs={{0,1},{1,0},{2,3},{3,2},{4,5},{5,4},{6,7},{7,6},{8,9},{9,8},{10,11... | collective-permute-start | bytes 3145736 | tf_op jit(solution)/shard_map/ppermute | solution.py:420
  13.2 0.7 copy-start.6
  13.2 1.0 copy-start.2
  13.2 1.0 copy-start.3
  14.7 30.5 %copy-start.1 = (bf16[2,8192]{1,0:T(2,128)(2,1)S(1)}, bf16[2,8192]{1,0:T(2,128)(2,1)}, u32[]{:S(2)}) copy-start(bf16[2,8192]{1,0:T(2,128)(2,1)} %hidden_ref.3) | copy-start | bytes 98308
  23.6 21.6 %copy-start = (bf16[256,8192]{1,0:T(8,128)(2,1)S(1)}, bf16[256,8192]{1,0:T(8,128)(2,1)}, u32[]{:S(2)}) copy-start(bf16[256,8192]{1,0:T(8,128)(2,1)} %w_ref.3) | copy-start | bytes 12582916
  46.6 3.3 %collective-permute-start.4 = (bf16[64,4096]{1,0:T(8,128)(2,1)S(1)}, bf16[64,4096]{1,0:T(8,128)(2,1)S(1)}, u32[]{:S(2)}, u32[]{:S(2)}) collective-permute-start(bf16[64,4096]{1,0:T(8,128)(2,1)S(1)} %get-tuple-element.20), channel_id=1, source_target_pairs={{0,1},{1,0},{2,3},{3,2},{4,5},{5,4},{6,7},{7,6},{8,9},{9,8},{10,11... | collective-permute-start | bytes 1572872 | tf_op jit(solution)/shard_map/ppermute | solution.py:420
  49.4 32.9 %copy-start.4 = (f32[2,2]{1,0:T(2,128)S(1)}, f32[2,2]{1,0:T(2,128)}, u32[]{:S(2)}) copy-start(f32[2,2]{1,0:T(2,128)} %param.24) | copy-start | bytes 52
  49.4 32.9 %copy-start.5 = (s32[2,2]{1,0:T(2,128)S(1)}, s32[2,2]{1,0:T(2,128)}, u32[]{:S(2)}) copy-start(s32[2,2]{1,0:T(2,128)} %param.23) | copy-start | bytes 52
  80.7 12.3 %collective-permute-start.9 = (bf16[64,4096]{1,0:T(8,128)(2,1)S(1)}, bf16[64,4096]{1,0:T(8,128)(2,1)S(1)}, u32[]{:S(2)}, u32[]{:S(2)}) collective-permute-start(bf16[64,4096]{1,0:T(8,128)(2,1)S(1)} %reshape.32.after_ref.p0), channel_id=1, source_target_pairs={{0,4},{1,17},{2,6},{3,19},{4,0},{5,21},{6,2},{7,23},{8,12},{9,25},... | collective-permute-start | bytes 1572872 | tf_op jit(solution)/shard_map/ppermute | solution.py:479
  80.8 12.4 %collective-permute-start.11 = (bf16[64,4096]{1,0:T(8,128)(2,1)S(1)}, bf16[64,4096]{1,0:T(8,128)(2,1)S(1)}, u32[]{:S(2)}, u32[]{:S(2)}) collective-permute-start(bf16[64,4096]{1,0:T(8,128)(2,1)S(1)} %reshape.32.after_ref.p0), channel_id=1, source_target_pairs={{0,6},{1,25},{2,0},{3,27},{4,2},{5,29},{6,4},{7,31},{8,14},{9,1},{... | collective-permute-start | bytes 1572872 | tf_op jit(solution)/shard_map/ppermute | solution.py:479
  81.4 14.8 %collective-permute-start.7 = (bf16[64,4096]{1,0:T(8,128)(2,1)S(1)}, bf16[64,4096]{1,0:T(8,128)(2,1)S(1)}, u32[]{:S(2)}, u32[]{:S(2)}) collective-permute-start(bf16[64,4096]{1,0:T(8,128)(2,1)S(1)} %reshape.32.after_ref.p0), channel_id=1, source_target_pairs={{0,2},{1,9},{2,4},{3,11},{4,6},{5,13},{6,0},{7,15},{8,10},{9,17},{... | collective-permute-start | bytes 1572872 | tf_op jit(solution)/shard_map/ppermute | solution.py:479
  82.4 3.0 %collective-permute-start.13 = (f32[2,4]{1,0:T(2,128)S(1)}, f32[2,4]{1,0:T(2,128)S(1)}, u32[]{:S(2)}, u32[]{:S(2)}) collective-permute-start(f32[2,4]{1,0:T(2,128)S(1)} %fusion), channel_id=1, source_target_pairs={{0,1},{1,0},{2,3},{3,2},{4,5},{5,4},{6,7},{7,6},{8,9},{9,8},{10,11... | collective-permute-start | bytes 104 | tf_op jit(solution)/shard_map/ppermute | solution.py:420
  85.5 13.8 %collective-permute-start.6 = (bf16[64,4096]{1,0:T(8,128)(2,1)S(1)}, bf16[64,4096]{1,0:T(8,128)(2,1)S(1)}, u32[]{:S(2)}, u32[]{:S(2)}) collective-permute-start(bf16[64,4096]{1,0:T(8,128)(2,1)S(1)} %reshape.32.after_ref.p0), channel_id=1, source_target_pairs={{0,1},{1,0},{2,3},{3,2},{4,5},{5,4},{6,7},{7,6},{8,9},{9,8},{10,11... | collective-permute-start | bytes 1572872 | tf_op jit(solution)/shard_map/ppermute | solution.py:420
  93.0 6.4 %collective-permute-start.10 = (bf16[64,4096]{1,0:T(8,128)(2,1)S(1)}, bf16[64,4096]{1,0:T(8,128)(2,1)S(1)}, u32[]{:S(2)}, u32[]{:S(2)}) collective-permute-start(bf16[64,4096]{1,0:T(8,128)(2,1)S(1)} %collective-permute-done.9.p2), channel_id=1, source_target_pairs={{0,1},{1,0},{2,3},{3,2},{4,5},{5,4},{6,7},{7,6},{8,9},{9,8},{10,11... | collective-permute-start | bytes 1572872 | tf_op jit(solution)/shard_map/ppermute | solution.py:420
  93.2 6.2 %collective-permute-start.12 = (bf16[64,4096]{1,0:T(8,128)(2,1)S(1)}, bf16[64,4096]{1,0:T(8,128)(2,1)S(1)}, u32[]{:S(2)}, u32[]{:S(2)}) collective-permute-start(bf16[64,4096]{1,0:T(8,128)(2,1)S(1)} %collective-permute-done.11.p3), channel_id=1, source_target_pairs={{0,1},{1,0},{2,3},{3,2},{4,5},{5,4},{6,7},{7,6},{8,9},{9,8},{10,11... | collective-permute-start | bytes 1572872 | tf_op jit(solution)/shard_map/ppermute | solution.py:420
  96.2 3.1 %collective-permute-start.8 = (bf16[64,4096]{1,0:T(8,128)(2,1)S(1)}, bf16[64,4096]{1,0:T(8,128)(2,1)S(1)}, u32[]{:S(2)}, u32[]{:S(2)}) collective-permute-start(bf16[64,4096]{1,0:T(8,128)(2,1)S(1)} %collective-permute-done.7.p1), channel_id=1, source_target_pairs={{0,1},{1,0},{2,3},{3,2},{4,5},{5,4},{6,7},{7,6},{8,9},{9,8},{10,11... | collective-permute-start | bytes 1572872 | tf_op jit(solution)/shard_map/ppermute | solution.py:420
  102.0 1.5 %collective-permute-start.14 = (bf16[256,384]{1,0:T(8,128)(2,1)S(1)}, bf16[256,384]{1,0:T(8,128)(2,1)S(1)}, u32[]{:S(2)}, u32[]{:S(2)}) collective-permute-start(bf16[256,384]{1,0:T(8,128)(2,1)S(1)} %shard_map.144.inner_ref), channel_id=1, source_target_pairs={{0,1},{1,0},{2,3},{3,2},{4,5},{5,4},{6,7},{7,6},{8,9},{9,8},{10,11... | collective-permute-start | bytes 589832 | tf_op jit(solution)/shard_map/ppermute | solution.py:420
  105.3 8.4 %collective-permute-start.15 = (bf16[64,4096]{1,0:T(8,128)(2,1)S(1)}, bf16[64,4096]{1,0:T(8,128)(2,1)S(1)}, u32[]{:S(2)}, u32[]{:S(2)}) collective-permute-start(bf16[64,4096]{1,0:T(8,128)(2,1)S(1)} %get-tuple-element.27), channel_id=1, source_target_pairs={{0,6},{1,25},{2,0},{3,27},{4,2},{5,29},{6,4},{7,31},{8,14},{9,1},{... | collective-permute-start | bytes 1572872 | tf_op jit(solution)/shard_map/ppermute | solution.py:486
  106.0 9.9 %collective-permute-start.16 = (bf16[64,4096]{1,0:T(8,128)(2,1)S(1)}, bf16[64,4096]{1,0:T(8,128)(2,1)S(1)}, u32[]{:S(2)}, u32[]{:S(2)}) collective-permute-start(bf16[64,4096]{1,0:T(8,128)(2,1)S(1)} %get-tuple-element.28), channel_id=1, source_target_pairs={{0,4},{1,17},{2,6},{3,19},{4,0},{5,21},{6,2},{7,23},{8,12},{9,25},... | collective-permute-start | bytes 1572872 | tf_op jit(solution)/shard_map/ppermute | solution.py:486
  107.8 13.6 %collective-permute-start.17 = (bf16[64,4096]{1,0:T(8,128)(2,1)S(1)}, bf16[64,4096]{1,0:T(8,128)(2,1)S(1)}, u32[]{:S(2)}, u32[]{:S(2)}) collective-permute-start(bf16[64,4096]{1,0:T(8,128)(2,1)S(1)} %get-tuple-element.29), channel_id=1, source_target_pairs={{0,2},{1,9},{2,4},{3,11},{4,6},{5,13},{6,0},{7,15},{8,10},{9,17},{... | collective-permute-start | bytes 1572872 | tf_op jit(solution)/shard_map/ppermute | solution.py:486
  138.3 1.3 collective-permute-start.18

commit v6 on v5

--- a/solution.py
+++ b/solution.py
@@ -365,33 +365,54 @@
     )(inner, in_vmem(down))
 
 
-def fourth_kernel(at_ref, other_ref, w_ref, half_ref, o0, o1, o2, o3, x_ref):
+def fourth_kernel(at_ref, other_ref, w_ref, half_ref, *refs):
+    outs, x_ref = refs[:-1], refs[-1]
     units = other_ref.shape[1]
     for a in range(4):
         for b in range(4):
             line, line_b = (4 * a + b) * 16, (4 * b + a) * 16
             x_ref[line : line + 16, :] = other_ref[line_b : line_b + 16, :]
-    outs = (o0, o1, o2, o3)
     width = HALF // 4
     for part in range(4):
         cols = slice(part * width, (part + 1) * width)
         value = (half_ref[:, cols] + dot(x_ref[...], w_ref[units:, cols])).astype(BF)
+        here = slice(part % 2 * width, (part % 2 + 1) * width)
         for a in range(4):
             for b in range(4):
                 line = (4 * a + b) * 16
-                outs[a][pl.ds(rolled(at_ref[1], b), 16), cols] = value[line : line + 16]
+                outs[2 * a + part // 2][pl.ds(rolled(at_ref[1], b), 16), here] = value[line : line + 16]
 
 
 def expert_fourth(at, other, down, half):
     return pl.pallas_call(
         fourth_kernel,
         in_specs=[SCALARS] + [WHOLE] * 3,
-        out_specs=[WHOLE] * 4,
-        out_shape=[jax.ShapeDtypeStruct((64, HALF), BF)] * 4,
+        out_specs=[WHOLE] * 8,
+        out_shape=[jax.ShapeDtypeStruct((64, HALF // 2), BF)] * 8,
         scratch_shapes=[pltpu.VMEM(other.shape, BF)],
         compiler_params=pltpu.CompilerParams(vmem_limit_bytes=12 * MB),
         cost_estimate=pl.CostEstimate(flops=800000000, bytes_accessed=9 * MB, transcendentals=0),
     )(at, other, in_vmem(down), half)
+
+
+def total_kernel(*refs):
+    out_ref = refs[-1]
+    width = HALF // 2
+    for part in range(2):
+        value = functools.reduce(jnp.add, [ref[...].astype(F32) for ref in refs[3 * part : 3 * part + 3]])
+        for chip in range(16):
+            out_ref[chip, :, part * width : (part + 1) * width] = value[4 * chip : 4 * chip + 4].astype(BF)
+
+
+def total(first, second):
+    return pl.pallas_call(
+        total_kernel,
+        in_specs=[WHOLE] * 6,
+        out_specs=WHOLE,
+        out_shape=jax.ShapeDtypeStruct((16, 4, HALF), BF),
+        compiler_params=pltpu.CompilerParams(vmem_limit_bytes=8 * MB),
+        cost_estimate=pl.CostEstimate(flops=1000000, bytes_accessed=2 * MB, transcendentals=0),
+    )(*first, *second)
 
 
 def mix_kernel(at_ref, got_ref, residual_ref, weights_ref, kept_ref, sent_ref):
@@ -483,10 +504,16 @@
     inner = expert_second(at, pieces_b, gate_up, gain, acc, square)
     other = swap(inner)
     out = expert_fourth(at, other, down, expert_third(inner, down))
-    out = [out[0]] + [lax.ppermute(out[s], PLANE, line_shift(4 - s)) for s in (1, 2, 3)]
-    out = functools.reduce(jnp.add, [piece.astype(F32) for piece in out]).astype(BF)
+    (a0, b0), (a1, b1), (a2, b2), (a3, b3) = [(out[2 * i], out[2 * i + 1]) for i in range(4)]
+    ahead = lambda value: lax.ppermute(value, PLANE, line_shift(1))
+    back = lambda value: lax.ppermute(value, PLANE, line_shift(3))
+    plus = lambda first, second: (first.astype(F32) + second.astype(F32)).astype(BF)
+    via_a, via_b = ahead(a2), back(b2)
+    near_b, near_a = ahead(b3), back(a1)
+    far_a, far_b = ahead(plus(a3, via_a)), back(plus(b1, via_b))
+    out = total((a0, near_a, far_a), (b0, near_b, far_b))
     out = lax.all_to_all(
-        out.reshape(16, 4, HALF), ALL, split_axis=0, concat_axis=0, tiled=True, axis_index_groups=wide
+        out, ALL, split_axis=0, concat_axis=0, tiled=True, axis_index_groups=wide
     )
     kept, sent = mix(at, out, residual, weights)
     got = swap(sent)

time: 141 us -> 140 us (level)
  waiting for transfers between devices: 23.1 us -> 18.3 us
  starting transfers between devices: 23.3 us -> 26.1 us
    ppermute x3 -> x6, waiting for transfers between devices: 13.6 us -> 8.85 us  [the longest x3 4.62 us: local(): ahead = lambda value: lax.ppermute(value, PLANE, line_shift(1))]
    ppermute x3 -> x6, starting transfers between devices: 2.47 us -> 4.93 us  [the longest x3 3.96 us: local(): back = lambda value: lax.ppermute(value, PLANE, line_shift(3))]
  transfers between devices with their start and end apart: 20 -> 23, of which waited for: 9 -> 12; matrix products, arithmetic and copies ran while one was open for 3% -> 3% of each run, Pallas kernels for 16% -> 16%
where the time goes in v6:
time: 140 us; the launch traced here: 139 us
  blocking collectives  61.6 us (44%)
  Pallas kernels  27.3 us (20%)
  starting transfers between devices  26.1 us (19%)
  waiting for transfers between devices  18.3 us (13%)
  other arithmetic  2.98 us (2%)
  local copies, waits for them, and re-layouts  2.65 us (2%)
    all_to_all x1, blocking collectives, local(): lax.all_to_all(out, ALL, split_axis=0, concat_axis=0, tiled=True, axis_in...  16.7 us
    all_to_all x1, blocking collectives, local(): lax.all_to_all(sent, ALL, split_axis=0, concat_axis=0, tiled=True, axis_i...  16.7 us
    all_to_all x1, blocking collectives, local(): lax.all_to_all(parts, ('z', 'y'), split_axis=0, concat_axis=0, tiled=True)  14.6 us
    all_to_all x1, blocking collectives, local(): lax.all_to_all(summed, ('z', 'y'), split_axis=0, concat_axis=0, tiled=True)  13.6 us
    ppermute x13, starting transfers between devices, swap(): return lax.ppermute(value, 'c', SWAP)  11.2 us
    all_to_all x1, starting transfers between devices, local(): lax.all_to_all(q, PLANE, split_axis=0, concat_axis=0, tiled=True)  8.3 us
    pallas_call x1, Pallas kernels, fetch(): pl.pallas_call(fetch_kernel, in_specs=[SCALARS] + [pl.BlockSpec(memory_sp...  7.07 us
    pallas_call x1, Pallas kernels, attend(): pl.pallas_call(attend_kernel, grid=(1,), in_specs=[pl.BlockSpec(a.shape,...  6.87 us
  transfers between devices with their start and end apart: 23, of which 12 were waited for; matrix products, arithmetic and copies ran while one was open for 3% of the time, Pallas kernels for 16%

profile of v6, /device:TPU:1, one launch (start us, length us, event | category | flops | bytes accessed | tf_op | source)
XLA Modules:
  0.0 139.2 jit_solution(11652198298328373703)
XLA Ops:
  0.0 1.4 %collective-permute-start.5 = (bf16[384,8192]{1,0:T(8,128)(2,1)}, bf16[384,8192]{1,0:T(8,128)(2,1)}, u32[]{:S(2)}, u32[]{:S(2)}) collective-permute-start(bf16[384,8192]{1,0:T(8,128)(2,1)} %bitcast.13), channel_id=1, source_target_pairs={{0,1},{1,0},{2,3},{3,2},{4,5},{5,4},{6,7},{7,6},{8,9},{9,8},{10,11... | collective-permute-start | bytes 18874376 | tf_op jit(solution)/shard_map/ppermute | solution.py:441
  1.4 0.5 collective-permute-start.3
  1.9 1.7 %shard_map.136 = bf16[32,2,4096]{2,1,0:T(2,128)(2,1)} custom-call(bf16[2,8192]{1,0:T(2,128)(2,1)} %q_ref.1), custom_call_target="tpu_custom_call" | custom-call | bytes 1048576 | tf_op jit(solution)/shard_map/pallas_call | solution.py:107
  3.6 8.3 %all-to-all-start = ((bf16[32,2,4096]{2,1,0:T(2,128)(2,1)}), bf16[32,2,4096]{2,1,0:T(2,128)(2,1)S(1)}, u32[]{:S(2)}, u32[]{:S(2)}) async-start(bf16[32,2,4096]{2,1,0:T(2,128)(2,1)} %shard_map.136), calls=%async_computation | async-start | bytes 1048576 | tf_op jit(solution)/shard_map/all_to_all | solution.py:477
  11.9 0.3 collective-permute-start
  12.2 0.3 collective-permute-start.1
  12.5 0.7 reshape.27.gain_ref
  13.3 0.6 copy-done.6
  13.9 0.1 copy.16
  14.0 0.2 copy-done.2
  14.2 0.1 copy-done.3
  14.3 0.5 pad_maximum_fusion
  14.7 0.2 reshape.25.sa_ref
  14.9 0.1 pad_add_fusion.1.refs_1_.at_ref
  15.0 1.4 %pad_maximum_fusion.1 = bf16[64,2,2048]{2,1,0:T(2,128)(2,1)S(1)} fusion(bf16[64,2,1024]{2,1,0:T(2,128)(2,1)} %collective-permute-done.3, bf16[64,2,1024]{2,1,0:T(2,128)(2,1)S(1)} %collective-permute-done.2), kind=kLoop, calls=%fused_computation.2 | loop fusion | flops 1048576 | bytes 1048576 | tf_op jit(solution)/shard_map/concatenate | solution.py:479
  16.5 0.2 reshape.26.sb_ref
  16.7 6.8 %all-to-all-done = bf16[32,2,4096]{2,1,0:T(2,128)(2,1)S(1)} async-done(((bf16[32,2,4096]{2,1,0:T(2,128)(2,1)}), bf16[32,2,4096]{2,1,0:T(2,128)(2,1)S(1)}, u32[]{:S(2)}, u32[]{:S(2)}) %all-to-all-start) | async-done | bytes 524320 | tf_op jit(solution)/shard_map/all_to_all | solution.py:477
  23.4 0.2 reshape.24.q_ref
  23.7 6.9 %shard_map.138 = bf16[16,72,256]{2,1,0:T(8,128)(2,1)S(1)} custom-call(bf16[64,4096]{1,0:T(8,128)(2,1)S(1)} %reshape.24.q_ref, bf16[512,1024]{1,0:T(8,128)(2,1)} %ka_ref.1, bf16[512,1024]{1,0:T(8,128)(2,1)S(1)} %collective-permute-done.kb_ref, bf16[512,1024]{1,0:T(8,128)(2,1)} %va_ref.1, bf16[512,1024]{1,0:T(8,128)(2,1)} %collective-permute-done.1.vb_ref, ...), custom_call_target="tpu_custom_call" | custom-call | flops 1400000000 | bytes 6291456 | tf_op jit(solution)/shard_map/pallas_call | solution.py:189
  30.6 14.6 %all_to_all.25.got_ref = bf16[16,72,256]{2,1,0:T(8,128)(2,1)S(1)} all-to-all(bf16[16,72,256]{2,1,0:T(8,128)(2,1)S(1)} %shard_map.138), channel_id=1, replica_groups=mesh['x'=4,'z'=4,'y'=4,'c'=2] {'z','y'}, dimensions={0} | all-to-all | bytes 1179648 | tf_op jit(solution)/shard_map/all_to_all | solution.py:489
  45.2 1.4 shard_map.139
  46.6 1.8 %collective-permute-start.4 = (bf16[64,4096]{1,0:T(8,128)(2,1)S(1)}, bf16[64,4096]{1,0:T(8,128)(2,1)S(1)}, u32[]{:S(2)}, u32[]{:S(2)}) collective-permute-start(bf16[64,4096]{1,0:T(8,128)(2,1)S(1)} %get-tuple-element.24), channel_id=1, source_target_pairs={{0,1},{1,0},{2,3},{3,2},{4,5},{5,4},{6,7},{7,6},{8,9},{9,8},{10,11... | collective-permute-start | bytes 1572872 | tf_op jit(solution)/shard_map/ppermute | solution.py:441
  48.4 1.1 shard_map.140
  49.4 0.4 collective-permute-done.4
  49.9 0.1 add_convert_fusion
  50.0 0.2 reshape.28
  50.2 13.6 %all_to_all.26.got_ref = bf16[16,4,4096]{2,1,0:T(4,128)(2,1)S(1)} all-to-all(bf16[16,4,4096]{2,1,0:T(4,128)(2,1)S(1)} %reshape.28), channel_id=1, replica_groups=mesh['x'=4,'z'=4,'y'=4,'c'=2] {'z','y'}, dimensions={0} | all-to-all | bytes 1048576 | tf_op jit(solution)/shard_map/all_to_all | solution.py:494
  63.8 0.1 shard_map.141
  63.9 16.7 %all_to_all.27 = bf16[16,4,4096]{2,1,0:T(4,128)(2,1)S(1)} all-to-all(bf16[16,4,4096]{2,1,0:T(4,128)(2,1)S(1)} %get-tuple-element.25), channel_id=1, replica_groups={{0,32,64,96,8,40,72,104,16,48,80,112,24,56,88,120},{2,34,66,98,10,42,74..., dimensions={0} | all-to-all | bytes 1048576 | tf_op jit(solution)/shard_map/all_to_all | solution.py:497
  80.6 0.1 reshape.29.after_ref.p0
  80.7 0.1 collective-permute-start.9
  80.8 0.6 collective-permute-start.11
  81.4 0.9 collective-permute-start.7
  82.4 0.1 fusion
  82.4 2.2 %collective-permute-start.13 = (f32[2,4]{1,0:T(2,128)S(1)}, f32[2,4]{1,0:T(2,128)S(1)}, u32[]{:S(2)}, u32[]{:S(2)}) collective-permute-start(f32[2,4]{1,0:T(2,128)S(1)} %fusion), channel_id=1, source_target_pairs={{0,1},{1,0},{2,3},{3,2},{4,5},{5,4},{6,7},{7,6},{8,9},{9,8},{10,11... | collective-permute-start | bytes 104 | tf_op jit(solution)/shard_map/ppermute | solution.py:441
  84.7 0.8 collective-permute-done.13
  85.5 0.4 collective-permute-start.6
  85.9 7.1 %shard_map.142 = (bf16[8192,768]{1,0:T(8,128)(2,1)S(1)}, bf16[768,4096]{1,0:T(8,128)(2,1)S(1)}) custom-call(s32[4]{0:T(128)S(1)} %pad_add_fusion.1.refs_1_.at_ref, bf16[64,4096]{1,0:T(8,128)(2,1)S(1)} %reshape.29.after_ref.p0, bf16[8192,384]{1,0:T(8,128)(2,1)} %bitcast.15, bf16[8192,384]{1,0:T(8,128)(2,1)} %bitcast.16, bf16[384,8192]{1,0:T(8,128)(2,1)} %bitcast.14, ...), custom_call_target="tpu_custom_call" | custom-call | bytes 23068672 | tf_op jit(solution)/shard_map/pallas_call | solution.py:78
  93.0 0.2 collective-permute-start.10
  93.2 2.7 %collective-permute-start.12 = (bf16[64,4096]{1,0:T(8,128)(2,1)S(1)}, bf16[64,4096]{1,0:T(8,128)(2,1)S(1)}, u32[]{:S(2)}, u32[]{:S(2)}) collective-permute-start(bf16[64,4096]{1,0:T(8,128)(2,1)S(1)} %collective-permute-done.11.p3), channel_id=1, source_target_pairs={{0,1},{1,0},{2,3},{3,2},{4,5},{5,4},{6,7},{7,6},{8,9},{9,8},{10,11... | collective-permute-start | bytes 1572872 | tf_op jit(solution)/shard_map/ppermute | solution.py:441
  95.9 0.4 collective-permute-done.7.p1
  96.3 0.6 collective-permute-start.8
  96.8 2.5 %shard_map.143 = (f32[256,768]{1,0:T(8,128)S(1)}, f32[256,128]{1,0:T(8,128)S(1)}) custom-call(s32[4]{0:T(128)S(1)} %pad_add_fusion.1.refs_1_.at_ref, bf16[64,4096]{1,0:T(8,128)(2,1)S(1)} %reshape.29.after_ref.p0, bf16[64,4096]{1,0:T(8,128)(2,1)S(1)} %collective-permute-done.7.p1, bf16[64,4096]{1,0:T(8,128)(2,1)S(1)} %collective-permute-done.9.p2, ...), custom_call_target="tpu_custom_call" | custom-call | flops 16000000000 | bytes 9437184 | tf_op jit(solution)/shard_map/pallas_call | solution.py:315
  99.4 2.6 %shard_map.144.inner_ref = bf16[256,384]{1,0:T(8,128)(2,1)S(1)} custom-call(s32[4]{0:T(128)S(1)} %pad_add_fusion.1.refs_1_.at_ref, bf16[64,4096]{1,0:T(8,128)(2,1)S(1)} %collective-permute-done.6.p0, bf16[64,4096]{1,0:T(8,128)(2,1)S(1)} %collective-permute-done.8.p1, bf16[64,4096]{1,0:T(8,128)(2,1)S(1)} %collective-permute-done.10.p2, ...), custom_call_target="tpu_custom_call" | custom-call | flops 1600000000 | bytes 9437184 | tf_op jit(solution)/shard_map/pallas_call | solution.py:338
  102.0 0.1 collective-permute-start.14
  102.1 1.3 shard_map.145.half_ref
  103.4 0.2 collective-permute-done.14.other_ref
  103.5 1.8 %shard_map.146 = (bf16[64,2048]{1,0:T(8,128)(2,1)S(1)}, bf16[64,2048]{1,0:T(8,128)(2,1)S(1)}, bf16[64,2048]{1,0:T(8,128)(2,1)S(1)}, bf16[64,2048]{1,0:T(8,128)(2...) custom-call(s32[4]{0:T(128)S(1)} %pad_add_fusion.1.refs_1_.at_ref, ...), custom_call_target="tpu_custom_call" | custom-call | flops 800000000 | bytes 9437184 | tf_op jit(solution)/shard_map/pallas_call | solution.py:387
  105.4 0.6 collective-permute-start.19
  106.0 0.9 collective-permute-start.16
  106.9 1.8 %collective-permute-start.15 = (bf16[64,2048]{1,0:T(8,128)(2,1)S(1)}, bf16[64,2048]{1,0:T(8,128)(2,1)S(1)}, u32[]{:S(2)}, u32[]{:S(2)}) collective-permute-start(bf16[64,2048]{1,0:T(8,128)(2,1)S(1)} %get-tuple-element.31), channel_id=1, source_target_pairs={{0,6},{1,25},{2,0},{3,27},{4,2},{5,29},{6,4},{7,31},{8,14},{9,1},{... | collective-permute-start | bytes 786440 | tf_op jit(solution)/shard_map/ppermute | solution.py:509
  108.7 2.3 %collective-permute-done.19 = bf16[64,2048]{1,0:T(8,128)(2,1)S(1)} collective-permute-done((bf16[64,2048]{1,0:T(8,128)(2,1)S(1)}, bf16[64,2048]{1,0:T(8,128)(2,1)S(1)}, u32[]{:S(2)}, u32[]{:S(2)}) %collective-permute-start.19) | collective-permute-done | bytes 262176 | tf_op jit(solution)/shard_map/ppermute | solution.py:509
  111.0 1.5 %collective-permute-start.20 = (bf16[64,2048]{1,0:T(8,128)(2,1)S(1)}, bf16[64,2048]{1,0:T(8,128)(2,1)S(1)}, u32[]{:S(2)}, u32[]{:S(2)}) collective-permute-start(bf16[64,2048]{1,0:T(8,128)(2,1)S(1)} %add_convert_fusion.1), channel_id=1, source_target_pairs={{0,6},{1,25},{2,0},{3,27},{4,2},{5,29},{6,4},{7,31},{8,14},{9,1},{... | collective-permute-start | bytes 786440 | tf_op jit(solution)/shard_map/ppermute | solution.py:509
  112.6 0.2 collective-permute-done.16
  112.9 0.9 collective-permute-done.15.refs_1_
  113.8 1.8 %collective-permute-done.18.refs_4_ = bf16[64,2048]{1,0:T(8,128)(2,1)S(1)} collective-permute-done((bf16[64,2048]{1,0:T(8,128)(2,1)S(1)}, bf16[64,2048]{1,0:T(8,128)(2,1)S(1)}, u32[]{:S(2)}, u32[]{:S(2)}) %collective-permute-start.18) | collective-permute-done | bytes 262176 | tf_op jit(solution)/shard_map/ppermute | solution.py:508
  115.5 1.1 collective-permute-done.20.refs_5_
  116.6 2.7 %collective-permute-done.17.refs_2_ = bf16[64,2048]{1,0:T(8,128)(2,1)S(1)} collective-permute-done((bf16[64,2048]{1,0:T(8,128)(2,1)S(1)}, bf16[64,2048]{1,0:T(8,128)(2,1)S(1)}, u32[]{:S(2)}, u32[]{:S(2)}) %collective-permute-start.17) | collective-permute-done | bytes 262176 | tf_op jit(solution)/shard_map/ppermute | solution.py:508
  119.3 0.2 shard_map.147
  119.5 16.7 %all_to_all.28.got_ref = bf16[16,4,4096]{2,1,0:T(4,128)(2,1)S(1)} all-to-all(bf16[16,4,4096]{2,1,0:T(4,128)(2,1)S(1)} %shard_map.147), channel_id=1, replica_groups={{0,32,64,96,8,40,72,104,16,48,80,112,24,56,88,120},{2,34,66,98,10,42,74..., dimensions={0} | all-to-all | bytes 1048576 | tf_op jit(solution)/shard_map/all_to_all | solution.py:515
  136.2 0.7 shard_map.148
  136.9 0.8 collective-permute-start.21
  137.7 0.8 collective-permute-done.21
  138.5 0.7 broadcast_select_fusion
  (32 shorter events, 0.3 us)
Async XLA Ops:
  0.0 63.8 %collective-permute-start.5 = (bf16[384,8192]{1,0:T(8,128)(2,1)}, bf16[384,8192]{1,0:T(8,128)(2,1)}, u32[]{:S(2)}, u32[]{:S(2)}) collective-permute-start(bf16[384,8192]{1,0:T(8,128)(2,1)} %bitcast.13), channel_id=1, source_target_pairs={{0,1},{1,0},{2,3},{3,2},{4,5},{5,4},{6,7},{7,6},{8,9},{9,8},{10,11... | collective-permute-start | bytes 18874376 | tf_op jit(solution)/shard_map/ppermute | solution.py:441
  1.4 13.6 %collective-permute-start.2 = (bf16[64,2,1024]{2,1,0:T(2,128)(2,1)}, bf16[64,2,1024]{2,1,0:T(2,128)(2,1)S(1)}, u32[]{:S(2)}, u32[]{:S(2)}) collective-permute-start(bf16[64,2,1024]{2,1,0:T(2,128)(2,1)} %param.17), channel_id=1, source_target_pairs={{0,1},{1,0},{2,3},{3,2},{4,5},{5,4},{6,7},{7,6},{8,9},{9,8},{10,11... | collective-permute-start | bytes 786440 | tf_op jit(solution)/shard_map/ppermute | solution.py:441
  1.4 13.6 %collective-permute-start.3 = (bf16[64,2,1024]{2,1,0:T(2,128)(2,1)}, bf16[64,2,1024]{2,1,0:T(2,128)(2,1)}, u32[]{:S(2)}, u32[]{:S(2)}) collective-permute-start(bf16[64,2,1024]{2,1,0:T(2,128)(2,1)} %param.18), channel_id=1, source_target_pairs={{0,1},{1,0},{2,3},{3,2},{4,5},{5,4},{6,7},{7,6},{8,9},{9,8},{10,11... | collective-permute-start | bytes 786440 | tf_op jit(solution)/shard_map/ppermute | solution.py:441
  3.6 19.9 %all-to-all-start = ((bf16[32,2,4096]{2,1,0:T(2,128)(2,1)}), bf16[32,2,4096]{2,1,0:T(2,128)(2,1)S(1)}, u32[]{:S(2)}, u32[]{:S(2)}) async-start(bf16[32,2,4096]{2,1,0:T(2,128)(2,1)} %shard_map.136), calls=%async_computation | async-start | bytes 1048576 | tf_op jit(solution)/shard_map/all_to_all | solution.py:477
  11.9 11.8 %collective-permute-start = (bf16[512,1024]{1,0:T(8,128)(2,1)}, bf16[512,1024]{1,0:T(8,128)(2,1)S(1)}, u32[]{:S(2)}, u32[]{:S(2)}) collective-permute-start(bf16[512,1024]{1,0:T(8,128)(2,1)} %ka_ref.1), channel_id=1, source_target_pairs={{0,1},{1,0},{2,3},{3,2},{4,5},{5,4},{6,7},{7,6},{8,9},{9,8},{10,11... | collective-permute-start | bytes 3145736 | tf_op jit(solution)/shard_map/ppermute | solution.py:441
  12.2 11.5 %collective-permute-start.1 = (bf16[512,1024]{1,0:T(8,128)(2,1)}, bf16[512,1024]{1,0:T(8,128)(2,1)}, u32[]{:S(2)}, u32[]{:S(2)}) collective-permute-start(bf16[512,1024]{1,0:T(8,128)(2,1)} %va_ref.1), channel_id=1, source_target_pairs={{0,1},{1,0},{2,3},{3,2},{4,5},{5,4},{6,7},{7,6},{8,9},{9,8},{10,11... | collective-permute-start | bytes 3145736 | tf_op jit(solution)/shard_map/ppermute | solution.py:441
  13.2 0.7 copy-start.6
  13.2 1.0 copy-start.2
  13.2 1.0 copy-start.3
  14.7 30.5 %copy-start.1 = (bf16[2,8192]{1,0:T(2,128)(2,1)S(1)}, bf16[2,8192]{1,0:T(2,128)(2,1)}, u32[]{:S(2)}) copy-start(bf16[2,8192]{1,0:T(2,128)(2,1)} %hidden_ref.3) | copy-start | bytes 98308
  23.6 21.6 %copy-start = (bf16[256,8192]{1,0:T(8,128)(2,1)S(1)}, bf16[256,8192]{1,0:T(8,128)(2,1)}, u32[]{:S(2)}) copy-start(bf16[256,8192]{1,0:T(8,128)(2,1)} %w_ref.3) | copy-start | bytes 12582916
  46.6 3.3 %collective-permute-start.4 = (bf16[64,4096]{1,0:T(8,128)(2,1)S(1)}, bf16[64,4096]{1,0:T(8,128)(2,1)S(1)}, u32[]{:S(2)}, u32[]{:S(2)}) collective-permute-start(bf16[64,4096]{1,0:T(8,128)(2,1)S(1)} %get-tuple-element.24), channel_id=1, source_target_pairs={{0,1},{1,0},{2,3},{3,2},{4,5},{5,4},{6,7},{7,6},{8,9},{9,8},{10,11... | collective-permute-start | bytes 1572872 | tf_op jit(solution)/shard_map/ppermute | solution.py:441
  49.4 32.9 %copy-start.4 = (f32[2,2]{1,0:T(2,128)S(1)}, f32[2,2]{1,0:T(2,128)}, u32[]{:S(2)}) copy-start(f32[2,2]{1,0:T(2,128)} %param.24) | copy-start | bytes 52
  49.4 32.9 %copy-start.5 = (s32[2,2]{1,0:T(2,128)S(1)}, s32[2,2]{1,0:T(2,128)}, u32[]{:S(2)}) copy-start(s32[2,2]{1,0:T(2,128)} %param.23) | copy-start | bytes 52
  80.7 12.3 %collective-permute-start.9 = (bf16[64,4096]{1,0:T(8,128)(2,1)S(1)}, bf16[64,4096]{1,0:T(8,128)(2,1)S(1)}, u32[]{:S(2)}, u32[]{:S(2)}) collective-permute-start(bf16[64,4096]{1,0:T(8,128)(2,1)S(1)} %reshape.29.after_ref.p0), channel_id=1, source_target_pairs={{0,4},{1,17},{2,6},{3,19},{4,0},{5,21},{6,2},{7,23},{8,12},{9,25},... | collective-permute-start | bytes 1572872 | tf_op jit(solution)/shard_map/ppermute | solution.py:500
  80.8 12.4 %collective-permute-start.11 = (bf16[64,4096]{1,0:T(8,128)(2,1)S(1)}, bf16[64,4096]{1,0:T(8,128)(2,1)S(1)}, u32[]{:S(2)}, u32[]{:S(2)}) collective-permute-start(bf16[64,4096]{1,0:T(8,128)(2,1)S(1)} %reshape.29.after_ref.p0), channel_id=1, source_target_pairs={{0,6},{1,25},{2,0},{3,27},{4,2},{5,29},{6,4},{7,31},{8,14},{9,1},{... | collective-permute-start | bytes 1572872 | tf_op jit(solution)/shard_map/ppermute | solution.py:500
  81.4 14.8 %collective-permute-start.7 = (bf16[64,4096]{1,0:T(8,128)(2,1)S(1)}, bf16[64,4096]{1,0:T(8,128)(2,1)S(1)}, u32[]{:S(2)}, u32[]{:S(2)}) collective-permute-start(bf16[64,4096]{1,0:T(8,128)(2,1)S(1)} %reshape.29.after_ref.p0), channel_id=1, source_target_pairs={{0,2},{1,9},{2,4},{3,11},{4,6},{5,13},{6,0},{7,15},{8,10},{9,17},{... | collective-permute-start | bytes 1572872 | tf_op jit(solution)/shard_map/ppermute | solution.py:500
  82.4 3.0 %collective-permute-start.13 = (f32[2,4]{1,0:T(2,128)S(1)}, f32[2,4]{1,0:T(2,128)S(1)}, u32[]{:S(2)}, u32[]{:S(2)}) collective-permute-start(f32[2,4]{1,0:T(2,128)S(1)} %fusion), channel_id=1, source_target_pairs={{0,1},{1,0},{2,3},{3,2},{4,5},{5,4},{6,7},{7,6},{8,9},{9,8},{10,11... | collective-permute-start | bytes 104 | tf_op jit(solution)/shard_map/ppermute | solution.py:441
  85.5 13.8 %collective-permute-start.6 = (bf16[64,4096]{1,0:T(8,128)(2,1)S(1)}, bf16[64,4096]{1,0:T(8,128)(2,1)S(1)}, u32[]{:S(2)}, u32[]{:S(2)}) collective-permute-start(bf16[64,4096]{1,0:T(8,128)(2,1)S(1)} %reshape.29.after_ref.p0), channel_id=1, source_target_pairs={{0,1},{1,0},{2,3},{3,2},{4,5},{5,4},{6,7},{7,6},{8,9},{9,8},{10,11... | collective-permute-start | bytes 1572872 | tf_op jit(solution)/shard_map/ppermute | solution.py:441
  93.0 6.4 %collective-permute-start.10 = (bf16[64,4096]{1,0:T(8,128)(2,1)S(1)}, bf16[64,4096]{1,0:T(8,128)(2,1)S(1)}, u32[]{:S(2)}, u32[]{:S(2)}) collective-permute-start(bf16[64,4096]{1,0:T(8,128)(2,1)S(1)} %collective-permute-done.9.p2), channel_id=1, source_target_pairs={{0,1},{1,0},{2,3},{3,2},{4,5},{5,4},{6,7},{7,6},{8,9},{9,8},{10,11... | collective-permute-start | bytes 1572872 | tf_op jit(solution)/shard_map/ppermute | solution.py:441
  93.2 6.2 %collective-permute-start.12 = (bf16[64,4096]{1,0:T(8,128)(2,1)S(1)}, bf16[64,4096]{1,0:T(8,128)(2,1)S(1)}, u32[]{:S(2)}, u32[]{:S(2)}) collective-permute-start(bf16[64,4096]{1,0:T(8,128)(2,1)S(1)} %collective-permute-done.11.p3), channel_id=1, source_target_pairs={{0,1},{1,0},{2,3},{3,2},{4,5},{5,4},{6,7},{7,6},{8,9},{9,8},{10,11... | collective-permute-start | bytes 1572872 | tf_op jit(solution)/shard_map/ppermute | solution.py:441
  96.3 3.1 %collective-permute-start.8 = (bf16[64,4096]{1,0:T(8,128)(2,1)S(1)}, bf16[64,4096]{1,0:T(8,128)(2,1)S(1)}, u32[]{:S(2)}, u32[]{:S(2)}) collective-permute-start(bf16[64,4096]{1,0:T(8,128)(2,1)S(1)} %collective-permute-done.7.p1), channel_id=1, source_target_pairs={{0,1},{1,0},{2,3},{3,2},{4,5},{5,4},{6,7},{7,6},{8,9},{9,8},{10,11... | collective-permute-start | bytes 1572872 | tf_op jit(solution)/shard_map/ppermute | solution.py:441
  102.0 1.5 %collective-permute-start.14 = (bf16[256,384]{1,0:T(8,128)(2,1)S(1)}, bf16[256,384]{1,0:T(8,128)(2,1)S(1)}, u32[]{:S(2)}, u32[]{:S(2)}) collective-permute-start(bf16[256,384]{1,0:T(8,128)(2,1)S(1)} %shard_map.144.inner_ref), channel_id=1, source_target_pairs={{0,1},{1,0},{2,3},{3,2},{4,5},{5,4},{6,7},{7,6},{8,9},{9,8},{10,11... | collective-permute-start | bytes 589832 | tf_op jit(solution)/shard_map/ppermute | solution.py:441
  105.4 5.6 %collective-permute-start.19 = (bf16[64,2048]{1,0:T(8,128)(2,1)S(1)}, bf16[64,2048]{1,0:T(8,128)(2,1)S(1)}, u32[]{:S(2)}, u32[]{:S(2)}) collective-permute-start(bf16[64,2048]{1,0:T(8,128)(2,1)S(1)} %get-tuple-element.37), channel_id=1, source_target_pairs={{0,6},{1,25},{2,0},{3,27},{4,2},{5,29},{6,4},{7,31},{8,14},{9,1},{... | collective-permute-start | bytes 786440 | tf_op jit(solution)/shard_map/ppermute | solution.py:509
  106.0 6.7 %collective-permute-start.16 = (bf16[64,2048]{1,0:T(8,128)(2,1)S(1)}, bf16[64,2048]{1,0:T(8,128)(2,1)S(1)}, u32[]{:S(2)}, u32[]{:S(2)}) collective-permute-start(bf16[64,2048]{1,0:T(8,128)(2,1)S(1)} %get-tuple-element.33), channel_id=1, source_target_pairs={{0,2},{1,9},{2,4},{3,11},{4,6},{5,13},{6,0},{7,15},{8,10},{9,17},{... | collective-permute-start | bytes 786440 | tf_op jit(solution)/shard_map/ppermute | solution.py:508
  106.9 6.9 %collective-permute-start.15 = (bf16[64,2048]{1,0:T(8,128)(2,1)S(1)}, bf16[64,2048]{1,0:T(8,128)(2,1)S(1)}, u32[]{:S(2)}, u32[]{:S(2)}) collective-permute-start(bf16[64,2048]{1,0:T(8,128)(2,1)S(1)} %get-tuple-element.31), channel_id=1, source_target_pairs={{0,6},{1,25},{2,0},{3,27},{4,2},{5,29},{6,4},{7,31},{8,14},{9,1},{... | collective-permute-start | bytes 786440 | tf_op jit(solution)/shard_map/ppermute | solution.py:509
  108.7 6.9 %collective-permute-start.18 = (bf16[64,2048]{1,0:T(8,128)(2,1)S(1)}, bf16[64,2048]{1,0:T(8,128)(2,1)S(1)}, u32[]{:S(2)}, u32[]{:S(2)}) collective-permute-start(bf16[64,2048]{1,0:T(8,128)(2,1)S(1)} %get-tuple-element.35), channel_id=1, source_target_pairs={{0,2},{1,9},{2,4},{3,11},{4,6},{5,13},{6,0},{7,15},{8,10},{9,17},{... | collective-permute-start | bytes 786440 | tf_op jit(solution)/shard_map/ppermute | solution.py:508
  111.0 5.6 %collective-permute-start.20 = (bf16[64,2048]{1,0:T(8,128)(2,1)S(1)}, bf16[64,2048]{1,0:T(8,128)(2,1)S(1)}, u32[]{:S(2)}, u32[]{:S(2)}) collective-permute-start(bf16[64,2048]{1,0:T(8,128)(2,1)S(1)} %add_convert_fusion.1), channel_id=1, source_target_pairs={{0,6},{1,25},{2,0},{3,27},{4,2},{5,29},{6,4},{7,31},{8,14},{9,1},{... | collective-permute-start | bytes 786440 | tf_op jit(solution)/shard_map/ppermute | solution.py:509
  112.8 6.5 %collective-permute-start.17 = (bf16[64,2048]{1,0:T(8,128)(2,1)S(1)}, bf16[64,2048]{1,0:T(8,128)(2,1)S(1)}, u32[]{:S(2)}, u32[]{:S(2)}) collective-permute-start(bf16[64,2048]{1,0:T(8,128)(2,1)S(1)} %add_convert_fusion.2), channel_id=1, source_target_pairs={{0,2},{1,9},{2,4},{3,11},{4,6},{5,13},{6,0},{7,15},{8,10},{9,17},{... | collective-permute-start | bytes 786440 | tf_op jit(solution)/shard_map/ppermute | solution.py:508
  136.9 1.6 %collective-permute-start.21 = (bf16[2,4096]{1,0:T(2,128)(2,1)S(1)}, bf16[2,4096]{1,0:T(2,128)(2,1)S(1)}, u32[]{:S(2)}, u32[]{:S(2)}) collective-permute-start(bf16[2,4096]{1,0:T(2,128)(2,1)S(1)} %get-tuple-element.40), channel_id=1, source_target_pairs={{0,1},{1,0},{2,3},{3,2},{4,5},{5,4},{6,7},{7,6},{8,9},{9,8},{10,11... | collective-permute-start | bytes 49160 | tf_op jit(solution)/shard_map/ppermute | solution.py:441

commit v7 on v6

--- a/solution.py
+++ b/solution.py
@@ -395,19 +395,19 @@
     )(at, other, in_vmem(down), half)
 
 
-def total_kernel(*refs):
+def total_kernel(count, *refs):
     out_ref = refs[-1]
     width = HALF // 2
-    for part in range(2):
-        value = functools.reduce(jnp.add, [ref[...].astype(F32) for ref in refs[3 * part : 3 * part + 3]])
+    for part, terms in enumerate((refs[:count], refs[count:-1])):
+        value = functools.reduce(jnp.add, [ref[...].astype(F32) for ref in terms])
         for chip in range(16):
             out_ref[chip, :, part * width : (part + 1) * width] = value[4 * chip : 4 * chip + 4].astype(BF)
 
 
 def total(first, second):
     return pl.pallas_call(
-        total_kernel,
-        in_specs=[WHOLE] * 6,
+        functools.partial(total_kernel, len(first)),
+        in_specs=[WHOLE] * (len(first) + len(second)),
         out_specs=WHOLE,
         out_shape=jax.ShapeDtypeStruct((16, 4, HALF), BF),
         compiler_params=pltpu.CompilerParams(vmem_limit_bytes=8 * MB),
@@ -508,10 +508,12 @@
     ahead = lambda value: lax.ppermute(value, PLANE, line_shift(1))
     back = lambda value: lax.ppermute(value, PLANE, line_shift(3))
     plus = lambda first, second: (first.astype(F32) + second.astype(F32)).astype(BF)
-    via_a, via_b = ahead(a2), back(b2)
-    near_b, near_a = ahead(b3), back(a1)
-    far_a, far_b = ahead(plus(a3, via_a)), back(plus(b1, via_b))
-    out = total((a0, near_a, far_a), (b0, near_b, far_b))
+    via_b = back(b2)
+    two_a = lax.ppermute(a2, PLANE, line_shift(2))
+    three_a, three_b = ahead(a3), ahead(b3)
+    one_a = back(a1)
+    one_b = back(plus(b1, via_b))
+    out = total((a0, one_a, three_a, two_a), (b0, three_b, one_b))
     out = lax.all_to_all(
         out, ALL, split_axis=0, concat_axis=0, tiled=True, axis_index_groups=wide
     )

time: 140 us -> 139 us (level)
  blocking collectives: 61.6 us -> 58.6 us
  starting transfers between devices: 26.1 us -> 28.8 us
    all_to_all x1, blocking collectives: 16.7 us -> 13.7 us  [local(): lax.all_to_all(out, ALL, split_axis=0, concat_axis=0, tiled=True, axis_in...]
    ppermute x0 -> x1, waiting for transfers between devices: none -> 2.44 us  [local(): two_a = lax.ppermute(a2, PLANE, line_shift(2))]
    ppermute x3 -> x2, waiting for transfers between devices: 4.62 us -> 2.64 us  [local(): ahead = lambda value: lax.ppermute(value, PLANE, line_shift(1))]
    ppermute x13, starting transfers between devices: 11.2 us -> 13.1 us  [swap(): return lax.ppermute(value, 'c', SWAP)]
    ppermute x0 -> x1, starting transfers between devices: none -> 1.83 us  [local(): two_a = lax.ppermute(a2, PLANE, line_shift(2))]
    ppermute x3, starting transfers between devices: 3.96 us -> 2.55 us  [local(): back = lambda value: lax.ppermute(value, PLANE, line_shift(3))]
  transfers between devices with their start and end apart: 23 -> 23, of which waited for: 12 -> 11; matrix products, arithmetic and copies ran while one was open for 3% -> 3% of each run, Pallas kernels for 16% -> 16%
where the time goes in v7:
time: 139 us; the launch traced here: 138 us
  blocking collectives  58.6 us (42%)
  starting transfers between devices  28.8 us (21%)
  Pallas kernels  27.3 us (20%)
  waiting for transfers between devices  17.6 us (13%)
  other arithmetic  2.92 us (2%)
  local copies, waits for them, and re-layouts  2.65 us (2%)
    all_to_all x1, blocking collectives, local(): lax.all_to_all(sent, ALL, split_axis=0, concat_axis=0, tiled=True, axis_i...  16.7 us
    all_to_all x1, blocking collectives, local(): lax.all_to_all(parts, ('z', 'y'), split_axis=0, concat_axis=0, tiled=True)  14.6 us
    all_to_all x1, blocking collectives, local(): lax.all_to_all(out, ALL, split_axis=0, concat_axis=0, tiled=True, axis_in...  13.7 us
    all_to_all x1, blocking collectives, local(): lax.all_to_all(summed, ('z', 'y'), split_axis=0, concat_axis=0, tiled=True)  13.6 us
    ppermute x13, starting transfers between devices, swap(): return lax.ppermute(value, 'c', SWAP)  13.1 us
    all_to_all x1, starting transfers between devices, local(): lax.all_to_all(q, PLANE, split_axis=0, concat_axis=0, tiled=True)  8.3 us
    pallas_call x1, Pallas kernels, fetch(): pl.pallas_call(fetch_kernel, in_specs=[SCALARS] + [pl.BlockSpec(memory_sp...  7.07 us
    pallas_call x1, Pallas kernels, attend(): pl.pallas_call(attend_kernel, grid=(1,), in_specs=[pl.BlockSpec(a.shape,...  6.87 us
  transfers between devices with their start and end apart: 23, of which 11 were waited for; matrix products, arithmetic and copies ran while one was open for 3% of the time, Pallas kernels for 16%

profile of v7, /device:TPU:1, one launch (start us, length us, event | category | flops | bytes accessed | tf_op | source)
XLA Modules:
  0.0 138.2 jit_solution(5370557113840402614)
XLA Ops:
  0.0 1.4 %collective-permute-start.5 = (bf16[384,8192]{1,0:T(8,128)(2,1)}, bf16[384,8192]{1,0:T(8,128)(2,1)}, u32[]{:S(2)}, u32[]{:S(2)}) collective-permute-start(bf16[384,8192]{1,0:T(8,128)(2,1)} %bitcast.13), channel_id=1, source_target_pairs={{0,1},{1,0},{2,3},{3,2},{4,5},{5,4},{6,7},{7,6},{8,9},{9,8},{10,11... | collective-permute-start | bytes 18874376 | tf_op jit(solution)/shard_map/ppermute | solution.py:441
  1.4 0.5 collective-permute-start.3
  1.9 1.7 %shard_map.136 = bf16[32,2,4096]{2,1,0:T(2,128)(2,1)} custom-call(bf16[2,8192]{1,0:T(2,128)(2,1)} %q_ref.1), custom_call_target="tpu_custom_call" | custom-call | bytes 1048576 | tf_op jit(solution)/shard_map/pallas_call | solution.py:107
  3.6 8.3 %all-to-all-start = ((bf16[32,2,4096]{2,1,0:T(2,128)(2,1)}), bf16[32,2,4096]{2,1,0:T(2,128)(2,1)S(1)}, u32[]{:S(2)}, u32[]{:S(2)}) async-start(bf16[32,2,4096]{2,1,0:T(2,128)(2,1)} %shard_map.136), calls=%async_computation | async-start | bytes 1048576 | tf_op jit(solution)/shard_map/all_to_all | solution.py:477
  11.9 0.3 collective-permute-start
  12.2 0.3 collective-permute-start.1
  12.5 0.7 reshape.27.gain_ref
  13.3 0.6 copy-done.6
  13.9 0.1 copy.16
  14.0 0.2 copy-done.2
  14.3 0.5 pad_maximum_fusion
  14.7 0.2 reshape.25.sa_ref
  14.9 0.1 pad_add_fusion.1.refs_1_.at_ref
  15.0 1.4 %pad_maximum_fusion.1 = bf16[64,2,2048]{2,1,0:T(2,128)(2,1)S(1)} fusion(bf16[64,2,1024]{2,1,0:T(2,128)(2,1)} %collective-permute-done.3, bf16[64,2,1024]{2,1,0:T(2,128)(2,1)S(1)} %collective-permute-done.2), kind=kLoop, calls=%fused_computation.2 | loop fusion | flops 1048576 | bytes 1048576 | tf_op jit(solution)/shard_map/concatenate | solution.py:479
  16.5 0.2 reshape.26.sb_ref
  16.7 6.8 %all-to-all-done = bf16[32,2,4096]{2,1,0:T(2,128)(2,1)S(1)} async-done(((bf16[32,2,4096]{2,1,0:T(2,128)(2,1)}), bf16[32,2,4096]{2,1,0:T(2,128)(2,1)S(1)}, u32[]{:S(2)}, u32[]{:S(2)}) %all-to-all-start) | async-done | bytes 524320 | tf_op jit(solution)/shard_map/all_to_all | solution.py:477
  23.4 0.2 reshape.24.q_ref
  23.7 6.9 %shard_map.138 = bf16[16,72,256]{2,1,0:T(8,128)(2,1)S(1)} custom-call(bf16[64,4096]{1,0:T(8,128)(2,1)S(1)} %reshape.24.q_ref, bf16[512,1024]{1,0:T(8,128)(2,1)} %ka_ref.1, bf16[512,1024]{1,0:T(8,128)(2,1)S(1)} %collective-permute-done.kb_ref, bf16[512,1024]{1,0:T(8,128)(2,1)} %va_ref.1, bf16[512,1024]{1,0:T(8,128)(2,1)} %collective-permute-done.1.vb_ref, ...), custom_call_target="tpu_custom_call" | custom-call | flops 1400000000 | bytes 6291456 | tf_op jit(solution)/shard_map/pallas_call | solution.py:189
  30.6 14.6 %all_to_all.25.got_ref = bf16[16,72,256]{2,1,0:T(8,128)(2,1)S(1)} all-to-all(bf16[16,72,256]{2,1,0:T(8,128)(2,1)S(1)} %shard_map.138), channel_id=1, replica_groups=mesh['x'=4,'z'=4,'y'=4,'c'=2] {'z','y'}, dimensions={0} | all-to-all | bytes 1179648 | tf_op jit(solution)/shard_map/all_to_all | solution.py:489
  45.2 1.4 shard_map.139
  46.6 1.8 %collective-permute-start.4 = (bf16[64,4096]{1,0:T(8,128)(2,1)S(1)}, bf16[64,4096]{1,0:T(8,128)(2,1)S(1)}, u32[]{:S(2)}, u32[]{:S(2)}) collective-permute-start(bf16[64,4096]{1,0:T(8,128)(2,1)S(1)} %get-tuple-element.24), channel_id=1, source_target_pairs={{0,1},{1,0},{2,3},{3,2},{4,5},{5,4},{6,7},{7,6},{8,9},{9,8},{10,11... | collective-permute-start | bytes 1572872 | tf_op jit(solution)/shard_map/ppermute | solution.py:441
  48.4 1.1 shard_map.140
  49.4 0.4 collective-permute-done.4
  49.9 0.1 add_convert_fusion
  50.0 0.2 reshape.28
  50.2 13.6 %all_to_all.26.got_ref = bf16[16,4,4096]{2,1,0:T(4,128)(2,1)S(1)} all-to-all(bf16[16,4,4096]{2,1,0:T(4,128)(2,1)S(1)} %reshape.28), channel_id=1, replica_groups=mesh['x'=4,'z'=4,'y'=4,'c'=2] {'z','y'}, dimensions={0} | all-to-all | bytes 1048576 | tf_op jit(solution)/shard_map/all_to_all | solution.py:494
  63.8 0.1 shard_map.141
  63.9 16.7 %all_to_all.27 = bf16[16,4,4096]{2,1,0:T(4,128)(2,1)S(1)} all-to-all(bf16[16,4,4096]{2,1,0:T(4,128)(2,1)S(1)} %get-tuple-element.25), channel_id=1, replica_groups={{0,32,64,96,8,40,72,104,16,48,80,112,24,56,88,120},{2,34,66,98,10,42,74..., dimensions={0} | all-to-all | bytes 1048576 | tf_op jit(solution)/shard_map/all_to_all | solution.py:497
  80.6 0.1 reshape.29.after_ref.p0
  80.7 0.1 collective-permute-start.9
  80.8 0.6 collective-permute-start.11
  81.4 0.9 collective-permute-start.7
  82.4 0.1 fusion
  82.4 2.2 %collective-permute-start.13 = (f32[2,4]{1,0:T(2,128)S(1)}, f32[2,4]{1,0:T(2,128)S(1)}, u32[]{:S(2)}, u32[]{:S(2)}) collective-permute-start(f32[2,4]{1,0:T(2,128)S(1)} %fusion), channel_id=1, source_target_pairs={{0,1},{1,0},{2,3},{3,2},{4,5},{5,4},{6,7},{7,6},{8,9},{9,8},{10,11... | collective-permute-start | bytes 104 | tf_op jit(solution)/shard_map/ppermute | solution.py:441
  84.7 0.8 collective-permute-done.13
  85.5 0.4 collective-permute-start.6
  85.9 7.1 %shard_map.142 = (bf16[8192,768]{1,0:T(8,128)(2,1)S(1)}, bf16[768,4096]{1,0:T(8,128)(2,1)S(1)}) custom-call(s32[4]{0:T(128)S(1)} %pad_add_fusion.1.refs_1_.at_ref, bf16[64,4096]{1,0:T(8,128)(2,1)S(1)} %reshape.29.after_ref.p0, bf16[8192,384]{1,0:T(8,128)(2,1)} %bitcast.15, bf16[8192,384]{1,0:T(8,128)(2,1)} %bitcast.16, bf16[384,8192]{1,0:T(8,128)(2,1)} %bitcast.14, ...), custom_call_target="tpu_custom_call" | custom-call | bytes 23068672 | tf_op jit(solution)/shard_map/pallas_call | solution.py:78
  93.0 0.2 collective-permute-start.10
  93.2 2.7 %collective-permute-start.12 = (bf16[64,4096]{1,0:T(8,128)(2,1)S(1)}, bf16[64,4096]{1,0:T(8,128)(2,1)S(1)}, u32[]{:S(2)}, u32[]{:S(2)}) collective-permute-start(bf16[64,4096]{1,0:T(8,128)(2,1)S(1)} %collective-permute-done.11.p3), channel_id=1, source_target_pairs={{0,1},{1,0},{2,3},{3,2},{4,5},{5,4},{6,7},{7,6},{8,9},{9,8},{10,11... | collective-permute-start | bytes 1572872 | tf_op jit(solution)/shard_map/ppermute | solution.py:441
  95.9 0.4 collective-permute-done.7.p1
  96.3 0.6 collective-permute-start.8
  96.8 2.5 %shard_map.143 = (f32[256,768]{1,0:T(8,128)S(1)}, f32[256,128]{1,0:T(8,128)S(1)}) custom-call(s32[4]{0:T(128)S(1)} %pad_add_fusion.1.refs_1_.at_ref, bf16[64,4096]{1,0:T(8,128)(2,1)S(1)} %reshape.29.after_ref.p0, bf16[64,4096]{1,0:T(8,128)(2,1)S(1)} %collective-permute-done.7.p1, bf16[64,4096]{1,0:T(8,128)(2,1)S(1)} %collective-permute-done.9.p2, ...), custom_call_target="tpu_custom_call" | custom-call | flops 16000000000 | bytes 9437184 | tf_op jit(solution)/shard_map/pallas_call | solution.py:315
  99.4 2.6 %shard_map.144.inner_ref = bf16[256,384]{1,0:T(8,128)(2,1)S(1)} custom-call(s32[4]{0:T(128)S(1)} %pad_add_fusion.1.refs_1_.at_ref, bf16[64,4096]{1,0:T(8,128)(2,1)S(1)} %collective-permute-done.6.p0, bf16[64,4096]{1,0:T(8,128)(2,1)S(1)} %collective-permute-done.8.p1, bf16[64,4096]{1,0:T(8,128)(2,1)S(1)} %collective-permute-done.10.p2, ...), custom_call_target="tpu_custom_call" | custom-call | flops 1600000000 | bytes 9437184 | tf_op jit(solution)/shard_map/pallas_call | solution.py:338
  102.0 0.1 collective-permute-start.14
  102.1 1.3 shard_map.145.half_ref
  103.4 0.2 collective-permute-done.14.other_ref
  103.5 1.8 %shard_map.146 = (bf16[64,2048]{1,0:T(8,128)(2,1)S(1)}, bf16[64,2048]{1,0:T(8,128)(2,1)S(1)}, bf16[64,2048]{1,0:T(8,128)(2,1)S(1)}, bf16[64,2048]{1,0:T(8,128)(2...) custom-call(s32[4]{0:T(128)S(1)} %pad_add_fusion.1.refs_1_.at_ref, ...), custom_call_target="tpu_custom_call" | custom-call | flops 800000000 | bytes 9437184 | tf_op jit(solution)/shard_map/pallas_call | solution.py:387
  105.4 0.6 collective-permute-start.19
  106.0 0.4 collective-permute-start.15
  106.4 1.1 collective-permute-start.16
  107.5 1.8 %collective-permute-start.17 = (bf16[64,2048]{1,0:T(8,128)(2,1)S(1)}, bf16[64,2048]{1,0:T(8,128)(2,1)S(1)}, u32[]{:S(2)}, u32[]{:S(2)}) collective-permute-start(bf16[64,2048]{1,0:T(8,128)(2,1)S(1)} %get-tuple-element.33), channel_id=1, source_target_pairs={{0,4},{1,17},{2,6},{3,19},{4,0},{5,21},{6,2},{7,23},{8,12},{9,25},... | collective-permute-start | bytes 786440 | tf_op jit(solution)/shard_map/ppermute | solution.py:512
  109.3 0.3 collective-permute-start.18
  109.6 1.3 collective-permute-done.19
  111.0 1.5 %collective-permute-start.20 = (bf16[64,2048]{1,0:T(8,128)(2,1)S(1)}, bf16[64,2048]{1,0:T(8,128)(2,1)S(1)}, u32[]{:S(2)}, u32[]{:S(2)}) collective-permute-start(bf16[64,2048]{1,0:T(8,128)(2,1)S(1)} %add_convert_fusion.1), channel_id=1, source_target_pairs={{0,6},{1,25},{2,0},{3,27},{4,2},{5,29},{6,4},{7,31},{8,14},{9,1},{... | collective-permute-start | bytes 786440 | tf_op jit(solution)/shard_map/ppermute | solution.py:509
  112.6 1.2 collective-permute-done.15.refs_1_
  113.8 2.4 %collective-permute-done.17.refs_3_ = bf16[64,2048]{1,0:T(8,128)(2,1)S(1)} collective-permute-done((bf16[64,2048]{1,0:T(8,128)(2,1)S(1)}, bf16[64,2048]{1,0:T(8,128)(2,1)S(1)}, u32[]{:S(2)}, u32[]{:S(2)}) %collective-permute-start.17) | collective-permute-done | bytes 262176 | tf_op jit(solution)/shard_map/ppermute | solution.py:512
  116.2 2.6 %collective-permute-done.18.refs_5_ = bf16[64,2048]{1,0:T(8,128)(2,1)S(1)} collective-permute-done((bf16[64,2048]{1,0:T(8,128)(2,1)S(1)}, bf16[64,2048]{1,0:T(8,128)(2,1)S(1)}, u32[]{:S(2)}, u32[]{:S(2)}) %collective-permute-start.18) | collective-permute-done | bytes 262176 | tf_op jit(solution)/shard_map/ppermute | solution.py:508
  118.8 0.6 collective-permute-done.20.refs_6_
  119.4 0.3 shard_map.147
  119.7 13.7 %all_to_all.28.got_ref = bf16[16,4,4096]{2,1,0:T(4,128)(2,1)S(1)} all-to-all(bf16[16,4,4096]{2,1,0:T(4,128)(2,1)S(1)} %shard_map.147), channel_id=1, replica_groups={{0,32,64,96,8,40,72,104,16,48,80,112,24,56,88,120},{2,34,66,98,10,42,74..., dimensions={0} | all-to-all | bytes 1048576 | tf_op jit(solution)/shard_map/all_to_all | solution.py:517
  133.4 0.7 shard_map.148
  134.1 2.6 %collective-permute-start.21 = (bf16[2,4096]{1,0:T(2,128)(2,1)S(1)}, bf16[2,4096]{1,0:T(2,128)(2,1)S(1)}, u32[]{:S(2)}, u32[]{:S(2)}) collective-permute-start(bf16[2,4096]{1,0:T(2,128)(2,1)S(1)} %get-tuple-element.40), channel_id=1, source_target_pairs={{0,1},{1,0},{2,3},{3,2},{4,5},{5,4},{6,7},{7,6},{8,9},{9,8},{10,11... | collective-permute-start | bytes 49160 | tf_op jit(solution)/shard_map/ppermute | solution.py:441
  136.7 0.8 collective-permute-done.21
  137.6 0.7 broadcast_select_fusion
  (31 shorter events, 0.3 us)
Async XLA Ops:
  0.0 63.8 %collective-permute-start.5 = (bf16[384,8192]{1,0:T(8,128)(2,1)}, bf16[384,8192]{1,0:T(8,128)(2,1)}, u32[]{:S(2)}, u32[]{:S(2)}) collective-permute-start(bf16[384,8192]{1,0:T(8,128)(2,1)} %bitcast.13), channel_id=1, source_target_pairs={{0,1},{1,0},{2,3},{3,2},{4,5},{5,4},{6,7},{7,6},{8,9},{9,8},{10,11... | collective-permute-start | bytes 18874376 | tf_op jit(solution)/shard_map/ppermute | solution.py:441
  1.4 13.6 %collective-permute-start.2 = (bf16[64,2,1024]{2,1,0:T(2,128)(2,1)}, bf16[64,2,1024]{2,1,0:T(2,128)(2,1)S(1)}, u32[]{:S(2)}, u32[]{:S(2)}) collective-permute-start(bf16[64,2,1024]{2,1,0:T(2,128)(2,1)} %param.17), channel_id=1, source_target_pairs={{0,1},{1,0},{2,3},{3,2},{4,5},{5,4},{6,7},{7,6},{8,9},{9,8},{10,11... | collective-permute-start | bytes 786440 | tf_op jit(solution)/shard_map/ppermute | solution.py:441
  1.4 13.6 %collective-permute-start.3 = (bf16[64,2,1024]{2,1,0:T(2,128)(2,1)}, bf16[64,2,1024]{2,1,0:T(2,128)(2,1)}, u32[]{:S(2)}, u32[]{:S(2)}) collective-permute-start(bf16[64,2,1024]{2,1,0:T(2,128)(2,1)} %param.18), channel_id=1, source_target_pairs={{0,1},{1,0},{2,3},{3,2},{4,5},{5,4},{6,7},{7,6},{8,9},{9,8},{10,11... | collective-permute-start | bytes 786440 | tf_op jit(solution)/shard_map/ppermute | solution.py:441
  3.6 19.9 %all-to-all-start = ((bf16[32,2,4096]{2,1,0:T(2,128)(2,1)}), bf16[32,2,4096]{2,1,0:T(2,128)(2,1)S(1)}, u32[]{:S(2)}, u32[]{:S(2)}) async-start(bf16[32,2,4096]{2,1,0:T(2,128)(2,1)} %shard_map.136), calls=%async_computation | async-start | bytes 1048576 | tf_op jit(solution)/shard_map/all_to_all | solution.py:477
  11.9 11.8 %collective-permute-start = (bf16[512,1024]{1,0:T(8,128)(2,1)}, bf16[512,1024]{1,0:T(8,128)(2,1)S(1)}, u32[]{:S(2)}, u32[]{:S(2)}) collective-permute-start(bf16[512,1024]{1,0:T(8,128)(2,1)} %ka_ref.1), channel_id=1, source_target_pairs={{0,1},{1,0},{2,3},{3,2},{4,5},{5,4},{6,7},{7,6},{8,9},{9,8},{10,11... | collective-permute-start | bytes 3145736 | tf_op jit(solution)/shard_map/ppermute | solution.py:441
  12.2 11.5 %collective-permute-start.1 = (bf16[512,1024]{1,0:T(8,128)(2,1)}, bf16[512,1024]{1,0:T(8,128)(2,1)}, u32[]{:S(2)}, u32[]{:S(2)}) collective-permute-start(bf16[512,1024]{1,0:T(8,128)(2,1)} %va_ref.1), channel_id=1, source_target_pairs={{0,1},{1,0},{2,3},{3,2},{4,5},{5,4},{6,7},{7,6},{8,9},{9,8},{10,11... | collective-permute-start | bytes 3145736 | tf_op jit(solution)/shard_map/ppermute | solution.py:441
  13.2 0.7 copy-start.6
  13.2 1.0 copy-start.2
  13.2 1.0 copy-start.3
  14.7 30.5 %copy-start.1 = (bf16[2,8192]{1,0:T(2,128)(2,1)S(1)}, bf16[2,8192]{1,0:T(2,128)(2,1)}, u32[]{:S(2)}) copy-start(bf16[2,8192]{1,0:T(2,128)(2,1)} %hidden_ref.3) | copy-start | bytes 98308
  23.6 21.6 %copy-start = (bf16[256,8192]{1,0:T(8,128)(2,1)S(1)}, bf16[256,8192]{1,0:T(8,128)(2,1)}, u32[]{:S(2)}) copy-start(bf16[256,8192]{1,0:T(8,128)(2,1)} %w_ref.3) | copy-start | bytes 12582916
  46.6 3.3 %collective-permute-start.4 = (bf16[64,4096]{1,0:T(8,128)(2,1)S(1)}, bf16[64,4096]{1,0:T(8,128)(2,1)S(1)}, u32[]{:S(2)}, u32[]{:S(2)}) collective-permute-start(bf16[64,4096]{1,0:T(8,128)(2,1)S(1)} %get-tuple-element.24), channel_id=1, source_target_pairs={{0,1},{1,0},{2,3},{3,2},{4,5},{5,4},{6,7},{7,6},{8,9},{9,8},{10,11... | collective-permute-start | bytes 1572872 | tf_op jit(solution)/shard_map/ppermute | solution.py:441
  49.4 32.9 %copy-start.4 = (f32[2,2]{1,0:T(2,128)S(1)}, f32[2,2]{1,0:T(2,128)}, u32[]{:S(2)}) copy-start(f32[2,2]{1,0:T(2,128)} %param.24) | copy-start | bytes 52
  49.4 32.9 %copy-start.5 = (s32[2,2]{1,0:T(2,128)S(1)}, s32[2,2]{1,0:T(2,128)}, u32[]{:S(2)}) copy-start(s32[2,2]{1,0:T(2,128)} %param.23) | copy-start | bytes 52
  80.7 12.3 %collective-permute-start.9 = (bf16[64,4096]{1,0:T(8,128)(2,1)S(1)}, bf16[64,4096]{1,0:T(8,128)(2,1)S(1)}, u32[]{:S(2)}, u32[]{:S(2)}) collective-permute-start(bf16[64,4096]{1,0:T(8,128)(2,1)S(1)} %reshape.29.after_ref.p0), channel_id=1, source_target_pairs={{0,4},{1,17},{2,6},{3,19},{4,0},{5,21},{6,2},{7,23},{8,12},{9,25},... | collective-permute-start | bytes 1572872 | tf_op jit(solution)/shard_map/ppermute | solution.py:500
  80.8 12.4 %collective-permute-start.11 = (bf16[64,4096]{1,0:T(8,128)(2,1)S(1)}, bf16[64,4096]{1,0:T(8,128)(2,1)S(1)}, u32[]{:S(2)}, u32[]{:S(2)}) collective-permute-start(bf16[64,4096]{1,0:T(8,128)(2,1)S(1)} %reshape.29.after_ref.p0), channel_id=1, source_target_pairs={{0,6},{1,25},{2,0},{3,27},{4,2},{5,29},{6,4},{7,31},{8,14},{9,1},{... | collective-permute-start | bytes 1572872 | tf_op jit(solution)/shard_map/ppermute | solution.py:500
  81.4 14.8 %collective-permute-start.7 = (bf16[64,4096]{1,0:T(8,128)(2,1)S(1)}, bf16[64,4096]{1,0:T(8,128)(2,1)S(1)}, u32[]{:S(2)}, u32[]{:S(2)}) collective-permute-start(bf16[64,4096]{1,0:T(8,128)(2,1)S(1)} %reshape.29.after_ref.p0), channel_id=1, source_target_pairs={{0,2},{1,9},{2,4},{3,11},{4,6},{5,13},{6,0},{7,15},{8,10},{9,17},{... | collective-permute-start | bytes 1572872 | tf_op jit(solution)/shard_map/ppermute | solution.py:500
  82.4 3.0 %collective-permute-start.13 = (f32[2,4]{1,0:T(2,128)S(1)}, f32[2,4]{1,0:T(2,128)S(1)}, u32[]{:S(2)}, u32[]{:S(2)}) collective-permute-start(f32[2,4]{1,0:T(2,128)S(1)} %fusion), channel_id=1, source_target_pairs={{0,1},{1,0},{2,3},{3,2},{4,5},{5,4},{6,7},{7,6},{8,9},{9,8},{10,11... | collective-permute-start | bytes 104 | tf_op jit(solution)/shard_map/ppermute | solution.py:441
  85.5 13.8 %collective-permute-start.6 = (bf16[64,4096]{1,0:T(8,128)(2,1)S(1)}, bf16[64,4096]{1,0:T(8,128)(2,1)S(1)}, u32[]{:S(2)}, u32[]{:S(2)}) collective-permute-start(bf16[64,4096]{1,0:T(8,128)(2,1)S(1)} %reshape.29.after_ref.p0), channel_id=1, source_target_pairs={{0,1},{1,0},{2,3},{3,2},{4,5},{5,4},{6,7},{7,6},{8,9},{9,8},{10,11... | collective-permute-start | bytes 1572872 | tf_op jit(solution)/shard_map/ppermute | solution.py:441
  93.0 6.4 %collective-permute-start.10 = (bf16[64,4096]{1,0:T(8,128)(2,1)S(1)}, bf16[64,4096]{1,0:T(8,128)(2,1)S(1)}, u32[]{:S(2)}, u32[]{:S(2)}) collective-permute-start(bf16[64,4096]{1,0:T(8,128)(2,1)S(1)} %collective-permute-done.9.p2), channel_id=1, source_target_pairs={{0,1},{1,0},{2,3},{3,2},{4,5},{5,4},{6,7},{7,6},{8,9},{9,8},{10,11... | collective-permute-start | bytes 1572872 | tf_op jit(solution)/shard_map/ppermute | solution.py:441
  93.2 6.2 %collective-permute-start.12 = (bf16[64,4096]{1,0:T(8,128)(2,1)S(1)}, bf16[64,4096]{1,0:T(8,128)(2,1)S(1)}, u32[]{:S(2)}, u32[]{:S(2)}) collective-permute-start(bf16[64,4096]{1,0:T(8,128)(2,1)S(1)} %collective-permute-done.11.p3), channel_id=1, source_target_pairs={{0,1},{1,0},{2,3},{3,2},{4,5},{5,4},{6,7},{7,6},{8,9},{9,8},{10,11... | collective-permute-start | bytes 1572872 | tf_op jit(solution)/shard_map/ppermute | solution.py:441
  96.3 3.1 %collective-permute-start.8 = (bf16[64,4096]{1,0:T(8,128)(2,1)S(1)}, bf16[64,4096]{1,0:T(8,128)(2,1)S(1)}, u32[]{:S(2)}, u32[]{:S(2)}) collective-permute-start(bf16[64,4096]{1,0:T(8,128)(2,1)S(1)} %collective-permute-done.7.p1), channel_id=1, source_target_pairs={{0,1},{1,0},{2,3},{3,2},{4,5},{5,4},{6,7},{7,6},{8,9},{9,8},{10,11... | collective-permute-start | bytes 1572872 | tf_op jit(solution)/shard_map/ppermute | solution.py:441
  102.0 1.5 %collective-permute-start.14 = (bf16[256,384]{1,0:T(8,128)(2,1)S(1)}, bf16[256,384]{1,0:T(8,128)(2,1)S(1)}, u32[]{:S(2)}, u32[]{:S(2)}) collective-permute-start(bf16[256,384]{1,0:T(8,128)(2,1)S(1)} %shard_map.144.inner_ref), channel_id=1, source_target_pairs={{0,1},{1,0},{2,3},{3,2},{4,5},{5,4},{6,7},{7,6},{8,9},{9,8},{10,11... | collective-permute-start | bytes 589832 | tf_op jit(solution)/shard_map/ppermute | solution.py:441
  105.4 5.6 %collective-permute-start.19 = (bf16[64,2048]{1,0:T(8,128)(2,1)S(1)}, bf16[64,2048]{1,0:T(8,128)(2,1)S(1)}, u32[]{:S(2)}, u32[]{:S(2)}) collective-permute-start(bf16[64,2048]{1,0:T(8,128)(2,1)S(1)} %get-tuple-element.37), channel_id=1, source_target_pairs={{0,6},{1,25},{2,0},{3,27},{4,2},{5,29},{6,4},{7,31},{8,14},{9,1},{... | collective-permute-start | bytes 786440 | tf_op jit(solution)/shard_map/ppermute | solution.py:509
  106.0 7.8 %collective-permute-start.15 = (bf16[64,2048]{1,0:T(8,128)(2,1)S(1)}, bf16[64,2048]{1,0:T(8,128)(2,1)S(1)}, u32[]{:S(2)}, u32[]{:S(2)}) collective-permute-start(bf16[64,2048]{1,0:T(8,128)(2,1)S(1)} %get-tuple-element.31), channel_id=1, source_target_pairs={{0,6},{1,25},{2,0},{3,27},{4,2},{5,29},{6,4},{7,31},{8,14},{9,1},{... | collective-permute-start | bytes 786440 | tf_op jit(solution)/shard_map/ppermute | solution.py:509
  106.4 7.4 %collective-permute-start.16 = (bf16[64,2048]{1,0:T(8,128)(2,1)S(1)}, bf16[64,2048]{1,0:T(8,128)(2,1)S(1)}, u32[]{:S(2)}, u32[]{:S(2)}) collective-permute-start(bf16[64,2048]{1,0:T(8,128)(2,1)S(1)} %get-tuple-element.32), channel_id=1, source_target_pairs={{0,2},{1,9},{2,4},{3,11},{4,6},{5,13},{6,0},{7,15},{8,10},{9,17},{... | collective-permute-start | bytes 786440 | tf_op jit(solution)/shard_map/ppermute | solution.py:508
  107.5 8.7 %collective-permute-start.17 = (bf16[64,2048]{1,0:T(8,128)(2,1)S(1)}, bf16[64,2048]{1,0:T(8,128)(2,1)S(1)}, u32[]{:S(2)}, u32[]{:S(2)}) collective-permute-start(bf16[64,2048]{1,0:T(8,128)(2,1)S(1)} %get-tuple-element.33), channel_id=1, source_target_pairs={{0,4},{1,17},{2,6},{3,19},{4,0},{5,21},{6,2},{7,23},{8,12},{9,25},... | collective-permute-start | bytes 786440 | tf_op jit(solution)/shard_map/ppermute | solution.py:512
  109.3 9.5 %collective-permute-start.18 = (bf16[64,2048]{1,0:T(8,128)(2,1)S(1)}, bf16[64,2048]{1,0:T(8,128)(2,1)S(1)}, u32[]{:S(2)}, u32[]{:S(2)}) collective-permute-start(bf16[64,2048]{1,0:T(8,128)(2,1)S(1)} %get-tuple-element.35), channel_id=1, source_target_pairs={{0,2},{1,9},{2,4},{3,11},{4,6},{5,13},{6,0},{7,15},{8,10},{9,17},{... | collective-permute-start | bytes 786440 | tf_op jit(solution)/shard_map/ppermute | solution.py:508
  111.0 8.4 %collective-permute-start.20 = (bf16[64,2048]{1,0:T(8,128)(2,1)S(1)}, bf16[64,2048]{1,0:T(8,128)(2,1)S(1)}, u32[]{:S(2)}, u32[]{:S(2)}) collective-permute-start(bf16[64,2048]{1,0:T(8,128)(2,1)S(1)} %add_convert_fusion.1), channel_id=1, source_target_pairs={{0,6},{1,25},{2,0},{3,27},{4,2},{5,29},{6,4},{7,31},{8,14},{9,1},{... | collective-permute-start | bytes 786440 | tf_op jit(solution)/shard_map/ppermute | solution.py:509
  134.1 3.5 %collective-permute-start.21 = (bf16[2,4096]{1,0:T(2,128)(2,1)S(1)}, bf16[2,4096]{1,0:T(2,128)(2,1)S(1)}, u32[]{:S(2)}, u32[]{:S(2)}) collective-permute-start(bf16[2,4096]{1,0:T(2,128)(2,1)S(1)} %get-tuple-element.40), channel_id=1, source_target_pairs={{0,1},{1,0},{2,3},{3,2},{4,5},{5,4},{6,7},{7,6},{8,9},{9,8},{10,11... | collective-permute-start | bytes 49160 | tf_op jit(solution)/shard_map/ppermute | solution.py:441
